TPU v7x, 32 devices: a whole 2x2x4 slice. The times are simulated.
32 devices in a mesh: seq: 2 (over core), shard: 16 (over z, y, x).
Axes of the slice: x: 2, y: 2, z: 4, core: 2. Of those that a mesh axis runs over, the one named last changes fastest.
Arguments:
- tokens: bfloat16 [16, 8, 392, 512], P('shard', 'seq'), may hold values from -26 to 26
- norm1_gain: bfloat16 [512], P('shard'), may hold values from 0.099609375 to 1.8984375
- norm1_bias: bfloat16 [512], P('shard'), may hold values from -1.75 to 1.75
- qkv_weight: bfloat16 [512, 1536], P('shard'), may hold values from -0.25 to 0.25
- qv_bias: bfloat16 [1024], P('shard'), may hold values from -1.75 to 1.75
- position_table: bfloat16 [2535, 16], replicated, may hold values from -4 to 4
- proj_weight: bfloat16 [512, 512], P(None, 'shard'), may hold values from -1.5 to 1.5
- proj_bias: bfloat16 [512], P('shard'), may hold values from -1.75 to 1.75
- norm2_gain: bfloat16 [512], P('shard'), may hold values from 0.099609375 to 1.8984375
- norm2_bias: bfloat16 [512], P('shard'), may hold values from -1.75 to 1.75
- fc1_weight: bfloat16 [512, 2048], P('shard'), may hold values from -0.25 to 0.25
- fc1_bias: bfloat16 [2048], P('shard'), may hold values from -3 to 3
- fc2_weight: bfloat16 [2048, 512], P(None, 'shard'), may hold values from -0.125 to 0.125
- fc2_bias: bfloat16 [512], P('shard'), may hold values from -1.75 to 1.75
- rel_index: int32 [392, 392], replicated, may hold values from 0 to 2534, as said below
- region_ids: int32 [8, 392], P('seq'), may hold values from 0 to 26, as said below
- cotangent: bfloat16 [16, 8, 392, 512], P('shard', 'seq'), may hold values from -8 to 8
Outputs:
- block_out: bfloat16 [16, 8, 392, 512], P('shard', 'seq')
- input_grad: float32 [16, 8, 392, 512], P('shard', 'seq')
- norm1_gain_grad: float32 [512], P('shard')
- norm1_bias_grad: float32 [512], P('shard')
- qkv_weight_grad: float32 [512, 1536], P('shard')
- qv_bias_grad: float32 [1024], P('shard')
- position_table_grad: float32 [2535, 16], replicated
- proj_weight_grad: float32 [512, 512], P(None, 'shard')
- proj_bias_grad: float32 [512], P('shard')
- norm2_gain_grad: float32 [512], P('shard')
- norm2_bias_grad: float32 [512], P('shard')
- fc1_weight_grad: float32 [512, 2048], P('shard')
- fc1_bias_grad: float32 [2048], P('shard')
- fc2_weight_grad: float32 [2048, 512], P(None, 'shard')
- fc2_bias_grad: float32 [512], P('shard')
Inputs may be any that keep to these rules, and one draw needn't show every extreme that they name: `rel_index`: each relative offset of the two positions of a pair has a row of its own, relabelled anew in each draw; every row is used. `region_ids`: 9 a + 3 b + c with labels a, b, c that never fall along time, height and width of the shifted grid, each of the labels 0, 1, 2 occurring along each.
All inputs are finite; a program needn't handle non-finite values.
Results may differ from a plain program's by a relative error of at most 0.02.
Values may be sent and summed in bfloat16 or wider, within the bound.
No kernel may reach another device: no remote copies, remote signals or barrier semaphores. Data moves between devices by JAX's collectives and lax.ppermute only.
A program may use at most 448 MiB of HBM per device.

v0:
```python
import jax
import jax.numpy as jnp
import numpy as np
from jax import lax
from jax.sharding import PartitionSpec as P

HEADS = 16
HEAD_DIM = 32
WT = 8
WH = 7
WW = 7


EPS = 1e-05
MASKED = -1000000000.0
HIGH = lax.Precision.HIGHEST


def from_partner(shard, axis, stride):
    return lax.ppermute(shard, axis, [(i, i ^ 1 << stride) for i in range(lax.axis_size(axis))])


def norm_forward(values, gain, offset):
    mean = jnp.mean(values, axis=-1, keepdims=True)
    centred = values - mean
    variance = jnp.mean(centred * centred, axis=-1, keepdims=True)
    inverse = lax.rsqrt(variance + EPS)
    normed = centred * inverse
    return (normed * gain + offset, normed, inverse)


def norm_backward(out_grad, normed, inverse, gain):
    scaled = out_grad * gain
    inner = jnp.mean(scaled, axis=-1, keepdims=True)
    along = jnp.mean(scaled * normed, axis=-1, keepdims=True)
    return inverse * (scaled - inner - normed * along)


def gelu_exact(values):
    return 0.5 * values * (1.0 + lax.erf(values * 0.7071067811865476))


def gelu_slope(values):
    density = jnp.exp(-0.5 * values * values) * 0.3989422804014327
    return 0.5 * (1.0 + lax.erf(values * 0.7071067811865476)) + values * density


def offset_ones(extent):
    shape_three = (extent, extent, 2 * extent - 1)
    leading = lax.broadcasted_iota(jnp.int32, shape_three, 0)
    lagging = lax.broadcasted_iota(jnp.int32, shape_three, 1)
    target = lax.broadcasted_iota(jnp.int32, shape_three, 2)
    return (leading - lagging + extent - 1 == target).astype(jnp.float32)


def offset_ends(extent):
    spread = np.arange(2 * extent - 1)
    return (np.maximum(spread - (extent - 1), 0), np.maximum(extent - 1 - spread, 0))


def offset_labels(rel_index):
    time_lead, time_lag = offset_ends(WT)
    height_lead, height_lag = offset_ends(WH)
    width_lead, width_lag = offset_ends(WW)
    row_pos = (time_lead[:, None, None] * WH + height_lead[None, :, None]) * WW + width_lead[
        None, None, :
    ]
    col_pos = (time_lag[:, None, None] * WH + height_lag[None, :, None]) * WW + width_lag[
        None, None, :
    ]
    return rel_index[row_pos.astype(np.int32), col_pos.astype(np.int32)]


def to_block(windows, local_count):
    clip_count, chans = (windows.shape[0], windows.shape[-1])
    parted = windows.reshape(
        clip_count, local_count[0], local_count[1], local_count[2], WT, WH, WW, chans
    )
    parted = parted.transpose(0, 1, 4, 2, 5, 3, 6, 7)
    return parted.reshape(
        clip_count, local_count[0] * WT, local_count[1] * WH, local_count[2] * WW, chans
    )


def from_block(block, local_count):
    clip_count, chans = (block.shape[0], block.shape[-1])
    parted = block.reshape(
        clip_count, local_count[0], WT, local_count[1], WH, local_count[2], WW, chans
    )
    parted = parted.transpose(0, 1, 3, 5, 2, 4, 6, 7)
    return parted.reshape(clip_count, -1, WT * WH * WW, chans)


def roll_ahead(windows, local_count, bit_list):
    block = to_block(windows, local_count)
    for grid_dim, amount, bit_pos in (
        (1, WT // 2, bit_list[0]),
        (2, WH // 2, bit_list[1]),
        (3, WW // 2, bit_list[2]),
    ):
        if bit_pos < 0:
            block = jnp.roll(block, -amount, axis=grid_dim)
        else:
            front = lax.slice_in_dim(block, 0, amount, axis=grid_dim)
            arrived = from_partner(front, "seq", bit_pos)
            rest = lax.slice_in_dim(block, amount, block.shape[grid_dim], axis=grid_dim)
            block = jnp.concatenate([rest, arrived], axis=grid_dim)
    return from_block(block, local_count)


def roll_behind(windows, local_count, bit_list):
    block = to_block(windows, local_count)
    for grid_dim, amount, bit_pos in (
        (1, WT // 2, bit_list[0]),
        (2, WH // 2, bit_list[1]),
        (3, WW // 2, bit_list[2]),
    ):
        if bit_pos < 0:
            block = jnp.roll(block, amount, axis=grid_dim)
        else:
            extent = block.shape[grid_dim]
            trailing = lax.slice_in_dim(block, extent - amount, extent, axis=grid_dim)
            arrived = from_partner(trailing, "seq", bit_pos)
            rest = lax.slice_in_dim(block, 0, extent - amount, axis=grid_dim)
            block = jnp.concatenate([arrived, rest], axis=grid_dim)
    return from_block(block, local_count)


def body(
    tokens,
    norm1_gain,
    norm1_bias,
    qkv_weight,
    qv_bias,
    position_table,
    proj_weight,
    proj_bias,
    norm2_gain,
    norm2_bias,
    fc1_weight,
    fc1_bias,
    fc2_weight,
    fc2_bias,
    rel_index,
    region_ids,
    cotangent,
):
    levels = lax.axis_size("seq").bit_length() - 1
    local_count = [1 if levels > level_pos else 2 for level_pos in range(3)]
    bit_list = [levels - 1 - level_pos for level_pos in range(3)]
    clip_count, win_count, win_tokens, model_width = tokens.shape
    scale_factor = HEAD_DIM ** (-0.5)
    (
        gain_one,
        bias_one,
        w_qkv,
        qv_full,
        w_proj,
        b_proj,
        gain_two,
        bias_two,
        w_fc1,
        b_fc1,
        w_fc2,
        b_fc2,
    ) = (
        lax.all_gather(norm1_gain, "shard", axis=0, tiled=True),
        lax.all_gather(norm1_bias, "shard", axis=0, tiled=True),
        lax.all_gather(qkv_weight, "shard", axis=0, tiled=True),
        lax.all_gather(qv_bias, "shard", axis=0, tiled=True),
        lax.all_gather(proj_weight, "shard", axis=1, tiled=True),
        lax.all_gather(proj_bias, "shard", axis=0, tiled=True),
        lax.all_gather(norm2_gain, "shard", axis=0, tiled=True),
        lax.all_gather(norm2_bias, "shard", axis=0, tiled=True),
        lax.all_gather(fc1_weight, "shard", axis=0, tiled=True),
        lax.all_gather(fc1_bias, "shard", axis=0, tiled=True),
        lax.all_gather(fc2_weight, "shard", axis=1, tiled=True),
        lax.all_gather(fc2_bias, "shard", axis=0, tiled=True),
    )
    rows_in = tokens.astype(jnp.float32).reshape(-1, model_width)
    first, normed_one, inverse_one = norm_forward(
        rows_in, gain_one.astype(jnp.float32), bias_one.astype(jnp.float32)
    )
    first = first.astype(jnp.bfloat16)
    shifted = roll_ahead(
        first.reshape(clip_count, win_count, win_tokens, model_width), local_count, bit_list
    )
    shifted = shifted.reshape(-1, model_width)
    qkv = jnp.dot(shifted, w_qkv, preferred_element_type=jnp.float32)
    qv_wide = qv_full.astype(jnp.float32)
    qkv = qkv + jnp.concatenate(
        [qv_wide[:model_width], jnp.zeros((model_width,), jnp.float32), qv_wide[model_width:]]
    )
    clip_shape = (clip_count, win_count, win_tokens, model_width)
    queries = qkv[:, :model_width].astype(jnp.bfloat16).reshape(clip_shape)
    key_rows = qkv[:, model_width : 2 * model_width].astype(jnp.bfloat16).reshape(clip_shape)
    value_rows = qkv[:, 2 * model_width :].astype(jnp.bfloat16).reshape(clip_shape)
    labels = offset_labels(rel_index)
    ones_time, ones_height, ones_width = (offset_ones(WT), offset_ones(WH), offset_ones(WW))
    offset_table = jnp.take(position_table.astype(jnp.float32), labels, axis=0)
    pos_bias = jnp.einsum(
        "opqh,abo,cdp,efq->hacebdf",
        offset_table,
        ones_time,
        ones_height,
        ones_width,
        precision=HIGH,
    ).reshape(HEADS, win_tokens, win_tokens)
    same_region = region_ids[:, :, None] == region_ids[:, None, :]
    head_shape = (win_count, win_tokens, HEADS, HEAD_DIM)

    def clip_scores(query_part, key_part):
        scores = (
            jnp.einsum(
                "wihd,wjhd->whij",
                query_part.reshape(head_shape),
                key_part.reshape(head_shape),
                preferred_element_type=jnp.float32,
            )
            * scale_factor
        )
        return jnp.where(same_region[:, None], scores + pos_bias[None], MASKED)

    def attend_clip(inputs):
        query_part, key_part, value_part = inputs
        scores = clip_scores(query_part, key_part)
        top_score = jnp.max(scores, axis=-1, keepdims=True)
        expo = jnp.exp(scores - top_score)
        total = jnp.sum(expo, axis=-1, keepdims=True)
        attn_low = (expo / total).astype(jnp.bfloat16)
        context = jnp.einsum(
            "whij,wjhd->wihd",
            attn_low,
            value_part.reshape(head_shape),
            preferred_element_type=jnp.float32,
        )
        context = context.astype(jnp.bfloat16).reshape(win_count, win_tokens, model_width)
        return (context, (top_score + jnp.log(total))[..., 0])

    context, log_total = lax.map(attend_clip, (queries, key_rows, value_rows))
    context_back = roll_behind(context, local_count, bit_list).reshape(-1, model_width)
    branch = jnp.dot(context_back, w_proj, preferred_element_type=jnp.float32) + b_proj.astype(
        jnp.float32
    )
    mid = rows_in + branch
    second, normed_two, inverse_two = norm_forward(
        mid, gain_two.astype(jnp.float32), bias_two.astype(jnp.float32)
    )
    second = second.astype(jnp.bfloat16)
    hidden = jnp.dot(second, w_fc1, preferred_element_type=jnp.float32) + b_fc1.astype(jnp.float32)
    act = gelu_exact(hidden).astype(jnp.bfloat16)
    mlp = jnp.dot(act, w_fc2, preferred_element_type=jnp.float32) + b_fc2.astype(jnp.float32)
    block_out = (mid + mlp).astype(jnp.bfloat16).reshape(tokens.shape)
    w_qkv, w_proj, w_fc1, w_fc2, gain_one, gain_two = (
        lax.all_gather(qkv_weight, "shard", axis=0, tiled=True),
        lax.all_gather(proj_weight, "shard", axis=1, tiled=True),
        lax.all_gather(fc1_weight, "shard", axis=0, tiled=True),
        lax.all_gather(fc2_weight, "shard", axis=1, tiled=True),
        lax.all_gather(norm1_gain, "shard", axis=0, tiled=True),
        lax.all_gather(norm2_gain, "shard", axis=0, tiled=True),
    )
    out_grad = cotangent.reshape(-1, model_width)
    fc2_grad = jnp.einsum("tf,td->fd", act, out_grad, preferred_element_type=jnp.float32)
    fc2_bias_grad = jnp.sum(out_grad.astype(jnp.float32), axis=0)
    act_grad = jnp.einsum("td,fd->tf", out_grad, w_fc2, preferred_element_type=jnp.float32)
    hidden_grad = (act_grad * gelu_slope(hidden)).astype(jnp.bfloat16)
    fc1_grad = jnp.einsum("td,tf->df", second, hidden_grad, preferred_element_type=jnp.float32)
    fc1_bias_grad = jnp.sum(hidden_grad.astype(jnp.float32), axis=0)
    second_grad = jnp.einsum("tf,df->td", hidden_grad, w_fc1, preferred_element_type=jnp.float32)
    mid_grad = out_grad.astype(jnp.float32) + norm_backward(
        second_grad, normed_two, inverse_two, gain_two.astype(jnp.float32)
    )
    norm2_gain_grad = jnp.sum(second_grad * normed_two, axis=0)
    norm2_bias_grad = jnp.sum(second_grad, axis=0)
    branch_grad = mid_grad.astype(jnp.bfloat16)
    proj_grad = jnp.einsum(
        "td,te->de", context_back, branch_grad, preferred_element_type=jnp.float32
    )
    proj_bias_grad = jnp.sum(branch_grad.astype(jnp.float32), axis=0)
    back_grad = jnp.einsum(
        "te,de->td", branch_grad, w_proj, preferred_element_type=jnp.float32
    ).astype(jnp.bfloat16)
    context_grad = roll_ahead(back_grad.reshape(clip_shape), local_count, bit_list)

    def attend_back(table_total, inputs):
        query_part, key_part, value_part, log_part, grad_part = inputs
        scores = clip_scores(query_part, key_part)
        attn = jnp.exp(scores - log_part[..., None])
        attn_low = attn.astype(jnp.bfloat16)
        grad_heads = grad_part.reshape(head_shape)
        value_grad = jnp.einsum(
            "whij,wihd->wjhd", attn_low, grad_heads, preferred_element_type=jnp.float32
        )
        prob_grad = jnp.einsum(
            "wihd,wjhd->whij",
            grad_heads,
            value_part.reshape(head_shape),
            preferred_element_type=jnp.float32,
        )
        inner = jnp.sum(prob_grad * attn, axis=-1, keepdims=True)
        score_grad = (attn * (prob_grad - inner)).astype(jnp.bfloat16)
        query_grad = (
            jnp.einsum(
                "whij,wjhd->wihd",
                score_grad,
                key_part.reshape(head_shape),
                preferred_element_type=jnp.float32,
            )
            * scale_factor
        )
        key_grad = (
            jnp.einsum(
                "whij,wihd->wjhd",
                score_grad,
                query_part.reshape(head_shape),
                preferred_element_type=jnp.float32,
            )
            * scale_factor
        )
        flat_shape = (win_count, win_tokens, model_width)
        table_total = table_total + jnp.sum(score_grad.astype(jnp.float32), axis=0)
        return (
            table_total,
            (
                query_grad.astype(jnp.bfloat16).reshape(flat_shape),
                key_grad.astype(jnp.bfloat16).reshape(flat_shape),
                value_grad.astype(jnp.bfloat16).reshape(flat_shape),
            ),
        )

    table_total, (query_grad, key_grad, value_grad) = lax.scan(
        attend_back,
        jnp.zeros((HEADS, win_tokens, win_tokens), jnp.float32),
        (queries, key_rows, value_rows, log_total, context_grad),
    )
    qkv_grad = jnp.concatenate(
        [
            query_grad.reshape(-1, model_width),
            key_grad.reshape(-1, model_width),
            value_grad.reshape(-1, model_width),
        ],
        axis=1,
    )
    qkv_wgrad = jnp.einsum("td,te->de", shifted, qkv_grad, preferred_element_type=jnp.float32)
    qv_grad = jnp.concatenate(
        [
            jnp.sum(query_grad.astype(jnp.float32), axis=(0, 1, 2)),
            jnp.sum(value_grad.astype(jnp.float32), axis=(0, 1, 2)),
        ]
    )
    shifted_grad = jnp.einsum(
        "te,de->td", qkv_grad, w_qkv, preferred_element_type=jnp.float32
    ).astype(jnp.bfloat16)
    first_grad = roll_behind(shifted_grad.reshape(clip_shape), local_count, bit_list)
    first_grad = first_grad.reshape(-1, model_width).astype(jnp.float32)
    input_grad = mid_grad + norm_backward(
        first_grad, normed_one, inverse_one, gain_one.astype(jnp.float32)
    )
    norm1_gain_grad = jnp.sum(first_grad * normed_one, axis=0)
    norm1_bias_grad = jnp.sum(first_grad, axis=0)
    table_grid = table_total.reshape(HEADS, WT, WH, WW, WT, WH, WW)
    offset_grad = jnp.einsum(
        "hacebdf,abo,cdp,efq->opqh", table_grid, ones_time, ones_height, ones_width, precision=HIGH
    )
    table_grad = (
        jnp.zeros((position_table.shape[0], HEADS), jnp.float32)
        .at[labels.reshape(-1)]
        .set(offset_grad.reshape(-1, HEADS))
    )
    table_grad = lax.psum(table_grad, ("seq", "shard"))
    (
        sum_g1,
        sum_b1,
        sum_qkv,
        sum_qv,
        sum_proj,
        sum_pb,
        sum_g2,
        sum_b2,
        sum_fc1,
        sum_f1b,
        sum_fc2,
        sum_f2b,
    ) = (
        lax.psum(norm1_gain_grad.astype(jnp.bfloat16), "seq").astype(jnp.float32),
        lax.psum(norm1_bias_grad.astype(jnp.bfloat16), "seq").astype(jnp.float32),
        lax.psum(qkv_wgrad.astype(jnp.bfloat16), "seq").astype(jnp.float32),
        lax.psum(qv_grad.astype(jnp.bfloat16), "seq").astype(jnp.float32),
        lax.psum(proj_grad.astype(jnp.bfloat16), "seq").astype(jnp.float32),
        lax.psum(proj_bias_grad.astype(jnp.bfloat16), "seq").astype(jnp.float32),
        lax.psum(norm2_gain_grad.astype(jnp.bfloat16), "seq").astype(jnp.float32),
        lax.psum(norm2_bias_grad.astype(jnp.bfloat16), "seq").astype(jnp.float32),
        lax.psum(fc1_grad.astype(jnp.bfloat16), "seq").astype(jnp.float32),
        lax.psum(fc1_bias_grad.astype(jnp.bfloat16), "seq").astype(jnp.float32),
        lax.psum(fc2_grad.astype(jnp.bfloat16), "seq").astype(jnp.float32),
        lax.psum(fc2_bias_grad.astype(jnp.bfloat16), "seq").astype(jnp.float32),
    )
    (
        own_g1,
        own_b1,
        own_qkv,
        own_qv,
        own_proj,
        own_pb,
        own_g2,
        own_b2,
        own_fc1,
        own_f1b,
        own_fc2,
        own_f2b,
    ) = (
        lax.psum_scatter(
            sum_g1.astype(jnp.bfloat16), "shard", scatter_dimension=0, tiled=True
        ).astype(jnp.float32),
        lax.psum_scatter(
            sum_b1.astype(jnp.bfloat16), "shard", scatter_dimension=0, tiled=True
        ).astype(jnp.float32),
        lax.psum_scatter(
            sum_qkv.astype(jnp.bfloat16), "shard", scatter_dimension=0, tiled=True
        ).astype(jnp.float32),
        lax.psum_scatter(
            sum_qv.astype(jnp.bfloat16), "shard", scatter_dimension=0, tiled=True
        ).astype(jnp.float32),
        lax.psum_scatter(
            sum_proj.astype(jnp.bfloat16), "shard", scatter_dimension=1, tiled=True
        ).astype(jnp.float32),
        lax.psum_scatter(
            sum_pb.astype(jnp.bfloat16), "shard", scatter_dimension=0, tiled=True
        ).astype(jnp.float32),
        lax.psum_scatter(
            sum_g2.astype(jnp.bfloat16), "shard", scatter_dimension=0, tiled=True
        ).astype(jnp.float32),
        lax.psum_scatter(
            sum_b2.astype(jnp.bfloat16), "shard", scatter_dimension=0, tiled=True
        ).astype(jnp.float32),
        lax.psum_scatter(
            sum_fc1.astype(jnp.bfloat16), "shard", scatter_dimension=0, tiled=True
        ).astype(jnp.float32),
        lax.psum_scatter(
            sum_f1b.astype(jnp.bfloat16), "shard", scatter_dimension=0, tiled=True
        ).astype(jnp.float32),
        lax.psum_scatter(
            sum_fc2.astype(jnp.bfloat16), "shard", scatter_dimension=1, tiled=True
        ).astype(jnp.float32),
        lax.psum_scatter(
            sum_f2b.astype(jnp.bfloat16), "shard", scatter_dimension=0, tiled=True
        ).astype(jnp.float32),
    )
    return (
        block_out,
        input_grad.reshape(tokens.shape),
        own_g1,
        own_b1,
        own_qkv,
        own_qv,
        table_grad,
        own_proj,
        own_pb,
        own_g2,
        own_b2,
        own_fc1,
        own_f1b,
        own_fc2,
        own_f2b,
    )


def solution(mesh):
    return jax.shard_map(
        body,
        mesh=mesh,
        in_specs=(
            P("shard", "seq", None, None),
            P("shard"),
            P("shard"),
            P("shard", None),
            P("shard"),
            P(),
            P(None, "shard"),
            P("shard"),
            P("shard"),
            P("shard"),
            P("shard", None),
            P("shard"),
            P(None, "shard"),
            P("shard"),
            P(),
            P("seq", None),
            P("shard", "seq", None, None),
        ),
        out_specs=(
            P("shard", "seq", None, None),
            P("shard", "seq", None, None),
            P("shard"),
            P("shard"),
            P("shard", None),
            P("shard"),
            P(),
            P(None, "shard"),
            P("shard"),
            P("shard"),
            P("shard"),
            P("shard", None),
            P("shard"),
            P(None, "shard"),
            P("shard"),
        ),
        check_vma=False,
    )
```

profile of v0, /device:TPU:0, one launch (start us, length us, event | category | flops | bytes accessed | tf_op | source)
XLA Modules:
  0.0 1617.6 jit_solution(2397668901893098953)
XLA Ops:
  16.5 44.9 %all-reduce.16 = (bf16[1024]{0:T(1024)(128)(2,1)}, bf16[512]{0:T(512)(128)(2,1)S(1)}, bf16[512]{0:T(512)(128)(2,1)S(1)}, bf16[512]{0:T(512)(128)(2,1)}, bf16[512]{0:T(512)(128)(2,1)}, /*index=5*/bf16[512]{0:T(512)(128)(2,1)}) all-reduce(bf16[1024]{0:T(1024)(128)(2,1)S(1)} %dynamic-update-slice.2, ...), channel_id=1, replica_groups=mesh['seq'=2,'shard'=16] {'shard'}, use_global_device_ids=true, to_apply=%add.2 | all-reduce | flops 3584 | bytes 14336
  61.4 6.5 reshape.400
  70.0 7.4 convert_bitcast_fusion
  80.0 32.8 %gather_fusion = s32[2535]{0:T(1024)S(1)} fusion(s32[392,392]{1,0:T(8,128)S(1)} %copy-done, s32[2535]{0:T(1024)S(1)} %copy-done.2), kind=kCustom, calls=%fused_computation | custom fusion | bytes 40560 | tf_op jit(solution)/shard_map/gather | solution.py:71
  114.1 4.3 gather_fusion.1
  125.3 3.7 convolution_bitcast_fusion.2
  129.0 12.5 convolution_bitcast_fusion.1
  141.6 45.1 %convolution_bitcast_fusion = f32[16,8,7,7,8,7,7]{0,6,3,5,2,4,1:T(8,128)} fusion(f32[8,8,13,16,7,7,1]{3,5,4,2,1,0,6:T(8,128)} %convolution_bitcast_fusion.1), kind=kOutput, calls=%fused_computation.14 | convolution fusion | flops 383547264 | bytes 12443648 | tf_op jit(solution)/shard_map/opqh,abo,cdp,efq->hacebdf/dot_general | solution.py:201
  186.7 59.0 %copy.93 = f32[16,8,7,7,8,7,7]{0,6,5,4,3,2,1:T(8,128)} copy(f32[16,8,7,7,8,7,7]{0,6,3,5,2,4,1:T(8,128)} %convolution_bitcast_fusion) | data formatting | bytes 19668992 | tf_op jit(solution)/shard_map/opqh,abo,cdp,efq->hacebdf/transpose | solution.py:201
  245.6 85.5 %add.242 = f32[16,392,392]{0,2,1:T(8,128)} reshape(f32[16,8,7,7,8,7,7]{0,6,5,4,3,2,1:T(8,128)} %copy.93) | data formatting | bytes 19668992 | tf_op jit(solution)/shard_map/while/body/eval_jaxpr/add | solution.py:222
  331.2 54.5 %copy.94 = f32[16,392,392]{1,2,0:T(8,128)} copy(f32[16,392,392]{0,2,1:T(8,128)} %add.242) | data formatting | bytes 19668992 | tf_op jit(solution)/shard_map/while/body/eval_jaxpr/add | solution.py:222
  393.1 4.6 add_convert_fusion
  402.8 4.3 reshape.405
  407.0 3.5 copy.84
  410.5 6.5 reshape.404
  417.1 4.1 copy.83
  421.2 7.2 reshape.403
  428.4 25.6 %fusion.83 = (f32[4,16,392]{2,1,0:T(8,128)S(1)}, f32[4,16,392,392]{2,3,1,0:T(8,128)}) fusion(f32[16,392,392]{1,2,0:T(8,128)} %copy.94, bf16[4,392,16,32]{1,0,3,2:T(4,128)(2,1)} %reshape.405, bf16[4,392,16,32]{1,0,3,2:T(4,128)(2,1)S(1)} %reshape.404, pred[4,392,392]{1,2,0:T(8,128)(4,1)S(1)} %copy-done.23), kind=kOutput, calls=%fused_computation.159 | convolution fusion | flops 668720640 | bytes 53098752 | tf_op jit(solution)/shard_map/while/body/eval_jaxpr/wihd,wjhd->whij/dot_general | solution.py:214
  453.9 16.9 %fusion.2 = f32[4,16,392]{2,1,0:T(8,128)S(1)} fusion(f32[4,16,392,392]{2,3,1,0:T(8,128)} %get-tuple-element.164, f32[4,16,392]{2,1,0:T(8,128)S(1)} %get-tuple-element.163), kind=kLoop, calls=%fused_computation.12 | loop fusion | flops 19643904 | bytes 39538688 | tf_op jit(solution)/shard_map/while/body/eval_jaxpr/reduce_sum | solution.py:229
  470.9 18.2 %convert_bitcast_fusion.2 = bf16[4,392,16,32]{1,3,2,0:T(8,128)(2,1)S(1)} fusion(f32[4,16,392,392]{2,3,1,0:T(8,128)} %get-tuple-element.164, f32[4,16,392]{2,1,0:T(8,128)S(1)} %fusion.2, f32[4,16,392]{2,1,0:T(8,128)S(1)} %get-tuple-element.163, bf16[4,392,16,32]{1,0,3,2:T(4,128)(2,1)S(1)} %copy-done.16), kind=kOutput, calls=%fused_computation.63 | convolution fusion | flops 659714048 | bytes 42749952 | tf_op jit(solution)/shard_map/while/body/eval_jaxpr/whij,wjhd->wihd/dot_general | solution.py:231
  489.1 6.2 copy.97
  495.3 8.9 reshape.406
  507.8 35.3 %all-gather = bf16[16,1,128]{2,1,0:T(2,128)(2,1)S(1)} all-gather(bf16[1,1,128]{2,1,0:T(2,128)(2,1)S(1)} %bitcast.166), channel_id=1, replica_groups=mesh['seq'=2,'shard'=16] {'shard'}, dimensions={0}, use_global_device_ids=true | all-gather | bytes 4352 | tf_op jit(solution)/shard_map/all_gather | solution.py:176
  543.1 40.5 %all_gather.46 = bf16[512,512]{0,1:T(8,128)(2,1)S(1)} all-gather(bf16[512,32]{0,1:T(8,128)(2,1)S(1)} %copy-done.44), channel_id=1, replica_groups=mesh['seq'=2,'shard'=16] {'shard'}, dimensions={1}, use_global_device_ids=true | all-gather | bytes 557056 | tf_op jit(solution)/shard_map/all_gather | solution.py:171
  587.0 3.6 fusion.84
  593.0 10.9 multiply_convert_fusion.1
  603.9 11.0 fusion.87
  614.9 5.2 multiply_reduce_fusion.1
  634.8 5.6 reshape.413
  640.4 7.1 copy.102
  647.5 36.1 %multiply_reduce_fusion = (f32[4,16,392]{2,1,0:T(8,128)S(1)}, f32[4,16,392,392]{2,3,1,0:T(8,128)}) fusion(f32[4,16,392,392]{2,3,1,0:T(8,128)} %get-tuple-element.164, f32[4,16,392]{2,1,0:T(8,128)S(1)} %log_add_fusion, bf16[4,392,16,32]{1,3,2,0:T(8,128)(2,1)S(1)} %copy.102, bf16[4,392,16,32]{1,0,3,2:T(4,128)(2,1)} %reshape.403), kind=kOutput, calls=%fused_computation.7 | convolution fusion | flops 658886144 | bytes 82087936 | tf_op jit(solution)/shard_map/while/body/eval_jaxpr/wihd,wjhd->whij/dot_general | solution.py:294
  683.6 49.8 %convert_reduce_fusion = (f32[16,392,392]{1,2,0:T(8,128)}, bf16[4,16,392,392]{2,3,1,0:T(8,128)(2,1)}) fusion(f32[4,16,392,392]{2,3,1,0:T(8,128)} %get-tuple-element.171, f32[4,16,392]{2,1,0:T(8,128)S(1)} %get-tuple-element.170, f32[4,16,392,392]{2,3,1,0:T(8,128)} %get-tuple-element.164, f32[4,16,392]{2,1,0:T(8,128)S(1)} %log_add_fusion), kind=kLoop, calls=%fused_computation.5 | loop fusion | flops 56548352 | bytes 108380160 | tf_op jit(solution)/shard_map/while/body/eval_jaxpr/reduce_sum | solution.py:321
  733.4 14.5 fusion.86
  747.9 13.8 fusion.39
  761.7 20.8 %fusion.85 = (bf16[16,32]{1,0:T(8,128)(2,1)}, bf16[4,392,16,32]{1,3,2,0:T(8,128)(2,1)}) fusion(bf16[4,392,16,32]{1,3,2,0:T(8,128)(2,1)} %copy-done.13, f32[4,16,392,392]{2,3,1,0:T(8,128)} %get-tuple-element.164, f32[4,16,392]{2,1,0:T(8,128)S(1)} %log_add_fusion), kind=kOutput, calls=%fused_computation.161 | convolution fusion | flops 650681856 | bytes 42650624 | tf_op jit(solution)/shard_map/while/body/eval_jaxpr/whij,wihd->wjhd/dot_general | solution.py:291
  785.6 5.5 reshape.414
  793.8 3.1 copy.109
  796.9 5.1 reshape.415
  802.0 3.1 copy.112
  805.1 4.9 reshape.416
  810.0 45.9 %copy.115 = f32[16,392,392]{0,2,1:T(8,128)} copy(f32[16,392,392]{1,2,0:T(8,128)} %get-tuple-element.140) | data formatting | bytes 19668992 | tf_op jit(solution)/shard_map/while/body/eval_jaxpr/reduce_sum | solution.py:321
  855.9 86.0 %reshape.420 = f32[16,8,7,7,8,7,7]{0,6,5,4,3,2,1:T(8,128)} reshape(f32[16,392,392]{0,2,1:T(8,128)} %copy.115) | data formatting | bytes 19668992 | tf_op jit(solution)/shard_map/reshape | solution.py:361
  941.9 88.0 %fusion.17 = f32[13,16,8,7,8,7]{1,0,5,4,3,2:T(8,128)} fusion(f32[16,8,7,7,8,7,7]{0,6,5,4,3,2,1:T(8,128)} %reshape.420, pred[7,7,13,1,1,1,1]{2,1,0,6,5,4,3:T(8,128)(4,1)S(1)} %copy-done.46), kind=kOutput, calls=%fused_computation.30 | convolution fusion | flops 383545344 | bytes 12444285 | tf_op jit(solution)/shard_map/hacebdf,abo,cdp,efq->opqh/dot_general | solution.py:362
  1029.9 30.5 %fusion.23 = f32[13,16,8,8,13]{1,4,3,2,0:T(8,128)} fusion(f32[13,16,8,7,8,7]{1,0,5,4,3,2:T(8,128)} %fusion.17), kind=kOutput, calls=%fused_computation.60 | convolution fusion | flops 101758840 | bytes 3301376 | tf_op jit(solution)/shard_map/hacebdf,abo,cdp,efq->opqh/dot_general | solution.py:362
  1060.4 10.2 copy.134
  1070.6 8.0 convolution_bitcast_fusion.3
  1083.7 11.0 scatter_custom_fusion
  1099.0 6.8 convolution_convert_fusion.3
  1105.9 9.6 convolution_convert_fusion.2
  1115.6 8.3 convolution_convert_fusion.1
  1124.0 7.1 convolution_convert_fusion.4
  1138.5 4.4 convolution_convert_fusion.5
  1143.2 79.0 %all-reduce.22.cloned.1.call-done = f32[2535,16]{1,0:T(8,128)} async-done(((f32[2535,16]{1,0:T(8,128)}), f32[2535,16]{1,0:T(8,128)}) %all-reduce.22.cloned.1.call-update) | async-done | bytes 162256 | tf_op jit(solution)/shard_map/psum | solution.py:370
  1227.6 24.2 %fusion.22 = (bf16[512]{0:T(512)(128)(2,1)S(1)}, f32[2,2,8,7,7]{4,3,2,1,0:T(8,128)S(1)}, f32[2,2,8,7,7]{4,3,2,1,0:T(8,128)S(1)}, f32[2,2,8,7,7,512]{5,4,3,2,1,0:T(8,128)}) fusion(f32[1,1,8,2,7,2,7,512]{7,2,6,5,4,3,1,0:T(8,128)S(1)} %convert.27, f32[2,2,8,7,7]{4,3,2,1,0:T(8,128)S(1)} %copy-done.30, f32[1,1,2,2,8,7,7,512]{7,0,6,5,4,3,2,1:T(1,128)S(1)} %copy-done.6, ...), kind=kLoop, calls=%fused_computation.41 | loop fusion | flops 6418880 | bytes 9661952 | tf_op jit(solution)/shard_map/reduce_sum | solution.py:359
  1251.8 75.4 %all-reduce.15 = (bf16[512]{0:T(512)(128)(2,1)S(1)}, bf16[512]{0:T(512)(128)(2,1)S(1)}, bf16[512]{0:T(512)(128)(2,1)S(1)}, bf16[1024]{0:T(1024)(128)(2,1)S(1)}, ...) all-reduce(bf16[512]{0:T(512)(128)(2,1)S(1)} %dynamic-update-slice., ...), channel_id=1, replica_groups=mesh['seq'=2,'shard'=16] {'shard'}, use_global_device_ids=true, to_apply=%add.6 | all-reduce | flops 6656 | bytes 26624
  1327.3 4.7 reshape.422
  1332.4 9.2 add_convert_fusion.1
  1341.6 9.0 reduce-scatter.5.cloned.1.call-done
  1350.6 81.7 %reduce-scatter.9.cloned.1.call-done = bf16[32,2048]{1,0:T(8,128)(2,1)} async-done(((bf16[512,2048]{1,0:T(8,128)(2,1)}), bf16[32,2048]{1,0:T(8,128)(2,1)}) %reduce-scatter.9.cloned.1.call-update) | async-done | bytes 131088 | tf_op jit(solution)/shard_map/reduce_scatter | solution.py:436
  1432.3 80.3 %reduce-scatter.11.cloned.1.call-done = bf16[2048,32]{0,1:T(8,128)(2,1)} async-done(((bf16[2048,512]{0,1:T(8,128)(2,1)}), bf16[2048,32]{0,1:T(8,128)(2,1)}) %reduce-scatter.11.cloned.1.call-update) | async-done | bytes 131088 | tf_op jit(solution)/shard_map/reduce_scatter | solution.py:442
  1512.6 4.7 multiply_add_fusion
  1517.9 70.4 %reduce-scatter.7.cloned.1.call-done = bf16[512,32]{0,1:T(8,128)(2,1)} async-done(((bf16[512,512]{0,1:T(8,128)(2,1)}), bf16[512,32]{0,1:T(8,128)(2,1)}) %reduce-scatter.7.cloned.1.call-update) | async-done | bytes 32784 | tf_op jit(solution)/shard_map/reduce_scatter | solution.py:424
  1588.3 4.1 all-reduce.17
  1597.1 8.9 all-reduce.24.cloned.1.call-done
  (280 shorter events, 93.8 us)
Async XLA Ops:
  7.2 72.8 %copy-start = (s32[392,392]{1,0:T(8,128)S(1)}, s32[392,392]{1,0:T(8,128)}, u32[]{:S(2)}) copy-start(s32[392,392]{1,0:T(8,128)} %param.35) | copy-start | bytes 1843972
  7.2 60.8 %copy-start.3 = (bf16[1,4,392,512]{3,2,1,0:T(8,128)(2,1)S(1)}, bf16[1,4,392,512]{3,2,1,0:T(8,128)(2,1)}, u32[]{:S(2)}) copy-start(bf16[1,4,392,512]{3,2,1,0:T(8,128)(2,1)} %param.21) | copy-start | bytes 4816900
  7.2 385.9 %all-gather.5.cloned.1.call-start = ((), (), s32[]{:S(2)}) async-start(), calls=%async_computation.4 | async-start | bytes 1671168 | tf_op jit(solution)/shard_map/all_gather | solution.py:169
  7.9 585.1 %all-gather.7.cloned.1.call-start = ((), (), s32[]{:S(2)}) async-start(), calls=%async_computation.5 | async-start | bytes 2228224 | tf_op jit(solution)/shard_map/all_gather | solution.py:175
  8.7 595.2 %all-gather.9.cloned.1.call-start = ((), (), s32[]{:S(2)}) async-start(), calls=%async_computation.6 | async-start | bytes 2228224 | tf_op jit(solution)/shard_map/all_gather | solution.py:177
  61.4 8.0 copy-start.40
  68.3 9.1 copy-start.33
  68.5 9.0 copy-start.27
  69.2 8.2 copy-start.38
  79.7 307.5 %collective-permute-start = (bf16[1,4,14,14,512]{4,1,3,2,0:T(4,128)(2,1)}, bf16[1,4,14,14,512]{4,1,3,2,0:T(4,128)(2,1)}, u32[]{:S(2)}, u32[]{:S(2)}) collective-permute-start(bf16[1,4,14,14,512]{4,1,3,2,0:T(4,128)(2,1)} %get-tuple-element.157), channel_id=1, source_target_pairs={{0,16},{16,0},{1,17},{17,1},{2,18},{18,2},{3,19},{19,3},{4,20},{20... | collective-permute-start | bytes 2408456 | tf_op jit(solution)/shard_map/ppermute | solution.py:20
  79.7 33.9 %copy-start.35 = (bf16[2535,16]{0,1:T(8,128)(2,1)S(1)}, bf16[2535,16]{0,1:T(8,128)(2,1)}, u32[]{:S(2)}) copy-start(bf16[2535,16]{0,1:T(8,128)(2,1)} %param.26) | copy-start | bytes 243364
  79.7 1142.5 %all-reduce.22.cloned.1.call-start = ((), (), s32[]{:S(2)}) async-start(), calls=%async_computation.7 | async-start | bytes 2596864 | tf_op jit(solution)/shard_map/psum | solution.py:370
  331.2 54.5 %copy-start.51 = (bf16[1024]{0:T(1024)(128)(2,1)S(1)}, bf16[1024]{0:T(1024)(128)(2,1)}, u32[]{:S(2)}) copy-start(bf16[1024]{0:T(1024)(128)(2,1)} %get-tuple-element.122) | copy-start | bytes 6148
  331.2 54.5 %copy-start.45 = (s32[4,392]{1,0:T(4,128)S(1)}, s32[4,392]{1,0:T(4,128)}, u32[]{:S(2)}) copy-start(s32[4,392]{1,0:T(4,128)} %param.36) | copy-start | bytes 18820
  331.2 56.0 %copy-start.14 = (bf16[1,4,14,14,512]{4,1,3,2,0:T(4,128)(2,1)S(1)}, bf16[1,4,14,14,512]{4,1,3,2,0:T(4,128)(2,1)}, u32[]{:S(2)}) copy-start(bf16[1,4,14,14,512]{4,1,3,2,0:T(4,128)(2,1)} %get-tuple-element.158) | copy-start | bytes 2408452
  417.0 11.3 copy-start.10
  417.0 11.3 copy-start.23
  453.9 16.9 %copy-start.16 = (bf16[4,392,16,32]{1,0,3,2:T(4,128)(2,1)S(1)}, bf16[4,392,16,32]{1,0,3,2:T(4,128)(2,1)}, u32[]{:S(2)}) copy-start(bf16[4,392,16,32]{1,0,3,2:T(4,128)(2,1)} %reshape.403) | copy-start | bytes 4816900
  470.9 18.3 %copy-start.31 = (f32[4,16,392]{2,1,0:T(8,128)}, f32[4,16,392]{2,1,0:T(8,128)S(1)}, u32[]{:S(2)}) copy-start(f32[4,16,392]{2,1,0:T(8,128)S(1)} %fusion.2) | copy-start | bytes 301060
  505.1 2.7 copy-start.58
  505.1 2.7 copy-start.61
  505.1 37.9 %copy-start.57 = (bf16[512]{0:T(512)(128)(2,1)S(1)}, bf16[512]{0:T(512)(128)(2,1)}, u32[]{:S(2)}) copy-start(bf16[512]{0:T(512)(128)(2,1)} %get-tuple-element.126) | copy-start | bytes 3076
  505.1 37.9 %copy-start.56 = (bf16[512]{0:T(512)(128)(2,1)S(1)}, bf16[512]{0:T(512)(128)(2,1)}, u32[]{:S(2)}) copy-start(bf16[512]{0:T(512)(128)(2,1)} %get-tuple-element.127) | copy-start | bytes 3076
  505.1 38.0 %copy-start.44 = (bf16[512,32]{0,1:T(8,128)(2,1)S(1)}, bf16[512,32]{0,1:T(8,128)(2,1)}, u32[]{:S(2)}) copy-start(bf16[512,32]{0,1:T(8,128)(2,1)} %param.27) | copy-start | bytes 98308
  505.1 78.5 %collective-permute-start.1 = (bf16[1,4,14,14,512]{4,1,3,2,0:T(4,128)(2,1)S(1)}, bf16[1,4,14,14,512]{4,1,3,2,0:T(4,128)(2,1)S(1)}, u32[]{:S(2)}, u32[]{:S(2)}) collective-permute-start(bf16[1,4,14,14,512]{4,1,3,2,0:T(4,128)(2,1)S(1)} %get-tuple-element.155), channel_id=1, source_target_pairs={{0,16},{16,0},{1,17},{17,1},{2,18},{18,2},{3,19},{19,3},{4,20},{20... | collective-permute-start | bytes 2408456 | tf_op jit(solution)/shard_map/ppermute | solution.py:20
  543.1 50.0 %copy-start.54 = (f32[512]{0:T(512)}, f32[512]{0:T(512)S(1)}, u32[]{:S(2)}) copy-start(f32[512]{0:T(512)S(1)} %convert_element_type.247) | copy-start | bytes 6148
  543.1 77.0 %copy-start.49 = (f32[512]{0:T(512)}, f32[512]{0:T(512)S(1)}, u32[]{:S(2)}) copy-start(f32[512]{0:T(512)S(1)} %convert_element_type.246) | copy-start | bytes 6148
  590.6 29.5 %copy-start.36 = (f32[1568]{0:T(1024)}, f32[1568]{0:T(1024)S(1)}, u32[]{:S(2)}) copy-start(f32[1568]{0:T(1024)S(1)} %broadcast_multiply_fusion.4) | copy-start | bytes 18820
  593.0 27.2 %copy-start.42 = (f32[1568]{0:T(1024)}, f32[1568]{0:T(1024)S(1)}, u32[]{:S(2)}) copy-start(f32[1568]{0:T(1024)S(1)} %add_rsqrt_fusion) | copy-start | bytes 18820
  593.0 10.9 copy-start.20
  603.9 11.0 copy-start.8
  603.9 11.0 copy-start.62
  614.9 5.2 copy-start.64
  628.7 2.6 copy-start.32
  630.0 2.4 collective-permute-start.2
  647.5 36.1 %copy-start.13 = (bf16[4,392,16,32]{1,3,2,0:T(8,128)(2,1)}, bf16[4,392,16,32]{1,3,2,0:T(8,128)(2,1)S(1)}, u32[]{:S(2)}) copy-start(bf16[4,392,16,32]{1,3,2,0:T(8,128)(2,1)S(1)} %copy.102) | copy-start | bytes 4816900
  683.6 49.8 %copy-start.12 = (bf16[4,392,16,32]{1,0,3,2:T(4,128)(2,1)S(1)}, bf16[4,392,16,32]{1,0,3,2:T(4,128)(2,1)}, u32[]{:S(2)}) copy-start(bf16[4,392,16,32]{1,0,3,2:T(4,128)(2,1)} %reshape.405) | copy-start | bytes 4816900
  733.4 14.5 copy-start.11
  761.7 20.8 %copy-start.18 = (bf16[4,392,16,32]{1,3,2,0:T(8,128)(2,1)S(1)}, bf16[4,392,16,32]{1,3,2,0:T(8,128)(2,1)}, u32[]{:S(2)}) copy-start(bf16[4,392,16,32]{1,3,2,0:T(8,128)(2,1)} %get-tuple-element.175) | copy-start | bytes 4816900
  785.6 8.2 copy-start.15
  796.9 5.1 copy-start.17
  855.9 86.0 %copy-start.46 = (pred[7,7,13,1,1,1,1]{2,1,0,6,5,4,3:T(8,128)(4,1)S(1)}, pred[7,7,13,1,1,1,1]{2,1,0,6,5,4,3:T(8,128)(4,1)}, u32[]{:S(2)}) copy-start(pred[7,7,13,1,1,1,1]{2,1,0,6,5,4,3:T(8,128)(4,1)} %fusion.116) | copy-start | bytes 1915
  1081.1 13.7 copy-start.19
  1094.7 255.8 %reduce-scatter.5.cloned.1.call-start = ((), (), s32[]{:S(2)}) async-start(), calls=%async_computation.8 | async-start | bytes 1671168 | tf_op jit(solution)/shard_map/reduce_scatter | solution.py:418
  1094.8 4.2 copy-start.26
  1099.0 6.9 copy-start.37
  1099.0 6.9 copy-start.43
  1099.0 6.9 copy-start.50
  1099.0 6.9 copy-start.55
  1105.8 9.8 copy-start.21
  1105.8 326.5 %reduce-scatter.9.cloned.1.call-start = ((), (), s32[]{:S(2)}) async-start(), calls=%async_computation.10 | async-start | bytes 2228224 | tf_op jit(solution)/shard_map/reduce_scatter | solution.py:436
  1115.5 397.1 %reduce-scatter.11.cloned.1.call-start = ((), (), s32[]{:S(2)}) async-start(), calls=%async_computation.11 | async-start | bytes 2228224 | tf_op jit(solution)/shard_map/reduce_scatter | solution.py:442
  1123.9 464.4 %reduce-scatter.7.cloned.1.call-start = ((), (), s32[]{:S(2)}) async-start(), calls=%async_computation.9 | async-start | bytes 557056 | tf_op jit(solution)/shard_map/reduce_scatter | solution.py:424
  1134.4 3.9 copy-start.63
  1135.8 88.8 %collective-permute-start.3 = (bf16[1,4,14,14,512]{4,1,3,2,0:T(4,128)(2,1)}, bf16[1,4,14,14,512]{4,1,3,2,0:T(4,128)(2,1)S(1)}, u32[]{:S(2)}, u32[]{:S(2)}) collective-permute-start(bf16[1,4,14,14,512]{4,1,3,2,0:T(4,128)(2,1)} %get-tuple-element.151), channel_id=1, source_target_pairs={{0,16},{16,0},{1,17},{17,1},{2,18},{18,2},{3,19},{19,3},{4,20},{20... | collective-permute-start | bytes 2408456 | tf_op jit(solution)/shard_map/ppermute | solution.py:20
  1138.5 4.5 copy-start.47
  1138.5 4.6 copy-start.48
  1143.0 463.0 %all-reduce.24.cloned.1.call-start = ((), (), s32[]{:S(2)}) async-start(), calls=%async_computation.12 | async-start | bytes 720896 | tf_op jit(solution)/shard_map/psum | solution.py:387
  1227.5 24.3 %copy-start.52 = (bf16[512]{0:T(512)(128)(2,1)S(1)}, bf16[512]{0:T(512)(128)(2,1)}, u32[]{:S(2)}) copy-start(bf16[512]{0:T(512)(128)(2,1)} %get-tuple-element.142) | copy-start | bytes 3076
  1227.5 24.3 %copy-start.53 = (bf16[2048]{0:T(1024)(128)(2,1)S(1)}, bf16[2048]{0:T(1024)(128)(2,1)}, u32[]{:S(2)}) copy-start(bf16[2048]{0:T(1024)(128)(2,1)} %get-tuple-element.176) | copy-start | bytes 12292
  1227.6 24.2 %copy-start.59 = (bf16[512]{0:T(512)(128)(2,1)S(1)}, bf16[512]{0:T(512)(128)(2,1)}, u32[]{:S(2)}) copy-start(bf16[512]{0:T(512)(128)(2,1)} %get-tuple-element.107) | copy-start | bytes 3076
  1227.6 24.2 %copy-start.60 = (bf16[512]{0:T(512)(128)(2,1)S(1)}, bf16[512]{0:T(512)(128)(2,1)}, u32[]{:S(2)}) copy-start(bf16[512]{0:T(512)(128)(2,1)} %get-tuple-element.111) | copy-start | bytes 3076
  1332.4 180.2 %copy-start.5 = (bf16[1,4,392,512]{3,2,1,0:T(8,128)(2,1)S(1)}, bf16[1,4,392,512]{3,2,1,0:T(8,128)(2,1)}, u32[]{:S(2)}) copy-start(bf16[1,4,392,512]{3,2,1,0:T(8,128)(2,1)} %param.21) | copy-start | bytes 4816900
  1512.6 98.2 %copy-start.1 = (s32[392,392]{1,0:T(8,128)S(1)}, s32[392,392]{1,0:T(8,128)}, u32[]{:S(2)}) copy-start(s32[392,392]{1,0:T(8,128)} %param.35) | copy-start | bytes 1843972
  (14 other events, 23.8 us)
Sparse Core Ops, SparseCore 0:
  10.8 60.7 all-gather.4
  74.4 59.4 all-gather.6
  136.7 59.3 all-gather.8
  1094.9 127.2 all-reduce.21
  1226.8 123.6 reduce-scatter.4
  1352.7 79.5 reduce-scatter.8
  1434.5 77.9 reduce-scatter.10
  1514.8 73.4 reduce-scatter.6
  1591.0 14.9 all-reduce.23
where the time goes:
time: 1630 us; the launch traced here: 1620 us
  local copies, waits for them, and re-layouts  536 us (33%)
  matrix products  400 us (25%)
  waiting for transfers between devices  332 us (20%)
  blocking collectives  200 us (12%)
  other arithmetic  131 us (8%)
  between operations  18.4 us (1%)
    add x2, local copies, waits for them, and re-layouts, clip_scores(): return jnp.where(same_region[:, None], scores + pos_bias[None], MASKED)  140 us
    dot_general x3, matrix products, body(): jnp.einsum('hacebdf,abo,cdp,efq->opqh', table_grid, ones_time, ones_heigh...  126 us
    unnamed x2, blocking collectives  120 us
    reshape x1, local copies, waits for them, and re-layouts, body(): table_grid = table_total.reshape(HEADS, WT, WH, WW, WT, WH, WW)  86 us
    reduce_scatter x1, waiting for transfers between devices, body(): lax.psum_scatter(sum_fc1.astype(jnp.bfloat16), 'shard', scatter_dimension...  81.7 us
    reduce_scatter x1, waiting for transfers between devices, body(): lax.psum_scatter(sum_fc2.astype(jnp.bfloat16), 'shard', scatter_dimension...  80.3 us
    psum x1, waiting for transfers between devices, body(): table_grad = lax.psum(table_grad, ('seq', 'shard'))  79 us
    reduce_scatter x1, waiting for transfers between devices, body(): lax.psum_scatter(sum_proj.astype(jnp.bfloat16), 'shard', scatter_dimensio...  70.4 us
  transfers between devices with their start and end apart: 13, of which 7 were waited for; matrix products, arithmetic and copies ran while one was open for 35% of the time, Pallas kernels for 0%

commit v1 on v0

v1 whole, which is shorter than its diff:
```python
import jax
import jax.numpy as jnp
import numpy as np
from jax import lax
from jax.experimental import pallas as pl
from jax.experimental.pallas import tpu as pltpu
from jax.sharding import PartitionSpec as P

HEADS = 16
HEAD_DIM = 32
WT = 8
WH = 7
WW = 7
WIN_TOK = WT * WH * WW
EPS = 1e-05

BF=jnp.bfloat16; F32=jnp.float32
LOG2E=1.4426950408889634; LN2=0.6931471805599453
SCALE=HEAD_DIM**-0.5
BIG=-(2.0**30)
GROUP=4
VM=56*1024*1024

def nt(a,b): return lax.dot_general(a,b,(((1,),(1,)),((),())),preferred_element_type=F32)
def nn(a,b): return jnp.dot(a,b,preferred_element_type=F32)

def placed(block, at, rows):
    parts=[]
    if at: parts.append(jnp.zeros((at,block.shape[1]),block.dtype))
    parts.append(block)
    if rows-at-block.shape[0]: parts.append(jnp.zeros((rows-at-block.shape[0],block.shape[1]),block.dtype))
    return jnp.concatenate(parts,axis=0)

def attend_kernel(q_ref,k_ref,v_ref,bias_ref,mq_ref,mk_ref,ctx_ref,e_ref,r_ref):
    lhs=jnp.concatenate([k_ref[0],mk_ref[0]],axis=1)
    ones=jnp.ones((16,q_ref.shape[2]),BF)
    for h in range(GROUP):
        rows=slice(h*HEAD_DIM,(h+1)*HEAD_DIM)
        rhs=jnp.concatenate([placed(q_ref[0,rows,:],h*HEAD_DIM,GROUP*HEAD_DIM),placed(mq_ref[0],0,128)],axis=0)
        s=nn(lhs,rhs)+bias_ref[h]
        m=jnp.max(s,axis=0,keepdims=True)
        e=jnp.exp2(s-m).astype(BF)
        e_ref[0,h]=e
        c=nn(jnp.concatenate([v_ref[0,rows,:],ones],axis=0),e)
        r=1.0/c[HEAD_DIM:HEAD_DIM+1]
        ctx_ref[0,rows,:]=(c[:HEAD_DIM]*r).astype(BF)
        r_ref[0,0,h:h+1,:]=r

def attend(qT,k,vT,bias,mq,mk):
    nw,width,n=qT.shape
    ng=width//128
    return pl.pallas_call(
        attend_kernel,
        grid=(ng,nw),
        in_specs=[
            pl.BlockSpec((1,128,n),lambda g,w:(w,g,0)),
            pl.BlockSpec((1,n,128),lambda g,w:(w,0,g)),
            pl.BlockSpec((1,128,n),lambda g,w:(w,g,0)),
            pl.BlockSpec((GROUP,n,n),lambda g,w:(g,0,0)),
            pl.BlockSpec((1,32,n),lambda g,w:(w,0,0)),
            pl.BlockSpec((1,n,128),lambda g,w:(w,0,0)),
        ],
        out_specs=[
            pl.BlockSpec((1,128,n),lambda g,w:(w,g,0)),
            pl.BlockSpec((1,GROUP,n,n),lambda g,w:(w,g,0,0)),
            pl.BlockSpec((1,1,GROUP,n),lambda g,w:(w,g,0,0)),
        ],
        out_shape=[
            jax.ShapeDtypeStruct((nw,width,n),BF),
            jax.ShapeDtypeStruct((nw,ng*GROUP,n,n),BF),
            jax.ShapeDtypeStruct((nw,ng,GROUP,n),F32),
        ],
        compiler_params=pltpu.CompilerParams(vmem_limit_bytes=VM),
        name="attend",
    )(qT,k,vT,bias,mq,mk)

SPREAD=768
FLAT=1408
WIDE=2816

def spread_ones():
    n=WT*WH*WW
    tok=np.arange(n); c=tok//(WW*WT); e=tok//WT%WW; a=tok%WT
    out=np.zeros((n,SPREAD),np.float32); out[tok,c*104+e*8+a]=1
    return out

def lane16(mirror):
    out=np.zeros((128,256),np.float32)
    for u in range(16):
        for a in range(8):
            out[u*8+a,u*16+(7-a if mirror else a)]=1
    return out

def back_kernel(e_ref,k_ref,v_ref,q_ref,g_ref,ctx_ref,r_ref,sp_ref,l16_ref,dq_ref,dk_ref,dv_ref,tab_ref,tot,acc):
    w=pl.program_id(1); nw=pl.num_programs(1)
    n=q_ref.shape[2]
    dv=jnp.zeros((n,128),F32); dk=jnp.zeros((n,128),F32)
    @pl.when(w==0)
    def _():
        tot[...]=jnp.zeros_like(tot)
    for h in range(GROUP):
        rows=slice(h*HEAD_DIM,(h+1)*HEAD_DIM)
        go=g_ref[0,rows,:].astype(F32)*r_ref[0,0,h:h+1,:]
        inner=jnp.sum(go*ctx_ref[0,rows,:].astype(F32),axis=0,keepdims=True)
        rhs=placed(go.astype(BF),h*HEAD_DIM,128)
        e=e_ref[0,h]
        dp=nn(v_ref[0],rhs)
        ds=(e.astype(F32)*(dp-inner))
        dsl=ds.astype(BF)
        tot[h]+=ds
        dv+=nt(e,rhs)
        dk+=nt(dsl,placed(q_ref[0,rows,:],h*HEAD_DIM,128))
        dq_ref[0,rows,:]=(nn(k_ref[0,rows,:],dsl)*SCALE).astype(BF)
    dv_ref[0]=dv.astype(BF)
    dk_ref[0]=(dk*LN2).astype(BF)
    @pl.when(w==nw-1)
    def _():
        for h in range(GROUP):
            x=nn(tot[h].astype(BF),sp_ref[...])
            full=jnp.zeros((8,FLAT),F32)
            for d in range(WH):
                part=jnp.zeros((8,SPREAD),F32)
                for f in range(WW):
                    j=(d*WW+f)*8
                    part=part+pltpu.roll(x[j:j+8,:],8*(WW-1-f),1) if f<WW-1 else part+x[j:j+8,:]
                wide=jnp.concatenate([part,jnp.zeros((8,FLAT-SPREAD),F32)],axis=1)
                full=full+(pltpu.roll(wide,104*(WH-1-d),1) if d<WH-1 else wide)
            acc[h*8:(h+1)*8,:]=full
        a=acc[...]
        hi=a.astype(BF); lo=(a-hi.astype(F32)).astype(BF)
        wide=[]
        for t in range(FLAT//128):
            c=slice(t*128,(t+1)*128)
            wide.append(nn(hi[:,c],l16_ref[...])+nn(lo[:,c],l16_ref[...]))
        y=jnp.concatenate(wide,axis=1)
        for h in range(GROUP):
            z=pltpu.roll(y[h*8:(h+1)*8,:],0,1,stride=1,stride_axis=0)
            tab_ref[0,h:h+1,:]=jnp.sum(z,axis=0,keepdims=True)

def attend_back(e,kT,v,qT,gT,ctxT,r,sp,l16):
    nw,width,n=qT.shape
    ng=width//128
    feat=pl.BlockSpec((1,128,n),lambda g,w:(w,g,0))
    tok=pl.BlockSpec((1,n,128),lambda g,w:(w,0,g))
    return pl.pallas_call(
        back_kernel,
        grid=(ng,nw),
        in_specs=[
            pl.BlockSpec((1,GROUP,n,n),lambda g,w:(w,g,0,0)),
            feat,tok,feat,feat,feat,
            pl.BlockSpec((1,1,GROUP,n),lambda g,w:(w,g,0,0)),
            pl.BlockSpec(sp.shape,lambda g,w:(0,0)),
            pl.BlockSpec(l16.shape,lambda g,w:(0,0)),
        ],
        out_specs=[feat,tok,tok,pl.BlockSpec((1,GROUP,WIDE),lambda g,w:(g,0,0))],
        out_shape=[
            jax.ShapeDtypeStruct((nw,width,n),BF),
            jax.ShapeDtypeStruct((nw,n,width),BF),
            jax.ShapeDtypeStruct((nw,n,width),BF),
            jax.ShapeDtypeStruct((ng,GROUP,WIDE),F32),
        ],
        scratch_shapes=[pltpu.VMEM((GROUP,n,n),F32),pltpu.VMEM((GROUP*8,FLAT),F32)],
        compiler_params=pltpu.CompilerParams(vmem_limit_bytes=VM),
        name="attend_back",
    )(e,kT,v,qT,gT,ctxT,r,sp,l16)

def lane_maps(mirror):
    lane=np.arange(WIDE); pq=lane//16; o=lane%16
    p=pq//13; q=pq%13
    ok=(pq<169)&(o<15)
    if mirror: o=14-o
    A=o>=7; b=np.where(A,14-o,7-o); C=p>=6; d=np.where(C,12-p,6-p); E=q>=6; f=np.where(E,12-q,6-q)
    col=(b*WH+d)*WW+f
    corner=A*4+C*2+E*1
    return np.where(ok,col,-1).astype(np.int32), np.where(ok,corner,-1).astype(np.int32)

CORNER_ROWS=[(a*WH+c)*WW+e for a in (0,WT-1) for c in (0,WH-1) for e in (0,WW-1)]
TROWS=2560

def pick_kernel(rel_ref,maps_ref,table_ref,lab_ref,val_ref):
    rel=rel_ref[...]
    hi=(rel>>6).astype(F32).astype(BF); lo=(rel&63).astype(F32).astype(BF)
    both=jnp.concatenate([hi,lo],axis=0)
    n=rel.shape[1]
    corners=lax.broadcasted_iota(jnp.int32,(8,256),0)
    rows=lax.broadcasted_iota(jnp.int32,(n,256),0)
    trow=lax.broadcasted_iota(jnp.int32,(TROWS,256),0)
    for t in range(WIDE//256):
        c=slice(t*256,(t+1)*256)
        for version in range(2):
            col=maps_ref[2*version:2*version+1,c]; cor=maps_ref[2*version+1:2*version+2,c]
            m=jnp.where(rows==col,1.0,0.0).astype(BF)
            y=nn(both,m)
            full=y[:8]*64.0+y[8:]
            lab=jnp.sum(jnp.where(corners==cor,full,0.0),axis=0,keepdims=True)
            lab=jnp.where(cor>=0,lab,-1.0).astype(jnp.int32)
            lab_ref[version:version+1,c]=lab
            if version==0:
                hot=jnp.where(trow==lab,1.0,0.0).astype(BF)
                val_ref[:,c]=nn(table_ref[...],hot)

def pick(rel8,maps,tableT):
    return pl.pallas_call(
        pick_kernel,
        out_shape=[jax.ShapeDtypeStruct((2,WIDE),jnp.int32),jax.ShapeDtypeStruct((HEADS,WIDE),F32)],
        compiler_params=pltpu.CompilerParams(vmem_limit_bytes=VM),
        name="pick",
    )(rel8,maps,tableT)

def bias_kernel(val_ref,l8_ref,sp_ref,bias_ref,x_ref):
    base=jnp.broadcast_to(val_ref[0],(8,WIDE))
    z=pltpu.roll(base,WIDE-7,1,stride=1,stride_axis=0).astype(BF)
    narrow=jnp.concatenate([nn(z[:,t*256:(t+1)*256],l8_ref[...]) for t in range(FLAT//128)],axis=1)
    for d in range(WH):
        s=FLAT-104*(WH-1-d)
        wide=(pltpu.roll(narrow,s,1) if d<WH-1 else narrow)[:,:SPREAD]
        for f in range(WW):
            j=(d*WW+f)*8
            x_ref[j:j+8,:]=pltpu.roll(wide,SPREAD-8*(WW-1-f),1) if f<WW-1 else wide
    bias_ref[0]=nt(x_ref[...].astype(BF),sp_ref[...])*LOG2E

def bias_all(val,l8,sp):
    n=sp.shape[0]
    return pl.pallas_call(
        bias_kernel,
        grid=(HEADS,),
        in_specs=[pl.BlockSpec((1,1,WIDE),lambda h:(h,0,0)),pl.BlockSpec(l8.shape,lambda h:(0,0)),pl.BlockSpec(sp.shape,lambda h:(0,0))],
        out_specs=pl.BlockSpec((1,n,n),lambda h:(h,0,0)),
        out_shape=jax.ShapeDtypeStruct((HEADS,n,n),F32),
        scratch_shapes=[pltpu.VMEM((n,SPREAD),F32)],
        compiler_params=pltpu.CompilerParams(vmem_limit_bytes=VM),
        name="position_bias",
    )(val.reshape(HEADS,1,WIDE),l8,sp)

def spill_kernel(lab_ref,g_ref,out_ref):
    g=g_ref[...]
    hi=g.astype(BF); r1=g-hi.astype(F32); mid=r1.astype(BF); lo=(r1-mid.astype(F32)).astype(BF)
    three=jnp.concatenate([hi,mid,lo],axis=0)
    trow=lax.broadcasted_iota(jnp.int32,(TROWS,256),0)
    tot=jnp.zeros((48,TROWS),F32)
    for t in range(WIDE//256):
        c=slice(t*256,(t+1)*256)
        hot=jnp.where(trow==lab_ref[1:2,c],1.0,0.0).astype(BF)
        tot=tot+nt(three[:,c],hot)
    out_ref[...]=tot[:16]+tot[16:32]+tot[32:]

def spill(lab,g):
    return pl.pallas_call(
        spill_kernel,
        out_shape=jax.ShapeDtypeStruct((HEADS,TROWS),F32),
        compiler_params=pltpu.CompilerParams(vmem_limit_bytes=VM),
        name="table_rows",
    )(lab,g)


def from_partner(shard, axis, stride):
    return lax.ppermute(shard, axis, [(i, i ^ 1 << stride) for i in range(lax.axis_size(axis))])


def norm_forward(values, gain, offset):
    mean = jnp.mean(values, axis=-1, keepdims=True)
    centred = values - mean
    variance = jnp.mean(centred * centred, axis=-1, keepdims=True)
    inverse = lax.rsqrt(variance + EPS)
    normed = centred * inverse
    return (normed * gain + offset, normed, inverse)


def norm_backward(out_grad, normed, inverse, gain):
    scaled = out_grad * gain
    inner = jnp.mean(scaled, axis=-1, keepdims=True)
    along = jnp.mean(scaled * normed, axis=-1, keepdims=True)
    return inverse * (scaled - inner - normed * along)


def gelu_exact(values):
    return 0.5 * values * (1.0 + lax.erf(values * 0.7071067811865476))


def gelu_slope(values):
    density = jnp.exp(-0.5 * values * values) * 0.3989422804014327
    return 0.5 * (1.0 + lax.erf(values * 0.7071067811865476)) + values * density


def to_block(windows, local_count):
    clip_count, chans = (windows.shape[0], windows.shape[-1])
    parted = windows.reshape(
        clip_count, local_count[0], local_count[1], local_count[2], WT, WH, WW, chans
    )
    parted = parted.transpose(0, 1, 4, 2, 5, 3, 6, 7)
    return parted.reshape(
        clip_count, local_count[0] * WT, local_count[1] * WH, local_count[2] * WW, chans
    )


def from_block(block, local_count):
    clip_count, chans = (block.shape[0], block.shape[-1])
    parted = block.reshape(
        clip_count, local_count[0], WT, local_count[1], WH, local_count[2], WW, chans
    )
    parted = parted.transpose(0, 1, 3, 5, 2, 4, 6, 7)
    return parted.reshape(clip_count, -1, WT * WH * WW, chans)


def roll_ahead(windows, local_count, bit_list):
    block = to_block(windows, local_count)
    for grid_dim, amount, bit_pos in (
        (1, WT // 2, bit_list[0]),
        (2, WH // 2, bit_list[1]),
        (3, WW // 2, bit_list[2]),
    ):
        if bit_pos < 0:
            block = jnp.roll(block, -amount, axis=grid_dim)
        else:
            front = lax.slice_in_dim(block, 0, amount, axis=grid_dim)
            arrived = from_partner(front, "seq", bit_pos)
            rest = lax.slice_in_dim(block, amount, block.shape[grid_dim], axis=grid_dim)
            block = jnp.concatenate([rest, arrived], axis=grid_dim)
    return from_block(block, local_count)


def roll_behind(windows, local_count, bit_list):
    block = to_block(windows, local_count)
    for grid_dim, amount, bit_pos in (
        (1, WT // 2, bit_list[0]),
        (2, WH // 2, bit_list[1]),
        (3, WW // 2, bit_list[2]),
    ):
        if bit_pos < 0:
            block = jnp.roll(block, amount, axis=grid_dim)
        else:
            extent = block.shape[grid_dim]
            trailing = lax.slice_in_dim(block, extent - amount, extent, axis=grid_dim)
            arrived = from_partner(trailing, "seq", bit_pos)
            rest = lax.slice_in_dim(block, 0, extent - amount, axis=grid_dim)
            block = jnp.concatenate([arrived, rest], axis=grid_dim)
    return from_block(block, local_count)


HALF = 200


def hwt_order():
    place = np.arange(WIN_TOK)
    return (place % WT * WH + place // (WW * WT)) * WW + place // WT % WW


def roll_sources():
    own = np.full((4, WIN_TOK), -1)
    arrived = np.full((4, WIN_TOK), -1)
    for win in range(4):
        for place in range(WIN_TOK):
            t, h, w = place % WT, place // (WW * WT), place // WT % WW
            h = (win // 2 * WH + h + WH // 2) % (2 * WH)
            w = (win % 2 * WW + w + WW // 2) % (2 * WW)
            source = h // WH * 2 + w // WW
            inside = h % WH * WW + w % WW
            if t < WT // 2:
                own[win, place] = source * WIN_TOK + (t + WT // 2) * WH * WW + inside
            else:
                arrived[win, place] = source * HALF + (t - WT // 2) * WH * WW + inside
    return own.reshape(-1), arrived.reshape(-1)


def one_hot_rows(source, columns):
    return (jnp.asarray(source, jnp.int32)[:, None] == jnp.arange(columns, dtype=jnp.int32)[None, :]).astype(BF)


def swap_cores(part):
    return lax.ppermute(part, "seq", [(0, 1), (1, 0)])


def enter(windows, plan):
    clips, wins, toks, width = windows.shape
    if plan["levels"] == 1:
        arrived = swap_cores(windows[:, :, :HALF]).reshape(clips, wins * HALF, width)
        flat = windows.reshape(clips, wins * toks, width)
        own_hot, arrived_hot = plan["hots"]
        out = [
            jnp.dot(own_hot, flat[i], preferred_element_type=F32) + jnp.dot(arrived_hot, arrived[i], preferred_element_type=F32)
            for i in range(clips)
        ]
        return jnp.stack(out).astype(BF).reshape(clips * wins, toks, width)
    rolled = roll_ahead(windows, plan["local"], plan["bits"])
    rolled = rolled.reshape(clips * wins, WT, WH * WW, width).transpose(0, 2, 1, 3)
    return rolled.reshape(clips * wins, toks, width)


def leave(windows, plan, clips):
    count, toks, width = windows.shape
    wins = count // clips
    if plan["levels"] == 1:
        flat = windows.reshape(clips, wins * toks, width)
        own_hot, arrived_hot = plan["hots"]
        sent = jnp.stack([nt_first(arrived_hot, flat[i]) for i in range(clips)]).astype(BF)
        got = swap_cores(sent).reshape(clips, wins, HALF, width)
        kept = jnp.stack([nt_first(own_hot, flat[i]) for i in range(clips)]).astype(BF)
        kept = kept.reshape(clips, wins, toks, width)
        return kept + jnp.pad(got, ((0, 0), (0, 0), (0, toks - HALF), (0, 0)))
    rows = windows.reshape(count, WH * WW, WT, width).transpose(0, 2, 1, 3)
    return roll_behind(rows.reshape(clips, wins, toks, width), plan["local"], plan["bits"])


def nt_first(hot, rows):
    return lax.dot_general(hot, rows, (((0,), (0,)), ((), ())), preferred_element_type=F32)


def body(
    tokens, norm1_gain, norm1_bias, qkv_weight, qv_bias, position_table, proj_weight, proj_bias, norm2_gain,
    norm2_bias, fc1_weight, fc1_bias, fc2_weight, fc2_bias, rel_index, region_ids, cotangent,
):
    levels = lax.axis_size("seq").bit_length() - 1
    own_rows, arrived_rows = roll_sources()
    plan = {
        "levels": levels,
        "local": [1 if levels > level_pos else 2 for level_pos in range(3)],
        "bits": [levels - 1 - level_pos for level_pos in range(3)],
        "hots": (one_hot_rows(own_rows, 4 * WIN_TOK), one_hot_rows(arrived_rows, 4 * HALF)),
    }
    clips, wins, toks, width = tokens.shape
    gather = lambda part, axis: lax.all_gather(part, "shard", axis=axis, tiled=True)
    vectors = jnp.concatenate([norm1_gain, norm1_bias, qv_bias, proj_bias, norm2_gain, norm2_bias, fc1_bias, fc2_bias])
    vectors = lax.all_gather(vectors, "shard", axis=0, tiled=False).astype(F32)
    cuts = np.cumsum([part.shape[0] for part in (norm1_gain, norm1_bias, qv_bias, proj_bias, norm2_gain, norm2_bias, fc1_bias)])
    gain_one, bias_one, qv_full, b_proj, gain_two, bias_two, b_fc1, b_fc2 = [
        part.reshape(-1) for part in jnp.split(vectors, cuts, axis=1)
    ]
    w_qkv, w_proj, w_fc1, w_fc2 = gather(qkv_weight, 0), gather(proj_weight, 1), gather(fc1_weight, 0), gather(fc2_weight, 1)

    spread = jnp.asarray(spread_ones(), BF)
    wide8 = jnp.asarray(lane16(False).T, BF)
    wide16 = jnp.asarray(lane16(True), BF)
    maps = jnp.asarray(np.stack(lane_maps(False) + lane_maps(True)))
    rel8 = jnp.concatenate([rel_index[row : row + 1] for row in CORNER_ROWS], axis=0)
    table_rows = jnp.pad(position_table.T, ((0, 0), (0, TROWS - position_table.shape[0])))
    labels, values = pick(rel8, maps, table_rows)
    bias = bias_all(values, wide8, spread)

    region = region_ids[:, hwt_order()]
    region = jnp.broadcast_to(region[None], (clips, wins, toks)).reshape(-1, toks)
    mask_keys = (region[:, :, None] == jnp.arange(128)).astype(BF)
    mask_queries = jnp.where(region[:, None, :] == jnp.arange(32)[:, None], 0.0, BIG).astype(BF)

    rows_in = enter(tokens, plan).astype(F32)
    out_grad = enter(cotangent, plan)
    first, normed_one, inverse_one = norm_forward(rows_in, gain_one, bias_one)
    first = first.astype(BF)
    feature = jnp.einsum("de,wnd->wen", w_qkv, first, preferred_element_type=F32)
    q_t = ((feature[:, :width] + qv_full[:width, None]) * (SCALE * LOG2E)).astype(BF)
    k_t = feature[:, width : 2 * width].astype(BF)
    v_t = (feature[:, 2 * width :] + qv_full[width:, None]).astype(BF)
    token_k = jnp.einsum("wnd,de->wne", first, w_qkv[:, width : 2 * width], preferred_element_type=F32).astype(BF)
    token_v = jnp.einsum("wnd,de->wne", first, w_qkv[:, 2 * width :], preferred_element_type=F32)
    token_v = (token_v + qv_full[width:]).astype(BF)

    context_t, expo, inverse_sum = attend(q_t, token_k, v_t, bias, mask_queries, mask_keys)

    branch = jnp.einsum("wdn,de->wne", context_t, w_proj, preferred_element_type=F32) + b_proj
    mid = rows_in + branch
    second, normed_two, inverse_two = norm_forward(mid, gain_two, bias_two)
    second = second.astype(BF)
    hidden = jnp.einsum("wnd,df->wnf", second, w_fc1, preferred_element_type=F32) + b_fc1
    act = gelu_exact(hidden).astype(BF)
    mlp = jnp.einsum("wnf,fd->wnd", act, w_fc2, preferred_element_type=F32) + b_fc2
    block_out = leave((mid + mlp).astype(BF), plan, clips)

    fc2_grad = jnp.einsum("wnf,wnd->fd", act, out_grad, preferred_element_type=F32)
    fc2_bias_grad = jnp.sum(out_grad.astype(F32), axis=(0, 1))
    act_grad = jnp.einsum("wnd,fd->wnf", out_grad, w_fc2, preferred_element_type=F32)
    hidden_grad = (act_grad * gelu_slope(hidden)).astype(BF)
    fc1_grad = jnp.einsum("wnd,wnf->df", second, hidden_grad, preferred_element_type=F32)
    fc1_bias_grad = jnp.sum(hidden_grad.astype(F32), axis=(0, 1))
    second_grad = jnp.einsum("wnf,df->wnd", hidden_grad, w_fc1, preferred_element_type=F32)
    mid_grad = out_grad.astype(F32) + norm_backward(second_grad, normed_two, inverse_two, gain_two)
    norm2_gain_grad = jnp.sum(second_grad * normed_two, axis=(0, 1))
    norm2_bias_grad = jnp.sum(second_grad, axis=(0, 1))
    branch_grad = mid_grad.astype(BF)
    proj_grad = jnp.einsum("wdn,wne->de", context_t, branch_grad, preferred_element_type=F32)
    proj_bias_grad = jnp.sum(branch_grad.astype(F32), axis=(0, 1))
    context_grad_t = jnp.einsum("wne,de->wdn", branch_grad, w_proj, preferred_element_type=F32).astype(BF)

    dq_t, dk, dv, offsets = attend_back(expo, k_t, token_v, q_t, context_grad_t, context_t, inverse_sum, spread, wide16)

    wgrad_q = jnp.einsum("wnd,wen->de", first, dq_t, preferred_element_type=F32)
    wgrad_k = jnp.einsum("wnd,wne->de", first, dk, preferred_element_type=F32)
    wgrad_v = jnp.einsum("wnd,wne->de", first, dv, preferred_element_type=F32)
    qkv_wgrad = jnp.concatenate([wgrad_q, wgrad_k, wgrad_v], axis=1)
    qv_grad = jnp.concatenate([jnp.sum(dq_t.astype(F32), axis=(0, 2)), jnp.sum(dv.astype(F32), axis=(0, 1))])
    first_grad = (
        jnp.einsum("wen,de->wnd", dq_t, w_qkv[:, :width], preferred_element_type=F32)
        + jnp.einsum("wne,de->wnd", dk, w_qkv[:, width : 2 * width], preferred_element_type=F32)
        + jnp.einsum("wne,de->wnd", dv, w_qkv[:, 2 * width :], preferred_element_type=F32)
    )
    norm1_gain_grad = jnp.sum(first_grad * normed_one, axis=(0, 1))
    norm1_bias_grad = jnp.sum(first_grad, axis=(0, 1))
    input_grad = mid_grad + norm_backward(first_grad, normed_one, inverse_one, gain_one)
    input_grad = leave(input_grad.astype(BF), plan, clips).astype(F32)

    table_grad = spill(labels, lax.psum(offsets.reshape(HEADS, WIDE), ("seq", "shard")))
    table_grad = table_grad[:, : position_table.shape[0]].T

    def owned(grad, axis):
        total = lax.psum(grad.astype(BF), "seq")
        return lax.psum_scatter(total, "shard", scatter_dimension=axis, tiled=True).astype(F32)

    shards = lax.axis_size("shard")
    small = [norm1_gain_grad, norm1_bias_grad, qv_grad, proj_bias_grad, norm2_gain_grad, norm2_bias_grad, fc1_bias_grad, fc2_bias_grad]
    small = jnp.concatenate([part.reshape(shards, -1) for part in small], axis=1)
    small = lax.psum(small, ("seq", "shard"))
    small = lax.dynamic_index_in_dim(small, lax.axis_index("shard"), 0, keepdims=False)
    own_g1, own_b1, own_qv, own_pb, own_g2, own_b2, own_f1b, own_f2b = jnp.split(small, cuts)
    return (
        block_out, input_grad, own_g1, own_b1, owned(qkv_wgrad, 0), own_qv, table_grad, owned(proj_grad, 1), own_pb,
        own_g2, own_b2, owned(fc1_grad, 0), own_f1b, owned(fc2_grad, 1), own_f2b,
    )


def solution(mesh):
    return jax.shard_map(
        body,
        mesh=mesh,
        in_specs=(
            P("shard", "seq", None, None),
            P("shard"),
            P("shard"),
            P("shard", None),
            P("shard"),
            P(),
            P(None, "shard"),
            P("shard"),
            P("shard"),
            P("shard"),
            P("shard", None),
            P("shard"),
            P(None, "shard"),
            P("shard"),
            P(),
            P("seq", None),
            P("shard", "seq", None, None),
        ),
        out_specs=(
            P("shard", "seq", None, None),
            P("shard", "seq", None, None),
            P("shard"),
            P("shard"),
            P("shard", None),
            P("shard"),
            P(),
            P(None, "shard"),
            P("shard"),
            P("shard"),
            P("shard"),
            P("shard", None),
            P("shard"),
            P(None, "shard"),
            P("shard"),
        ),
        check_vma=False,
    )
```

time: 1630 us -> 806 us (0.49)
  local copies, waits for them, and re-layouts: 536 us -> 32.3 us
  matrix products: 400 us -> 116 us
  Pallas kernels: 0 us -> 105 us
  other arithmetic: 131 us -> 26.9 us
  blocking collectives: 200 us -> 127 us
  waiting for transfers between devices: 332 us -> 377 us
    dot_general x24 -> x26, matrix products: 400 us -> 116 us  [the longest x4 14.9 us: nt_first(): lax.dot_general(hot, rows, (((0,), (0,)), ((), ())), preferred_element_ty...]
    reshape x13 -> x8, local copies, waits for them, and re-layouts: 153 us -> 3.83 us  [the longest x1 1.72 us: bias_all(): val.reshape(HEADS, 1, WIDE)]
    add x2 -> x7, local copies, waits for them, and re-layouts: 140 us -> 0.53 us  [the longest x2 0.15 us: norm_forward(): return (normed * gain + offset, normed, inverse)]
    unnamed x9 -> x10, waiting for transfers between devices: 1.49 us -> 122 us
    unnamed x2 -> x0, blocking collectives: 120 us -> none
    pallas_call x0 -> x5, Pallas kernels: none -> 105 us  [the longest x1 41.4 us: attend_back(): pl.pallas_call(back_kernel, grid=(ng, nw), in_specs=[pl.BlockSpec((1, GRO...]
    reduce_sum x9 -> x3, other arithmetic: 94.5 us -> 5.02 us  [the longest x1 1.98 us: body(): jnp.sum(dq_t.astype(F32), axis=(0, 2))]
    psum x2, waiting for transfers between devices: 87.9 us -> 21.8 us  [the longest x1 13.5 us: owned(): total = lax.psum(grad.astype(BF), 'seq')]
  transfers between devices with their start and end apart: 13 -> 13, of which waited for: 7 -> 6; matrix products, arithmetic and copies ran while one was open for 35% -> 17% of each run, Pallas kernels for 0% -> 8%
where the time goes in v1:
time: 806 us; the launch traced here: 801 us
  waiting for transfers between devices  377 us (47%)
  blocking collectives  127 us (16%)
  matrix products  116 us (14%)
  Pallas kernels  105 us (13%)
  local copies, waits for them, and re-layouts  32.3 us (4%)
  other arithmetic  26.9 us (3%)
  between operations  14.7 us (2%)
    reduce_scatter x3, waiting for transfers between devices, owned(): lax.psum_scatter(total, 'shard', scatter_dimension=axis, tiled=True)  233 us
    unnamed x10, waiting for transfers between devices  122 us
    all_gather x1, blocking collectives, body(): vectors = lax.all_gather(vectors, 'shard', axis=0, tiled=False).astype(F32)  42.7 us
    all_gather x1, blocking collectives, body(): lax.all_gather(part, 'shard', axis=axis, tiled=True)  42.4 us
    pallas_call x1, Pallas kernels, attend_back(): pl.pallas_call(back_kernel, grid=(ng, nw), in_specs=[pl.BlockSpec((1, GRO...  41.4 us
    psum x1, blocking collectives, body(): small = lax.psum(small, ('seq', 'shard'))  37.5 us
    pallas_call x1, Pallas kernels, attend(): pl.pallas_call(attend_kernel, grid=(ng, nw), in_specs=[pl.BlockSpec((1, 1...  33.2 us
    pallas_call x1, Pallas kernels, bias_all(): pl.pallas_call(bias_kernel, grid=(HEADS,), in_specs=[pl.BlockSpec((1, 1,...  19.3 us
  transfers between devices with their start and end apart: 13, of which 6 were waited for; matrix products, arithmetic and copies ran while one was open for 17% of the time, Pallas kernels for 8%

profile of v1, /device:TPU:0, one launch (start us, length us, event | category | flops | bytes accessed | tf_op | source)
XLA Modules:
  0.0 800.7 jit_solution(14149786208548853090)
XLA Ops:
  8.9 2.1 slice.87
  11.4 1.2 slice.73
  13.0 42.7 %all-gather.1 = bf16[16,1,384]{2,1,0:T(2,128)(2,1)S(1)} all-gather(bf16[1,1,384]{2,1,0:T(2,128)(2,1)S(1)} %reshape.205), channel_id=2, replica_groups=mesh['seq'=2,'shard'=16] {'shard'}, dimensions={0}, use_global_device_ids=true | all-gather | bytes 13056 | tf_op jit(solution)/shard_map/all_gather | solution.py:423
  56.0 1.1 gather_fusion
  61.7 5.0 pick.1
  66.7 1.7 reshape.180.val_ref
  68.4 42.4 %all_gather.21 = bf16[512,512]{0,1:T(8,128)(2,1)} all-gather(bf16[512,32]{0,1:T(8,128)(2,1)S(1)} %copy-done.20), channel_id=1, replica_groups=mesh['seq'=2,'shard'=16] {'shard'}, dimensions={1}, use_global_device_ids=true | all-gather | bytes 557056 | tf_op jit(solution)/shard_map/all_gather | solution.py:421
  110.8 4.8 fusion.7
  115.6 19.3 %position_bias.1.bias_ref = f32[16,392,392]{2,1,0:T(8,128)} custom-call(f32[16,1,2816]{2,1,0:T(1,128)} %reshape.180.val_ref, bf16[256,128]{1,0:T(8,128)(2,1)} %constant.62.clone.l8_ref, bf16[392,768]{1,0:T(8,128)(2,1)} %constant.61.clone.sp_ref), custom_call_target="tpu_custom_call" | custom-call | tf_op jit(solution)/shard_map/position_bias/pallas_call | solution.py:224
  135.0 3.1 fusion.9
  138.1 3.1 fusion.56
  142.1 5.0 convert_reduce_fusion.2
  147.1 1.7 add_convert_fusion.5
  148.9 5.4 convolution_bitcast_fusion
  154.3 1.6 slice.121.k_ref
  156.9 2.1 convolution_convert_fusion.1.k_ref
  159.0 2.6 fusion.18
  161.6 33.2 %attend.1 = (bf16[4,512,392]{2,1,0:T(8,128)(2,1)}, bf16[4,16,392,392]{3,2,1,0:T(8,128)(2,1)}, f32[4,4,4,392]{3,2,1,0:T(4,128)}) custom-call(bf16[4,512,392]{2,1,0:T(8,128)(2,1)} %get-tuple-element.92.q_ref, bf16[4,392,512]{2,1,0:T(8,128)(2,1)} %convolution_convert_fusion.1.k_ref, bf16[4,512,392]{2,1,0:T(8,128)(2,1)} %get-tuple-element.91.v_ref, ...), custom_call_target="tpu_custom_call" | custom-call | tf_op jit(solution)/shard_map/attend/pallas_call | solution.py:52
  194.9 3.1 fusion.57
  198.0 1.7 copy-done.2
  200.4 2.1 add_convert_fusion.1.v_ref
  202.5 10.6 %multiply_convert_fusion = (bf16[4,392,2048]{2,1,0:T(8,128)(2,1)}, f32[4,392,2048]{2,1,0:T(8,128)}) fusion(f32[2048]{0:T(1024)S(1)} %slice_bitcast_fusion.9, bf16[512,2048]{1,0:T(8,128)(2,1)} %all-gather.8.cloned.1.call-done, f32[4,392,512]{2,1,0:T(8,128)} %copy-done.2, f32[512]{0:T(512)S(1)} %add.186, f32[512]{0:T(512)S(1)} %mul.147, ...), kind=kOutput, calls=%fused_computation.9 | convolution fusion | flops 3311616000 | bytes 24600832 | tf_op jit(solution)/shard_map/wnd,df->wnf/dot_general | solution.py:462
  213.1 11.7 %convert_reduce_fusion = (f32[2048]{0:T(1024)S(1)}, bf16[4,392,2048]{2,1,0:T(8,128)(2,1)S(1)}) fusion(f32[4,392,2048]{2,1,0:T(8,128)} %get-tuple-element.120, f32[2048]{0:T(1024)S(1)} %slice_bitcast_fusion.9, bf16[4,392,512]{2,1,0:T(8,128)(2,1)} %bitcast.140, bf16[2048,512]{0,1:T(8,128)(2,1)} %all-gather.10.cloned.1.call-done), kind=kOutput, calls=%fused_computation.8 | convolution fusion | flops 3330078720 | bytes 22986752 | tf_op jit(solution)/shard_map/wnd,fd->wnf/dot_general | solution.py:469
  224.8 4.7 multiply_reduce_fusion
  229.6 1.3 convert_reduce_fusion.3
  231.0 1.6 copy-done
  232.6 2.2 convolution_convert_fusion
  234.9 4.1 copy.65
  238.9 41.4 %attend_back.1 = (bf16[4,512,392]{2,1,0:T(8,128)(2,1)}, bf16[4,392,512]{2,1,0:T(8,128)(2,1)}, bf16[4,392,512]{2,1,0:T(8,128)(2,1)}, f32[4,4,2816]{2,1,0:T(4,128)}) custom-call(bf16[4,16,392,392]{3,2,1,0:T(8,128)(2,1)} %get-tuple-element.26.e_ref, bf16[4,512,392]{2,1,0:T(8,128)(2,1)} %slice.121.k_ref, bf16[4,392,512]{2,1,0:T(8,128)(2,1)} %add_convert_fusion.1.v_ref, ...), custom_call_target="tpu_custom_call" | custom-call | tf_op jit(solution)/shard_map/attend_back/pallas_call | solution.py:145
  280.3 1.7 reshape.193
  282.2 3.2 fusion.44
  285.5 1.1 fusion.42
  286.9 1.2 fusion.45
  288.0 1.2 pad_maximum_fusion
  289.3 2.6 copy.75
  291.9 8.7 %bitcast_convert_fusion = bf16[2048,512]{0,1:T(8,128)(2,1)} fusion(bf16[4,392,2048]{2,1,0:T(8,128)(2,1)} %get-tuple-element.119, bf16[4,392,512]{2,1,0:T(8,128)(2,1)} %bitcast.141), kind=kOutput, calls=%fused_computation.32 | convolution fusion | flops 3289382912 | bytes 10125312 | tf_op jit(solution)/shard_map/wnf,wnd->fd/dot_general | solution.py:467
  301.1 8.0 add_convert_fusion.3
  309.1 3.1 fusion.41
  312.4 2.0 convert_reduce_fusion.1
  314.4 1.7 convert_reduce_fusion.4
  316.2 9.4 %bitcast_convert_fusion.1 = bf16[512,2048]{1,0:T(8,128)(2,1)} fusion(bf16[4,392,2048]{2,1,0:T(8,128)(2,1)} %copy-done.35, f32[4,392,512]{2,1,0:T(8,128)} %copy-done.2, f32[512]{0:T(512)S(1)} %add.186, f32[512]{0:T(512)S(1)} %mul.147, f32[4,392]{1,0:T(4,128)S(1)} %add_rsqrt_fusion, f32[4,392]{1,0:T(4,128)S(1)} %broadcast_multiply_fusion.4), kind=kOutput, calls=%fused_computation.33 | convolution fusion | flops 3293396992 | bytes 11747584 | tf_op jit(solution)/shard_map/wnd,wnf->df/dot_general | solution.py:471
  325.9 3.2 fusion.47
  330.6 3.6 multiply_reduce_fusion.1
  334.3 3.4 add_convert_fusion
  337.8 3.1 fusion.40
  341.6 37.5 %psum.42 = f32[16,384]{1,0:T(8,128)S(1)} all-reduce(f32[16,384]{1,0:T(8,128)S(1)} %concatenate.26), channel_id=1, replica_groups=mesh['seq'=2,'shard'=16] {'seq','shard'}, use_global_device_ids=true, to_apply=%region_17.18 | all-reduce | flops 6144 | bytes 49152 | tf_op jit(solution)/shard_map/psum | solution.py:509
  379.1 3.7 fusion.43
  382.8 5.1 fusion.22
  388.0 3.6 fusion.23
  393.6 8.3 %all-reduce.7.cloned.1.call-done.g_ref = f32[16,2816]{1,0:T(8,128)} async-done(((f32[16,2816]{1,0:T(8,128)}), f32[16,2816]{1,0:T(8,128)}) %all-reduce.7.cloned.1.call-update) | async-done | bytes 180240 | tf_op jit(solution)/shard_map/psum | solution.py:499
  401.9 5.9 table_rows.1
  407.8 1.6 slice_bitcast_fusion.8
  409.4 2.6 pad_add_fusion
  412.0 120.7 %reduce-scatter.13.cloned.1.call-done = bf16[32,1536]{1,0:T(8,128)(2,1)} async-done(((bf16[512,1536]{1,0:T(8,128)(2,1)}), bf16[32,1536]{1,0:T(8,128)(2,1)}) %reduce-scatter.13.cloned.1.call-update) | async-done | bytes 98320
  532.6 1.8 copy.76
  534.4 79.9 %reduce-scatter.11.cloned.1.call-done = bf16[2048,32]{0,1:T(8,128)(2,1)} async-done(((bf16[2048,512]{0,1:T(8,128)(2,1)}), bf16[2048,32]{0,1:T(8,128)(2,1)}) %reduce-scatter.11.cloned.1.call-update) | async-done | bytes 131088 | tf_op jit(solution)/shard_map/reduce_scatter | solution.py:504
  614.4 80.2 %reduce-scatter.9.cloned.1.call-done = bf16[32,2048]{1,0:T(8,128)(2,1)} async-done(((bf16[512,2048]{1,0:T(8,128)(2,1)}), bf16[32,2048]{1,0:T(8,128)(2,1)}) %reduce-scatter.9.cloned.1.call-update) | async-done | bytes 131088 | tf_op jit(solution)/shard_map/reduce_scatter | solution.py:504
  694.7 3.3 add_convert_fusion.7
  697.9 72.8 %reduce-scatter.7.cloned.1.call-done = bf16[512,32]{0,1:T(8,128)(2,1)} async-done(((bf16[512,512]{0,1:T(8,128)(2,1)}), bf16[512,32]{0,1:T(8,128)(2,1)}) %reduce-scatter.7.cloned.1.call-update) | async-done | bytes 32784 | tf_op jit(solution)/shard_map/reduce_scatter | solution.py:504
  770.7 4.0 psum.49
  775.4 13.5 %all-reduce.9.cloned.1.call-done = (bf16[32,1536]{0,1:T(8,128)(2,1)}, bf16[32,2048]{1,0:T(8,128)(2,1)}, bf16[2048,32]{0,1:T(8,128)(2,1)}) async-done(((bf16[32,1536]{0,1:T(8,128)(2,1)}, bf16[32,2048]{1,0:T(8,128)(2,1)}, bf16[2048,32]{0,1:T(8,128)(2,1)}), (bf16[32,1536]{0,1:T(8,128)(2,1)}, bf16[32,2048]{1,0:T(8,128)(2,1)}, bf16[2048,32]{0,1:T(8,128)(2,1)})) %all-reduce.9.cloned.1.call-update) | async-done | bytes 360464 | tf_op jit(solution)/shard_map/psum | solution.py:503
  788.9 1.8 copy.69
  790.7 1.6 convert_element_type.177
  792.3 1.6 convert_element_type.179
  (147 shorter events, 16.4 us)
Async XLA Ops:
  7.2 48.7 %copy-start.22 = (s32[392]{0:T(512)S(1)}, s32[392]{0:T(512)}, u32[]{:S(2)}) copy-start(s32[392]{0:T(512)} %constant.76) | copy-start | bytes 4708
  7.2 103.6 %copy-start.33 = (s32[1568]{0:T(1024)S(1)}, s32[1568]{0:T(1024)}, u32[]{:S(2)}) copy-start(s32[1568]{0:T(1024)} %constant.59.clone) | copy-start | bytes 18820
  7.2 103.6 %copy-start.17 = (bf16[1,4,392,512]{3,2,1,0:T(8,128)(2,1)S(1)}, bf16[1,4,392,512]{3,2,1,0:T(8,128)(2,1)}, u32[]{:S(2)}) copy-start(bf16[1,4,392,512]{3,2,1,0:T(8,128)(2,1)} %param.41) | copy-start | bytes 4816900
  7.2 5.6 copy-start.30
  7.2 5.6 copy-start.29
  7.2 5.6 copy-start.28
  7.2 5.6 copy-start.27
  7.3 5.6 copy-start.26
  7.3 5.6 copy-start.25
  7.3 5.6 copy-start.24
  7.3 5.6 copy-start.23
  7.3 48.6 %copy-start.21 = (s32[4,392]{1,0:T(4,128)S(1)}, s32[4,392]{1,0:T(4,128)}, u32[]{:S(2)}) copy-start(s32[4,392]{1,0:T(4,128)} %param.40) | copy-start | bytes 18820
  7.3 53.1 %copy-start.19 = (bf16[2535,16]{0,1:T(8,128)(2,1)S(1)}, bf16[2535,16]{0,1:T(8,128)(2,1)}, u32[]{:S(2)}) copy-start(bf16[2535,16]{0,1:T(8,128)(2,1)} %param.30) | copy-start | bytes 243364
  7.3 61.1 %copy-start.20 = (bf16[512,32]{0,1:T(8,128)(2,1)S(1)}, bf16[512,32]{0,1:T(8,128)(2,1)}, u32[]{:S(2)}) copy-start(bf16[512,32]{0,1:T(8,128)(2,1)} %param.31) | copy-start | bytes 98308
  7.3 141.5 %all-gather.6.cloned.1.call-start = ((), (), s32[]{:S(2)}) async-start(), calls=%async_computation.4 | async-start | bytes 1671168 | tf_op jit(solution)/shard_map/all_gather | solution.py:421
  8.1 194.5 %all-gather.8.cloned.1.call-start = ((), (), s32[]{:S(2)}) async-start(), calls=%async_computation.5 | async-start | bytes 2228224 | tf_op jit(solution)/shard_map/all_gather | solution.py:421
  8.8 204.3 %all-gather.10.cloned.1.call-start = ((), (), s32[]{:S(2)}) async-start(), calls=%async_computation.6 | async-start | bytes 2228224 | tf_op jit(solution)/shard_map/all_gather | solution.py:421
  11.0 131.1 %collective-permute-start.2 = (bf16[1,4,200,512]{3,2,1,0:T(8,128)(2,1)}, bf16[1,4,200,512]{3,2,1,0:T(8,128)(2,1)}, u32[]{:S(2)}, u32[]{:S(2)}) collective-permute-start(bf16[1,4,200,512]{3,2,1,0:T(8,128)(2,1)} %slice.87), channel_id=1, source_target_pairs={{0,16},{16,0},{1,17},{17,1},{2,18},{18,2},{3,19},{19,3},{4,20},{20... | collective-permute-start | bytes 2457608 | tf_op jit(solution)/shard_map/ppermute | solution.py:370
  12.6 125.5 %collective-permute-start = (bf16[1,4,200,512]{3,2,1,0:T(8,128)(2,1)S(1)}, bf16[1,4,200,512]{3,2,1,0:T(8,128)(2,1)}, u32[]{:S(2)}, u32[]{:S(2)}) collective-permute-start(bf16[1,4,200,512]{3,2,1,0:T(8,128)(2,1)S(1)} %slice.73), channel_id=1, source_target_pairs={{0,16},{16,0},{1,17},{17,1},{2,18},{18,2},{3,19},{19,3},{4,20},{20... | collective-permute-start | bytes 2457608 | tf_op jit(solution)/shard_map/ppermute | solution.py:370
  12.8 389.1 %all-reduce.7.cloned.1.call-start = ((), (), s32[]{:S(2)}) async-start(), calls=%async_computation.7 | async-start | bytes 360448 | tf_op jit(solution)/shard_map/psum | solution.py:499
  115.6 19.3 %copy-start.18 = (bf16[1,4,392,512]{3,2,1,0:T(8,128)(2,1)S(1)}, bf16[1,4,392,512]{3,2,1,0:T(8,128)(2,1)}, u32[]{:S(2)}) copy-start(bf16[1,4,392,512]{3,2,1,0:T(8,128)(2,1)} %param.25) | copy-start | bytes 4816900
  135.0 3.1 copy-start.34
  154.2 1.9 copy-start.12
  154.3 2.6 copy-start.15
  161.6 33.2 %copy-start.7 = (bf16[512,512]{0,1:T(8,128)(2,1)S(1)}, bf16[512,512]{0,1:T(8,128)(2,1)}, u32[]{:S(2)}) copy-start(bf16[512,512]{0,1:T(8,128)(2,1)} %all_gather.21) | copy-start | bytes 1572868
  198.0 1.7 copy-start.2
  213.1 11.7 %copy-start.3 = (f32[4,392,512]{2,1,0:T(8,128)S(1)}, f32[4,392,512]{2,1,0:T(8,128)}, u32[]{:S(2)}) copy-start(f32[4,392,512]{2,1,0:T(8,128)} %copy-done.2) | copy-start | bytes 9633796
  213.1 11.7 %copy-start.31 = (bf16[512,2048]{1,0:T(8,128)(2,1)S(1)}, bf16[512,2048]{1,0:T(8,128)(2,1)}, u32[]{:S(2)}) copy-start(bf16[512,2048]{1,0:T(8,128)(2,1)} %all-gather.8.cloned.1.call-done) | copy-start | bytes 6291460
  224.8 4.8 copy-start.35
  224.8 4.8 copy-start.9
  229.6 3.0 copy-start.8
  231.0 1.6 copy-start
  282.0 250.6 %reduce-scatter.13.cloned.1.call-start = ((), (), s32[]{:S(2)}) async-start(), calls=%async_computation.11 | async-start | bytes 1671168
  282.2 3.2 copy-start.4
  282.2 3.2 copy-start.13
  285.4 1.4 copy-start.5
  291.9 322.5 %reduce-scatter.11.cloned.1.call-start = ((), (), s32[]{:S(2)}) async-start(), calls=%async_computation.10 | async-start | bytes 2228224 | tf_op jit(solution)/shard_map/reduce_scatter | solution.py:504
  300.6 394.0 %reduce-scatter.9.cloned.1.call-start = ((), (), s32[]{:S(2)}) async-start(), calls=%async_computation.9 | async-start | bytes 2228224 | tf_op jit(solution)/shard_map/reduce_scatter | solution.py:504
  309.0 3.1 copy-start.32
  312.1 97.3 %collective-permute-start.1 = (bf16[1,800,512]{2,1,0:T(8,128)(2,1)}, bf16[1,800,512]{2,1,0:T(8,128)(2,1)}, u32[]{:S(2)}, u32[]{:S(2)}) collective-permute-start(bf16[1,800,512]{2,1,0:T(8,128)(2,1)} %fusion.41), channel_id=1, source_target_pairs={{0,16},{16,0},{1,17},{17,1},{2,18},{18,2},{3,19},{19,3},{4,20},{20... | collective-permute-start | bytes 2457608 | tf_op jit(solution)/shard_map/ppermute | solution.py:370
  325.6 445.1 %reduce-scatter.7.cloned.1.call-start = ((), (), s32[]{:S(2)}) async-start(), calls=%async_computation.8 | async-start | bytes 557056 | tf_op jit(solution)/shard_map/reduce_scatter | solution.py:504
  325.9 3.2 copy-start.14
  325.9 3.2 copy-start.16
  329.1 1.4 copy-start.6
  337.8 3.1 copy-start.10
  337.8 41.3 %copy-start.1 = (f32[4,392,512]{2,1,0:T(8,128)S(1)}, f32[4,392,512]{2,1,0:T(8,128)}, u32[]{:S(2)}) copy-start(f32[4,392,512]{2,1,0:T(8,128)} %copy-done) | copy-start | bytes 9633796
  340.9 353.7 %collective-permute-start.3 = (bf16[1,800,512]{2,1,0:T(8,128)(2,1)}, bf16[1,800,512]{2,1,0:T(8,128)(2,1)}, u32[]{:S(2)}, u32[]{:S(2)}) collective-permute-start(bf16[1,800,512]{2,1,0:T(8,128)(2,1)} %fusion.40), channel_id=1, source_target_pairs={{0,16},{16,0},{1,17},{17,1},{2,18},{18,2},{3,19},{19,3},{4,20},{20... | collective-permute-start | bytes 2457608 | tf_op jit(solution)/shard_map/ppermute | solution.py:370
  382.8 5.1 copy-start.11
  391.6 397.3 %all-reduce.9.cloned.1.call-start = ((), (), s32[]{:S(2)}) async-start(), calls=%async_computation.12 | async-start | bytes 1310720 | tf_op jit(solution)/shard_map/psum | solution.py:503
Sparse Core Ops, SparseCore 0:
  10.9 61.8 all-gather.5
  75.6 59.8 all-gather.7
  138.3 59.4 all-gather.9
  282.1 119.7 all-reduce.6
  406.5 126.0 reduce-scatter.12
  534.7 79.5 reduce-scatter.10
  616.6 77.9 reduce-scatter.8
  696.9 73.8 reduce-scatter.6
  773.4 15.4 all-reduce.8

commit v2 on v1

v2 whole, which is shorter than its diff:
```python
import jax
import jax.numpy as jnp
import numpy as np
from jax import lax
from jax.experimental import pallas as pl
from jax.experimental.pallas import tpu as pltpu
from jax.sharding import PartitionSpec as P

HEADS = 16
HEAD_DIM = 32
WT = 8
WH = 7
WW = 7
WIN_TOK = WT * WH * WW
EPS = 1e-05

BF=jnp.bfloat16; F32=jnp.float32
LOG2E=1.4426950408889634; LN2=0.6931471805599453
SCALE=HEAD_DIM**-0.5
BIG=-(2.0**30)
GROUP=4
VM=56*1024*1024

def cost(micros):
    return pl.CostEstimate(flops=int(micros * 1e9), bytes_accessed=int(micros * 3.6e6), transcendentals=0)


def nt(a,b): return lax.dot_general(a,b,(((1,),(1,)),((),())),preferred_element_type=F32)
def nn(a,b): return jnp.dot(a,b,preferred_element_type=F32)

def placed(block, at, rows):
    parts=[]
    if at: parts.append(jnp.zeros((at,block.shape[1]),block.dtype))
    parts.append(block)
    if rows-at-block.shape[0]: parts.append(jnp.zeros((rows-at-block.shape[0],block.shape[1]),block.dtype))
    return jnp.concatenate(parts,axis=0)

def attend_kernel(q_ref,k_ref,v_ref,bias_ref,mq_ref,mk_ref,ctx_ref,ctx_tok_ref,e_ref,r_ref):
    parts=[]
    lhs=jnp.concatenate([k_ref[0],mk_ref[0]],axis=1)
    ones=jnp.ones((16,q_ref.shape[2]),BF)
    for h in range(GROUP):
        rows=slice(h*HEAD_DIM,(h+1)*HEAD_DIM)
        rhs=jnp.concatenate([placed(q_ref[0,rows,:],h*HEAD_DIM,GROUP*HEAD_DIM),placed(mq_ref[0],0,128)],axis=0)
        s=nn(lhs,rhs)+bias_ref[h]
        m=jnp.max(s,axis=0,keepdims=True)
        e=jnp.exp2(s-m).astype(BF)
        e_ref[0,h]=e
        c=nn(jnp.concatenate([v_ref[0,rows,:],ones],axis=0),e)
        r=1.0/c[HEAD_DIM:HEAD_DIM+1]
        c=c[:HEAD_DIM]*r
        parts.append(c)
        ctx_ref[0,rows,:]=c.astype(BF)
        r_ref[0,0,h:h+1,:]=r
    ctx_tok_ref[0]=jnp.transpose(jnp.concatenate(parts,axis=0)).astype(BF)

def attend(side,qT,k,vT,bias,mq,mk):
    nw,width,n=qT.shape
    ng=width//256
    first=side*ng
    wins=mk.shape[0]
    return pl.pallas_call(
        attend_kernel,
        grid=(ng,nw),
        in_specs=[
            pl.BlockSpec((1,128,n),lambda g,w:(w,first+g,0)),
            pl.BlockSpec((1,n,128),lambda g,w:(w,0,first+g)),
            pl.BlockSpec((1,128,n),lambda g,w:(w,first+g,0)),
            pl.BlockSpec((GROUP,n,n),lambda g,w:(g,0,0)),
            pl.BlockSpec((1,32,n),lambda g,w:(w%wins,0,0)),
            pl.BlockSpec((1,n,128),lambda g,w:(w%wins,0,0)),
        ],
        out_specs=[
            pl.BlockSpec((1,128,n),lambda g,w:(w,g,0)),
            pl.BlockSpec((1,n,128),lambda g,w:(w,0,g)),
            pl.BlockSpec((1,GROUP,n,n),lambda g,w:(w,g,0,0)),
            pl.BlockSpec((1,1,GROUP,n),lambda g,w:(w,g,0,0)),
        ],
        out_shape=[
            jax.ShapeDtypeStruct((nw,width//2,n),BF),
            jax.ShapeDtypeStruct((nw,n,width//2),BF),
            jax.ShapeDtypeStruct((nw,ng*GROUP,n,n),BF),
            jax.ShapeDtypeStruct((nw,ng,GROUP,n),F32),
        ],
        compiler_params=pltpu.CompilerParams(vmem_limit_bytes=VM),
        name="attend", cost_estimate=cost(17),
    )(qT,k,vT,bias,mq,mk)

SPREAD=768
FLAT=1408
WIDE=2816

def spread_ones():
    n=WT*WH*WW
    tok=np.arange(n); c=tok//(WW*WT); e=tok//WT%WW; a=tok%WT
    out=np.zeros((n,SPREAD),np.float32); out[tok,c*104+e*8+a]=1
    return out

def lane16(mirror):
    out=np.zeros((128,256),np.float32)
    for u in range(16):
        for a in range(8):
            out[u*8+a,u*16+(7-a if mirror else a)]=1
    return out

def back_kernel(e_ref,k_ref,v_ref,q_ref,g_ref,ctx_ref,r_ref,sp_ref,l16_ref,dq_ref,dk_ref,dv_ref,tab_ref,tot,acc):
    w=pl.program_id(0); nw=pl.num_programs(0)
    n=q_ref.shape[2]
    dv=jnp.zeros((n,128),F32); dk=jnp.zeros((n,128),F32); dq=[]
    @pl.when(w==0)
    def _():
        tot[...]=jnp.zeros_like(tot)
    for h in range(GROUP):
        rows=slice(h*HEAD_DIM,(h+1)*HEAD_DIM)
        go=g_ref[0,rows,:].astype(F32)*r_ref[0,0,h:h+1,:]
        inner=jnp.sum(go*ctx_ref[0,rows,:].astype(F32),axis=0,keepdims=True)
        rhs=placed(go.astype(BF),h*HEAD_DIM,128)
        e=e_ref[0,h]
        dp=nn(v_ref[0],rhs)
        ds=(e.astype(F32)*(dp-inner))
        dsl=ds.astype(BF)
        tot[h]+=ds
        dv+=nt(e,rhs)
        dk+=nt(dsl,placed(q_ref[0,rows,:],h*HEAD_DIM,128))
        dq.append(nn(k_ref[0,rows,:],dsl)*SCALE)
    dq_ref[0]=jnp.transpose(jnp.concatenate(dq,axis=0)).astype(BF)
    dv_ref[0]=dv.astype(BF)
    dk_ref[0]=(dk*LN2).astype(BF)
    @pl.when(w==nw-1)
    def _():
        for h in range(GROUP):
            x=nn(tot[h].astype(BF),sp_ref[...])
            full=jnp.zeros((8,FLAT),F32)
            for d in range(WH):
                part=jnp.zeros((8,SPREAD),F32)
                for f in range(WW):
                    j=(d*WW+f)*8
                    part=part+pltpu.roll(x[j:j+8,:],8*(WW-1-f),1) if f<WW-1 else part+x[j:j+8,:]
                wide=jnp.concatenate([part,jnp.zeros((8,FLAT-SPREAD),F32)],axis=1)
                full=full+(pltpu.roll(wide,104*(WH-1-d),1) if d<WH-1 else wide)
            acc[h*8:(h+1)*8,:]=full
        a=acc[...]
        hi=a.astype(BF); lo=(a-hi.astype(F32)).astype(BF)
        wide=[]
        for t in range(FLAT//128):
            c=slice(t*128,(t+1)*128)
            wide.append(nn(hi[:,c],l16_ref[...])+nn(lo[:,c],l16_ref[...]))
        y=jnp.concatenate(wide,axis=1)
        for h in range(GROUP):
            z=pltpu.roll(y[h*8:(h+1)*8,:],0,1,stride=1,stride_axis=0)
            tab_ref[0,h:h+1,:]=jnp.sum(z,axis=0,keepdims=True)

def attend_back(g,e,kT,v,qT,gT,ctxT,r,sp,l16):
    nw,width,n=qT.shape
    feat=pl.BlockSpec((1,128,n),lambda w:(w,g,0))
    tok=pl.BlockSpec((1,n,128),lambda w:(w,0,g))
    own=pl.BlockSpec((1,n,128),lambda w:(w,0,0))
    return pl.pallas_call(
        back_kernel,
        grid=(nw,),
        in_specs=[
            pl.BlockSpec((1,GROUP,n,n),lambda w:(w,g%2,0,0)),
            feat,tok,feat,feat,pl.BlockSpec((1,128,n),lambda w:(w,g%2,0)),
            pl.BlockSpec((1,1,GROUP,n),lambda w:(w,g%2,0,0)),
            pl.BlockSpec(sp.shape,lambda w:(0,0)),
            pl.BlockSpec(l16.shape,lambda w:(0,0)),
        ],
        out_specs=[own,own,own,pl.BlockSpec((1,GROUP,WIDE),lambda w:(0,0,0))],
        out_shape=[
            jax.ShapeDtypeStruct((nw,n,128),BF),
            jax.ShapeDtypeStruct((nw,n,128),BF),
            jax.ShapeDtypeStruct((nw,n,128),BF),
            jax.ShapeDtypeStruct((1,GROUP,WIDE),F32),
        ],
        scratch_shapes=[pltpu.VMEM((GROUP,n,n),F32),pltpu.VMEM((GROUP*8,FLAT),F32)],
        compiler_params=pltpu.CompilerParams(vmem_limit_bytes=VM),
        name="attend_back", cost_estimate=cost(12),
    )(e,kT,v,qT,gT,ctxT,r,sp,l16)

def lane_maps(mirror):
    lane=np.arange(WIDE); pq=lane//16; o=lane%16
    p=pq//13; q=pq%13
    ok=(pq<169)&(o<15)
    if mirror: o=14-o
    A=o>=7; b=np.where(A,14-o,7-o); C=p>=6; d=np.where(C,12-p,6-p); E=q>=6; f=np.where(E,12-q,6-q)
    col=(b*WH+d)*WW+f
    corner=A*4+C*2+E*1
    return np.where(ok,col,-1).astype(np.int32), np.where(ok,corner,-1).astype(np.int32)

CORNER_ROWS=[(a*WH+c)*WW+e for a in (0,WT-1) for c in (0,WH-1) for e in (0,WW-1)]

def prepare_kernel(rel_ref,maps_ref,table_ref,region_ref,order_ref,lab_ref,val_ref,mk_ref,mq_ref):
    n=rel_ref.shape[1]
    rel=jnp.concatenate([rel_ref[row:row+1,:] for row in CORNER_ROWS],axis=0)
    hi=(rel>>6).astype(F32).astype(BF); lo=(rel&63).astype(F32).astype(BF)
    both=jnp.concatenate([hi,lo],axis=0)
    corners=lax.broadcasted_iota(jnp.int32,(8,256),0)
    rows=lax.broadcasted_iota(jnp.int32,(n,256),0)
    trow=lax.broadcasted_iota(jnp.int32,(table_ref.shape[1],256),0)
    for t in range(WIDE//256):
        c=slice(t*256,(t+1)*256)
        for version in range(2):
            col=maps_ref[2*version:2*version+1,c]; cor=maps_ref[2*version+1:2*version+2,c]
            m=jnp.where(rows==col,1.0,0.0).astype(BF)
            y=nn(both,m)
            full=y[:8]*64.0+y[8:]
            lab=jnp.sum(jnp.where(corners==cor,full,0.0),axis=0,keepdims=True)
            lab=jnp.where(cor>=0,lab,-1.0).astype(jnp.int32)
            lab_ref[version:version+1,c]=lab
            if version==0:
                hot=jnp.where(trow==lab,1.0,0.0).astype(BF)
                val_ref[:,0,c]=nn(table_ref[...],hot)
    wins=region_ref.shape[0]
    region=jnp.concatenate([region_ref[...].astype(F32),jnp.zeros((16-wins,n),F32)],axis=0).astype(BF)
    across=nt(region,order_ref[...])
    down=nt(order_ref[...],region)
    lanes=lax.broadcasted_iota(jnp.int32,(n,128),1).astype(F32)
    subs=lax.broadcasted_iota(jnp.int32,(32,n),0).astype(F32)
    for w in range(wins):
        mk_ref[w]=jnp.where(down[:,w:w+1]==lanes,1.0,0.0).astype(BF)
        mq_ref[w]=jnp.where(across[w:w+1,:]==subs,0.0,BIG).astype(BF)

def prepare(rel_index,maps,table_t,region_ids,order):
    wins,n=region_ids.shape
    return pl.pallas_call(
        prepare_kernel,
        out_shape=[
            jax.ShapeDtypeStruct((2,WIDE),jnp.int32),
            jax.ShapeDtypeStruct((HEADS,1,WIDE),F32),
            jax.ShapeDtypeStruct((wins,n,128),BF),
            jax.ShapeDtypeStruct((wins,32,n),BF),
        ],
        compiler_params=pltpu.CompilerParams(vmem_limit_bytes=VM),
        name="prepare", cost_estimate=cost(6),
    )(rel_index,maps,table_t,region_ids,order)

def bias_kernel(val_ref,l8_ref,sp_ref,bias_ref,x_ref):
    base=jnp.broadcast_to(val_ref[0],(8,WIDE))
    z=pltpu.roll(base,WIDE-7,1,stride=1,stride_axis=0).astype(BF)
    narrow=jnp.concatenate([nn(z[:,t*256:(t+1)*256],l8_ref[...]) for t in range(FLAT//128)],axis=1)
    for d in range(WH):
        s=FLAT-104*(WH-1-d)
        wide=(pltpu.roll(narrow,s,1) if d<WH-1 else narrow)[:,:SPREAD]
        for f in range(WW):
            j=(d*WW+f)*8
            x_ref[j:j+8,:]=pltpu.roll(wide,SPREAD-8*(WW-1-f),1) if f<WW-1 else wide
    bias_ref[0]=nt(x_ref[...].astype(BF),sp_ref[...])*LOG2E

def bias_half(side,val,l8,sp):
    n=sp.shape[0]
    heads=HEADS//2
    return pl.pallas_call(
        bias_kernel,
        grid=(heads,),
        in_specs=[pl.BlockSpec((1,1,WIDE),lambda h:(side*heads+h,0,0)),pl.BlockSpec(l8.shape,lambda h:(0,0)),pl.BlockSpec(sp.shape,lambda h:(0,0))],
        out_specs=pl.BlockSpec((1,n,n),lambda h:(h,0,0)),
        out_shape=jax.ShapeDtypeStruct((heads,n,n),F32),
        scratch_shapes=[pltpu.VMEM((n,SPREAD),F32)],
        compiler_params=pltpu.CompilerParams(vmem_limit_bytes=VM),
        name="position_bias", cost_estimate=cost(10),
    )(val,l8,sp)

def spill_kernel(lab_ref,g_ref,out_ref):
    g=g_ref[...]
    hi=g.astype(BF); r1=g-hi.astype(F32); mid=r1.astype(BF); lo=(r1-mid.astype(F32)).astype(BF)
    three=jnp.concatenate([hi,mid,lo],axis=0)
    rows=out_ref.shape[1]
    trow=lax.broadcasted_iota(jnp.int32,(rows,256),0)
    tot=jnp.zeros((48,rows),F32)
    for t in range(WIDE//256):
        c=slice(t*256,(t+1)*256)
        hot=jnp.where(trow==lab_ref[1:2,c],1.0,0.0).astype(BF)
        tot=tot+nt(three[:,c],hot)
    out_ref[...]=tot[:16]+tot[16:32]+tot[32:]

def spill(lab,g,rows):
    return pl.pallas_call(
        spill_kernel,
        out_shape=jax.ShapeDtypeStruct((HEADS,rows),F32),
        compiler_params=pltpu.CompilerParams(vmem_limit_bytes=VM),
        name="table_rows", cost_estimate=cost(5),
    )(lab,g)


BLOCK = 32
B_FC1, B_PROJ, GAIN2, BIAS2, B_FC2, GAIN1, BIAS1, B_QV = range(8)
VEC_LANES = {B_FC1: (0, 128), GAIN1: (128, 32), BIAS1: (160, 32), B_QV: (192, 64), B_PROJ: (256, 32), GAIN2: (288, 32), BIAS2: (320, 32), B_FC2: (352, 32)}
VECTOR = 384


def load_weight(own_ref, other_ref, places_ref, held, sem, vecs=None):
    core = places_ref[64]
    lanes = slice(0, held.shape[2])
    copies = []
    for i in range(16):
        rows = pl.ds(i * BLOCK, BLOCK)
        own = own_ref.at[places_ref[i]]
        copies.append(pltpu.make_async_copy(own.at[:, lanes], held.at[core, rows, :], sem.at[2 * i]))
        copies.append(
            pltpu.make_async_copy(other_ref.at[places_ref[16 + i]].at[:, lanes], held.at[1 - core, rows, :], sem.at[2 * i + 1])
        )
        if vecs is not None:
            copies.append(pltpu.make_async_copy(own.at[0:16, held.shape[2] :], vecs.at[i], sem.at[32 + i]))
    for copy in copies:
        copy.start()
    for copy in copies:
        copy.wait()


def store_grad(total, places_ref, own_ref, send_ref):
    core = places_ref[64]

    def block(i, carry):
        own_ref[i, :, : total.shape[2]] = total[core, pl.ds(pl.multiple_of(places_ref[32 + i] * BLOCK, BLOCK), BLOCK), :].astype(BF)
        send_ref[i, :, : total.shape[2]] = total[1 - core, pl.ds(pl.multiple_of(places_ref[48 + i] * BLOCK, BLOCK), BLOCK), :].astype(BF)
        return carry

    lax.fori_loop(0, 16, block, 0)


def normalise(values):
    mean = jnp.mean(values, axis=-1, keepdims=True)
    centred = values - mean
    inverse = lax.rsqrt(jnp.mean(centred * centred, axis=-1, keepdims=True) + EPS)
    return centred * inverse, inverse


def project_kernel(
    places_ref, x_ref, own_ref, other_ref, q_ref, kt_ref, vt_ref, k_ref, v_ref, vec_ref, held, loose, sem
):
    @pl.when(pl.program_id(0) == 0)
    def _():
        load_weight(own_ref, other_ref, places_ref, held, sem, loose)
        rows = [loose[i].astype(F32) for i in range(16)]
        for name, (at, count) in VEC_LANES.items():
            parts = [row[at // 128 : at // 128 + 1, at % 128 : at % 128 + count] for row in rows]
            vec_ref[name : name + 1, : 16 * count] = jnp.concatenate(parts, axis=1)

    width = x_ref.shape[2]
    normed, _ = normalise(x_ref[0].astype(F32))
    first = (normed * vec_ref[GAIN1 : GAIN1 + 1, :width] + vec_ref[BIAS1 : BIAS1 + 1, :width]).astype(BF)
    left, right = nn(first, held[0]), nn(first, held[1])
    half = width // 2
    q = (left[:, :width] + vec_ref[B_QV : B_QV + 1, :width]) * (SCALE * LOG2E)
    k = jnp.concatenate([left[:, width:], right[:, :half]], axis=1)
    v = right[:, half:] + vec_ref[B_QV : B_QV + 1, width : 2 * width]
    q_ref[0] = jnp.transpose(q).astype(BF)
    kt_ref[0] = jnp.transpose(k).astype(BF)
    vt_ref[0] = jnp.transpose(v).astype(BF)
    k_ref[0] = k.astype(BF)
    v_ref[0] = v.astype(BF)


def project(places, x, own, other, hidden_width):
    nw, n, width = x.shape
    tok = pl.BlockSpec((1, n, width), lambda w, s: (w, 0, 0))
    feat = pl.BlockSpec((1, width, n), lambda w, s: (w, 0, 0))
    anywhere = pl.BlockSpec(memory_space=pl.ANY)
    vecs = (8, hidden_width)
    return pl.pallas_call(
        project_kernel,
        grid_spec=pltpu.PrefetchScalarGridSpec(
            num_scalar_prefetch=1,
            grid=(nw,),
            in_specs=[tok, anywhere, anywhere],
            out_specs=[feat, feat, feat, tok, tok, pl.BlockSpec(vecs, lambda w, s: (0, 0))],
            scratch_shapes=[
                pltpu.VMEM((2, 16 * BLOCK, own.shape[2] - 128), BF),
                pltpu.VMEM((16, 16, 128), BF),
                pltpu.SemaphoreType.DMA((48,)),
            ],
        ),
        out_shape=[jax.ShapeDtypeStruct((nw, width, n), BF)] * 3
        + [jax.ShapeDtypeStruct((nw, n, width), BF)] * 2
        + [jax.ShapeDtypeStruct(vecs, F32)],
        compiler_params=pltpu.CompilerParams(vmem_limit_bytes=VM),
        name="project", cost_estimate=cost(9),
    )(places, x, own, other)


TAIL = (0.254829592, -0.284496736, 1.421413741, -1.453152027, 1.061405429)


def normal_parts(values):
    t = pl.reciprocal(1.0 + (0.3275911 * 0.7071067811865476) * jnp.abs(values), approx=False)
    series = TAIL[4]
    for factor in TAIL[3::-1]:
        series = series * t + factor
    bell = jnp.exp2(values * values * (-0.5 * LOG2E))
    upper = (0.5 * t) * series * bell
    return jnp.where(values >= 0, 1.0 - upper, upper), bell * 0.3989422804014327


def column_sums(values):
    return jnp.sum(values, axis=0, keepdims=True)


def feed_kernel(
    places_ref, x_ref, ctx0_ref, ctx1_ref, og_ref, vec_ref, own_ref, other_ref, out_ref, mid_grad_ref, gt_ref, own_grad_ref,
    send_grad_ref, sums_ref, held, total, sem,
):
    step = pl.program_id(0)

    @pl.when(step == 0)
    def _():
        total[...] = jnp.zeros_like(total)
        sums_ref[...] = jnp.zeros_like(sums_ref)
        load_weight(own_ref, other_ref, places_ref, held, sem)

    width = x_ref.shape[2]
    half = width // 2
    chunk = (held.shape[2] - half) // 2
    vec = lambda row: vec_ref[row : row + 1, :width]
    ctx = (ctx0_ref[0], ctx1_ref[0])
    branch = nt(ctx[0], held[0, :, :half]) + nt(ctx[1], held[1, :, :half])
    mid = x_ref[0].astype(F32) + (branch + vec(B_PROJ))
    normed, inverse = normalise(mid)
    second = normed * vec(GAIN2) + vec(BIAS2)
    second_t = jnp.transpose(second).astype(BF)
    second = second.astype(BF)
    og = og_ref[0]
    og_t = jnp.transpose(og.astype(F32)).astype(BF)
    mlp = jnp.zeros(mid.shape, F32)
    second_grad = jnp.zeros(mid.shape, F32)
    for j in range(2):
        for part in range(2):
            piece = chunk // 2
            c1 = slice(half + part * piece, half + (part + 1) * piece)
            c2 = slice(half + chunk + part * piece, half + chunk + (part + 1) * piece)
            cols = slice(j * chunk + part * piece, j * chunk + (part + 1) * piece)
            fc1, fc2_t = held[j, :, c1], held[j, :, c2]
            hidden = nn(second, fc1) + vec_ref[B_FC1 : B_FC1 + 1, cols]
            act_grad = nn(og, fc2_t)
            phi_sum, density = normal_parts(hidden)
            act = (hidden * phi_sum).astype(BF)
            hidden_grad = act_grad * (phi_sum + hidden * density)
            sums_ref[0:1, cols] += column_sums(hidden_grad)
            hidden_grad = hidden_grad.astype(BF)
            mlp += nt(act, fc2_t)
            second_grad += nt(hidden_grad, fc1)
            total[j, :, c1] += nn(second_t, hidden_grad)
            total[j, :, c2] += nn(og_t, act)
    out_ref[0] = (mid + (mlp + vec(B_FC2))).astype(BF)
    scaled = second_grad * vec(GAIN2)
    inner = jnp.mean(scaled, axis=-1, keepdims=True)
    along = jnp.mean(scaled * normed, axis=-1, keepdims=True)
    og = og.astype(F32)
    mid_grad = og + inverse * (scaled - inner - normed * along)
    mid_grad_ref[0] = mid_grad
    low = mid_grad.astype(BF)
    sums_ref[1:2, :width] += column_sums(mid_grad)
    sums_ref[2:3, :width] += column_sums(second_grad * normed)
    sums_ref[3:4, :width] += column_sums(second_grad)
    sums_ref[4:5, :width] += column_sums(og)
    low_t = jnp.transpose(mid_grad).astype(BF)
    for j in range(2):
        total[j, :, :half] += nn(low_t, ctx[j])
        proj = jnp.transpose(held[j, :, :half].astype(F32)).astype(BF)
        gt_ref[0, j * half : (j + 1) * half, :] = nn(proj, low_t).astype(BF)

    @pl.when(step == pl.num_programs(0) - 1)
    def _():
        store_grad(total, places_ref, own_grad_ref, send_grad_ref)


def feed(places, x, ctx0, ctx1, og, vecs, own, other):
    nw, n, width = x.shape
    tok = pl.BlockSpec((1, n, width), lambda w, s: (w, 0, 0))
    feat = pl.BlockSpec((1, width, n), lambda w, s: (w, 0, 0))
    whole = pl.BlockSpec(own.shape, lambda w, s: (0, 0, 0))
    anywhere = pl.BlockSpec(memory_space=pl.ANY)
    side = pl.BlockSpec((1, n, width // 2), lambda w, s: (w, 0, 0))
    hidden_width = own.shape[2] - width // 2
    return pl.pallas_call(
        feed_kernel,
        grid_spec=pltpu.PrefetchScalarGridSpec(
            num_scalar_prefetch=1,
            grid=(nw,),
            in_specs=[tok, side, side, tok, pl.BlockSpec(vecs.shape, lambda w, s: (0, 0)), anywhere, anywhere],
            out_specs=[tok, tok, feat, whole, whole, pl.BlockSpec((8, hidden_width), lambda w, s: (0, 0))],
            scratch_shapes=[
                pltpu.VMEM((2, 16 * BLOCK, own.shape[2]), BF),
                pltpu.VMEM((2, 16 * BLOCK, own.shape[2]), F32),
                pltpu.SemaphoreType.DMA((32,)),
            ],
        ),
        out_shape=[
            jax.ShapeDtypeStruct((nw, n, width), BF),
            jax.ShapeDtypeStruct((nw, n, width), F32),
            jax.ShapeDtypeStruct((nw, width, n), BF),
            jax.ShapeDtypeStruct(own.shape, BF),
            jax.ShapeDtypeStruct(own.shape, BF),
            jax.ShapeDtypeStruct((8, hidden_width), F32),
        ],
        compiler_params=pltpu.CompilerParams(vmem_limit_bytes=VM),
        name="feed_forward", cost_estimate=cost(44),
    )(places, x, ctx0, ctx1, og, vecs, own, other)


def input_kernel(
    places_ref, x_ref, dq0, dk0, dv0, dq1, dk1, dv1, dq2, dk2, dv2, dq3, dk3, dv3, mid_grad_ref, vec_ref, fc_sums_ref,
    own_ref, other_ref, out_ref, own_grad_ref, send_grad_ref, held, total, sums, small, sem,
):
    step = pl.program_id(0)

    @pl.when(step == 0)
    def _():
        total[...] = jnp.zeros_like(total)
        sums[...] = jnp.zeros_like(sums)
        load_weight(own_ref, other_ref, places_ref, held, sem)

    width = x_ref.shape[2]
    half = width // 2
    vec = lambda row: vec_ref[row : row + 1, :width]
    normed, inverse = normalise(x_ref[0].astype(F32))
    first_t = jnp.transpose(normed * vec(GAIN1) + vec(BIAS1)).astype(BF)
    left = jnp.concatenate([dq0[0], dq1[0], dq2[0], dq3[0], dk0[0], dk1[0]], axis=1)
    right = jnp.concatenate([dk2[0], dk3[0], dv0[0], dv1[0], dv2[0], dv3[0]], axis=1)
    total[0] += nn(first_t, left)
    total[1] += nn(first_t, right)
    first_grad = (nt(left, held[0]) + nt(right, held[1])).astype(BF).astype(F32)
    scaled = first_grad * vec(GAIN1)
    inner = jnp.mean(scaled, axis=-1, keepdims=True)
    along = jnp.mean(scaled * normed, axis=-1, keepdims=True)
    out_ref[0] = (mid_grad_ref[0] + inverse * (scaled - inner - normed * along)).astype(BF)
    sums[0:1, :width] += column_sums(first_grad * normed)
    sums[1:2, :width] += column_sums(first_grad)
    sums[2:3, :width] += column_sums(left[:, :width].astype(F32))
    sums[2:3, width:] += column_sums(right[:, half:].astype(F32))

    @pl.when(step == pl.num_programs(0) - 1)
    def _():
        columns = total.shape[2]
        store_grad(total, places_ref, own_grad_ref, send_grad_ref)
        rows = {
            B_FC1: fc_sums_ref[0:1, :], B_PROJ: fc_sums_ref[1:2, :], GAIN2: fc_sums_ref[2:3, :], BIAS2: fc_sums_ref[3:4, :],
            B_FC2: fc_sums_ref[4:5, :], GAIN1: sums[0:1, :], BIAS1: sums[1:2, :], B_QV: sums[2:3, :],
        }
        for i in range(16):
            parts = [rows[name][:, i * count : (i + 1) * count] for name, (_, count) in VEC_LANES.items()]
            line = jnp.concatenate(parts, axis=1)
            small[i] = jnp.concatenate([line[:, :128], line[:, 128:256], line[:, 256:], jnp.zeros((BLOCK - 3, 128), F32)], axis=0)

        def block(i, carry):
            own_grad_ref[i, :, columns:] = small[places_ref[32 + i]].astype(BF)
            send_grad_ref[i, :, columns:] = small[places_ref[48 + i]].astype(BF)
            return carry

        lax.fori_loop(0, 16, block, 0)


def input_side(places, x, groups, mid_grad, vecs, fc_sums, own, other):
    nw, n, width = x.shape
    tok = pl.BlockSpec((1, n, width), lambda w, s: (w, 0, 0))
    part = pl.BlockSpec((1, n, 128), lambda w, s: (w, 0, 0))
    flat = lambda shape: pl.BlockSpec(shape, lambda w, s: (0,) * len(shape))
    anywhere = pl.BlockSpec(memory_space=pl.ANY)
    columns = own.shape[2] - 128
    grad = own.shape
    return pl.pallas_call(
        input_kernel,
        grid_spec=pltpu.PrefetchScalarGridSpec(
            num_scalar_prefetch=1,
            grid=(nw,),
            in_specs=[tok] + [part] * 12 + [tok, flat(vecs.shape), flat(fc_sums.shape), anywhere, anywhere],
            out_specs=[tok, flat(grad), flat(grad)],
            scratch_shapes=[
                pltpu.VMEM((2, 16 * BLOCK, columns), BF),
                pltpu.VMEM((2, 16 * BLOCK, columns), F32),
                pltpu.VMEM((8, 2 * width), F32),
                pltpu.VMEM((16, BLOCK, 128), F32),
                pltpu.SemaphoreType.DMA((32,)),
            ],
        ),
        out_shape=[
            jax.ShapeDtypeStruct((nw, n, width), BF),
            jax.ShapeDtypeStruct(grad, BF),
            jax.ShapeDtypeStruct(grad, BF),
        ],
        compiler_params=pltpu.CompilerParams(vmem_limit_bytes=VM),
        name="input_side", cost_estimate=cost(15),
    )(places, x, *[part for group in groups for part in group[:3]], mid_grad, vecs, fc_sums, own, other)


def from_partner(shard, axis, stride):
    return lax.ppermute(shard, axis, [(i, i ^ 1 << stride) for i in range(lax.axis_size(axis))])


def to_block(windows, local_count):
    clip_count, chans = (windows.shape[0], windows.shape[-1])
    parted = windows.reshape(
        clip_count, local_count[0], local_count[1], local_count[2], WT, WH, WW, chans
    )
    parted = parted.transpose(0, 1, 4, 2, 5, 3, 6, 7)
    return parted.reshape(
        clip_count, local_count[0] * WT, local_count[1] * WH, local_count[2] * WW, chans
    )


def from_block(block, local_count):
    clip_count, chans = (block.shape[0], block.shape[-1])
    parted = block.reshape(
        clip_count, local_count[0], WT, local_count[1], WH, local_count[2], WW, chans
    )
    parted = parted.transpose(0, 1, 3, 5, 2, 4, 6, 7)
    return parted.reshape(clip_count, -1, WT * WH * WW, chans)


def roll_ahead(windows, local_count, bit_list):
    block = to_block(windows, local_count)
    for grid_dim, amount, bit_pos in (
        (1, WT // 2, bit_list[0]),
        (2, WH // 2, bit_list[1]),
        (3, WW // 2, bit_list[2]),
    ):
        if bit_pos < 0:
            block = jnp.roll(block, -amount, axis=grid_dim)
        else:
            front = lax.slice_in_dim(block, 0, amount, axis=grid_dim)
            arrived = from_partner(front, "seq", bit_pos)
            rest = lax.slice_in_dim(block, amount, block.shape[grid_dim], axis=grid_dim)
            block = jnp.concatenate([rest, arrived], axis=grid_dim)
    return from_block(block, local_count)


def roll_behind(windows, local_count, bit_list):
    block = to_block(windows, local_count)
    for grid_dim, amount, bit_pos in (
        (1, WT // 2, bit_list[0]),
        (2, WH // 2, bit_list[1]),
        (3, WW // 2, bit_list[2]),
    ):
        if bit_pos < 0:
            block = jnp.roll(block, amount, axis=grid_dim)
        else:
            extent = block.shape[grid_dim]
            trailing = lax.slice_in_dim(block, extent - amount, extent, axis=grid_dim)
            arrived = from_partner(trailing, "seq", bit_pos)
            rest = lax.slice_in_dim(block, 0, extent - amount, axis=grid_dim)
            block = jnp.concatenate([arrived, rest], axis=grid_dim)
    return from_block(block, local_count)


KEEP = WT // 2 * WH * WW


def hwt_order():
    place = np.arange(WIN_TOK)
    return (place % WT * WH + place // (WW * WT)) * WW + place // WT % WW


def order_ones(shift):
    place = np.arange(WIN_TOK)
    out = np.zeros((WIN_TOK, WIN_TOK), np.float32)
    out[place, ((place + shift) % WT * WH + place // (WW * WT)) * WW + place // WT % WW] = 1
    return out


def tile_runs(win):
    runs = []
    for c in range(WH):
        h = (win // 2 * WH + c + WH // 2) % (2 * WH)
        for e, count in ((0, WW - WW // 2), (WW - WW // 2, WW // 2)):
            w = (win % 2 * WW + e + WW // 2) % (2 * WW)
            runs.append((h // WH * 2 + w // WW, h % WH * WW + w % WW, count))
    return runs


def swap_cores(part):
    return lax.ppermute(part, "seq", [(0, 1), (1, 0)])


def enter_kernel(own_ref, arrived_ref, order_ref, out_ref, held):
    _, n, width = own_ref.shape
    rows = lax.broadcasted_iota(jnp.int32, (n, width), 0)
    for source in range(4):
        values = jnp.where(rows >= KEEP, own_ref[source].astype(F32), arrived_ref[source].astype(F32)).astype(BF)
        held[source] = nn(order_ref[...], values)
    for win in range(4):
        parts = [held[source, 8 * at : 8 * (at + count), :] for source, at, count in tile_runs(win)]
        out_ref[win] = jnp.concatenate(parts, axis=0).astype(BF)


def leave_kernel(rows_ref, order_ref, out_ref, send_ref, held):
    for win in range(4):
        values = rows_ref[win].astype(F32)
        start = 0
        for source, at, count in tile_runs(win):
            held[source, 8 * at : 8 * (at + count), :] = values[8 * start : 8 * (start + count), :]
            start += count
    for source in range(4):
        values = nn(order_ref[...], held[source].astype(BF)).astype(out_ref.dtype)
        out_ref[source] = values
        send_ref[source] = values[: send_ref.shape[1]].astype(BF)


SENT = 208


def enter(windows, plan, arrived=None):
    clips, wins, toks, width = windows.shape
    if plan["levels"] == 1 and clips == 1:
        own = windows.reshape(wins, toks, width)
        return pl.pallas_call(
            enter_kernel,
            out_shape=jax.ShapeDtypeStruct(own.shape, BF),
            scratch_shapes=[pltpu.VMEM(own.shape, F32)],
            compiler_params=pltpu.CompilerParams(vmem_limit_bytes=VM),
            name="enter", cost_estimate=cost(4),
        )(own, arrived.reshape(own.shape), plan["order"])
    rolled = roll_ahead(windows, plan["local"], plan["bits"])
    rolled = rolled.reshape(clips * wins, WT, WH * WW, width).transpose(0, 2, 1, 3)
    return rolled.reshape(clips * wins, toks, width)


def leave(windows, plan, kind):
    wins, toks, width = windows.shape
    return pl.pallas_call(
        leave_kernel,
        out_shape=[jax.ShapeDtypeStruct(windows.shape, kind), jax.ShapeDtypeStruct((wins, SENT, width), BF)],
        scratch_shapes=[pltpu.VMEM(windows.shape, F32)],
        compiler_params=pltpu.CompilerParams(vmem_limit_bytes=VM),
        name="leave", cost_estimate=cost(4),
    )(windows, plan["order"].T)


def joined(kept, arrived):
    arrived = jnp.pad(arrived.astype(kept.dtype), ((0, 0), (0, kept.shape[1] - SENT), (0, 0)))
    rows = lax.broadcasted_iota(jnp.int32, kept.shape, 1)
    return jnp.where(rows < KEEP, arrived, kept)[None]


def leave_any(windows, plan, clips, kind):
    count, toks, width = windows.shape
    wins = count // clips
    if plan["levels"] == 1 and clips == 1:
        kept, sent = leave(windows, plan, kind)
        return joined(kept, swap_cores(sent))
    rows = windows.reshape(count, WH * WW, WT, width).transpose(0, 2, 1, 3)
    return roll_behind(rows.reshape(clips, wins, toks, width), plan["local"], plan["bits"]).astype(kind)


def pack_kernel(core_ref, qkv_ref, proj_ref, fc1_ref, fc2_ref, *rest):
    vec_refs, (qkv_out, fc_out) = rest[:-2], rest[-2:]

    def emit(side):
        half = qkv_ref.shape[1] // 2
        qkv_out[:, :half] = qkv_ref[:, side * half : (side + 1) * half]
        at = 0
        for ref in (proj_ref, fc1_ref, fc2_ref):
            half = ref.shape[1] // 2
            fc_out[:, at : at + half] = ref[:, side * half : (side + 1) * half]
            at += half

    half = qkv_ref.shape[1] // 2
    line = jnp.concatenate([ref[...].astype(F32).reshape(1, -1) for ref in vec_refs], axis=1)
    lines = [line[:, at : at + 128] for at in range(0, VECTOR, 128)]
    qkv_out[:, half:] = jnp.concatenate(lines + [jnp.zeros((BLOCK - len(lines), 128), F32)], axis=0).astype(BF)
    for side in range(2):
        @pl.when(core_ref[0] == side)
        def _():
            emit(side)


def pack(core, qkv, proj_t, fc1, fc2_t, vectors):
    columns = (proj_t.shape[1] + fc1.shape[1] + fc2_t.shape[1]) // 2
    vmem = pl.BlockSpec(memory_space=pltpu.VMEM)
    return pl.pallas_call(
        pack_kernel,
        in_specs=[pl.BlockSpec(memory_space=pltpu.SMEM)] + [vmem] * (4 + len(vectors)),
        out_shape=[
            jax.ShapeDtypeStruct((BLOCK, qkv.shape[1] // 2 + 128), BF),
            jax.ShapeDtypeStruct((BLOCK, columns), BF),
        ],
        compiler_params=pltpu.CompilerParams(vmem_limit_bytes=VM),
        name="pack", cost_estimate=cost(2),
    )(core, qkv, proj_t, fc1, fc2_t, *vectors)


def hop(part, flips):
    pairs = [(16 * c + s, 16 * c + (s ^ flips[c])) for c in range(2) for s in range(16)]
    return lax.ppermute(part, ("seq", "shard"), pairs)


def tree_places():
    me = lax.axis_index("shard")
    core = lax.axis_index("seq")
    entry = jnp.arange(16, dtype=jnp.int32)
    v, u, z = entry // 8, entry // 4 % 2, entry % 4
    straight, crossed = me ^ (4 * z + 2 * u + v), me ^ (4 * z + 2 * v + u)
    rel = me ^ entry
    z, y, x = rel // 4, rel // 2 % 2, rel % 2
    place_straight, place_crossed = x * 8 + y * 4 + z, y * 8 + x * 4 + z
    even = core == 0
    pick_core = lambda left, right: jnp.where(even, left, right)
    return jnp.concatenate(
        [
            pick_core(place_straight, place_crossed),
            pick_core(place_crossed, place_straight),
            pick_core(straight, crossed),
            pick_core(crossed, straight),
            jnp.broadcast_to(core, (1,)),
        ]
    ).astype(jnp.int32)


def tree_gather(part):
    arrived = yield [hop(part, (4 * k, 4 * k)) for k in range(1, 4)]
    stack = jnp.stack([part] + arrived)
    arrived = yield hop(stack, (2, 1))
    stack = jnp.concatenate([stack, arrived])
    arrived = yield hop(stack, (1, 2))
    stack = jnp.concatenate([stack, arrived])
    other = yield swap_cores(stack)
    yield stack, other


def tie(*items):
    return lax.optimization_barrier(items)


def add_low(left, right):
    return (left.astype(F32) + right.astype(F32)).astype(BF)


def tree_scatter(own, send):
    arrived = yield swap_cores(send)
    stack = add_low(own, arrived)
    arrived = yield hop(stack[8:], (1, 2))
    stack = add_low(stack[:8], arrived)
    arrived = yield hop(stack[4:], (2, 1))
    stack = add_low(stack[:4], arrived)
    arrived = yield [hop(stack[k], (4 * k, 4 * k)) for k in range(1, 4)]
    arrived = [part.astype(F32) for part in arrived]
    yield (stack[0].astype(F32) + arrived[0]) + (arrived[1] + arrived[2])


def finish(steps, pending):
    while True:
        try:
            pending = steps.send(pending)
        except StopIteration:
            return pending


def sides(part, core):
    other = swap_low(part)
    return [jnp.where(core == 0, part, other), jnp.where(core == 0, other, part)]


def swap_low(part):
    return swap_cores(part.astype(BF)).astype(F32)


def to_all(part):
    return lax.all_to_all(jnp.broadcast_to(part[None], (lax.axis_size("shard"),) + part.shape), "shard", 0, 0, tiled=True)


def body(
    tokens, norm1_gain, norm1_bias, qkv_weight, qv_bias, position_table, proj_weight, proj_bias, norm2_gain,
    norm2_bias, fc1_weight, fc1_bias, fc2_weight, fc2_bias, rel_index, region_ids, cotangent,
):
    levels = lax.axis_size("seq").bit_length() - 1
    clips, wins, toks, width = tokens.shape
    hidden_width = fc1_weight.shape[1]
    plan = {
        "levels": levels,
        "local": [1 if levels > level_pos else 2 for level_pos in range(3)],
        "bits": [levels - 1 - level_pos for level_pos in range(3)],
        "order": jnp.asarray(order_ones(WT // 2), BF),
    }
    vectors = [fc1_bias, norm1_gain, norm1_bias, qv_bias, proj_bias, norm2_gain, norm2_bias, fc2_bias]
    sizes = [part.shape[0] for part in vectors]
    spread = jnp.asarray(spread_ones(), BF)
    wide8 = jnp.asarray(lane16(False).T, BF)
    wide16 = jnp.asarray(lane16(True), BF)
    maps = jnp.asarray(np.stack(lane_maps(False) + lane_maps(True)))
    table = prepare(rel_index, maps, position_table.T, region_ids, jnp.asarray(order_ones(0), BF))
    if clips == 1 and lax.axis_size("shard") == 16 and lax.axis_size("seq") == 2:
        core = lax.axis_index("seq")
        places = tree_places()
        qkv_part, fc_part = pack(
            jnp.reshape(core, (1,)), qkv_weight, proj_weight.T, fc1_weight, fc2_weight.T, vectors
        )
        qkv_steps, fc_steps = tree_gather(qkv_part), tree_gather(fc_part)
        qkv_hop = next(qkv_steps)
        arrived = swap_cores(tokens)
        table, qkv_hop, arrived = tie(table, qkv_hop, arrived)
        labels, values, mask_keys, mask_queries = table
        qkv_hop = qkv_steps.send(qkv_hop)
        fc_hop = next(fc_steps)
        shifted = enter(tokens, plan, arrived)
        bias_low = bias_half(0, values, wide8, spread)
        qkv_hop, bias_low, shifted, values = tie(qkv_hop, bias_low, shifted, values)
        qkv_hop = qkv_steps.send(qkv_hop)
        arrived = swap_cores(cotangent)
        bias_high = bias_half(1, values, wide8, spread)
        out_grad = enter(cotangent, plan, arrived)
        qkv_hop, bias_high, out_grad, fc_hop = tie(qkv_hop, bias_high, out_grad, fc_hop)
        qkv_own, qkv_other = qkv_steps.send(qkv_steps.send(qkv_hop))
        fc_hop = fc_steps.send(fc_hop)
        q_t, k_t, v_t, token_k, token_v, vecs = project(places, shifted, qkv_own, qkv_other, hidden_width)
        q_t, fc_hop = tie(q_t, fc_hop)
        fc_hop = fc_steps.send(fc_hop)
        low = attend(0, q_t, token_k, v_t, bias_low, mask_queries, mask_keys)
        q_t, low, fc_hop = tie(q_t, low, fc_hop)
        fc_hop = fc_steps.send(fc_hop)
        high = attend(1, q_t, token_k, v_t, bias_high, mask_queries, mask_keys)
        high, fc_hop = tie(high, fc_hop)
        fc_own, fc_other = fc_steps.send(fc_hop)
        block_out, mid_grad, context_grad_t, fc_keep, fc_send, fc_sums = feed(
            places, shifted, low[1], high[1], out_grad, vecs, fc_own, fc_other
        )
        fc_steps = tree_scatter(fc_keep, fc_send)
        fc_hop = next(fc_steps)
        kept, sent = leave(block_out, plan, BF)
        block_out = joined(kept, swap_cores(sent))
        groups = []
        for g in range(width // 128):
            context_t, _, expo, inverse_sum = low if g < 2 else high
            groups.append(
                attend_back(g, expo, k_t, token_v, q_t, context_grad_t, context_t, inverse_sum, spread, wide16)
            )
            if g != 1:
                groups[-1], fc_hop, context_grad_t = tie(groups[-1], fc_hop, context_grad_t)
                fc_hop = fc_steps.send(fc_hop)
            else:
                groups[-1], context_grad_t = tie(groups[-1], context_grad_t)
        input_grad, qkv_keep, qkv_send = input_side(
            places, shifted, groups, mid_grad, vecs, fc_sums, qkv_own, qkv_other
        )
        qkv_steps = tree_scatter(qkv_keep, qkv_send)
        qkv_hop = next(qkv_steps)
        offsets = jnp.concatenate([group[3] for group in groups]).reshape(HEADS, WIDE)
        input_grad, offsets = tie(input_grad, offsets)
        offsets = jnp.sum(lax.all_to_all(offsets, "shard", 0, 0, tiled=True), axis=0)
        qkv_hop, offsets, fc_hop = tie(qkv_hop, offsets, fc_hop)
        qkv_hop = qkv_steps.send(qkv_hop)
        offsets = offsets + swap_cores(offsets)
        own_fc = finish(fc_steps, fc_hop)
        kept, sent = leave(input_grad, plan, F32)
        offsets = to_all(offsets)
        qkv_hop, offsets, kept, sent = tie(qkv_hop, offsets, kept, sent)
        qkv_hop = qkv_steps.send(qkv_hop)
        arrived = swap_cores(sent)
        table_grad = spill(labels, offsets, position_table.shape[0])
        qkv_hop, table_grad, arrived = tie(qkv_hop, table_grad, arrived)
        qkv_hop = qkv_steps.send(qkv_hop)
        input_grad = joined(kept, arrived)
        own_qkv = finish(qkv_steps, qkv_hop)
        small = own_qkv[: VECTOR // 128, width * 3 // 2 :].reshape(-1)
        own_fc, own_qkv = sides(own_fc, core), sides(own_qkv[:, : width * 3 // 2], core)
    else:
        straight = np.arange(16)
        places = jnp.asarray(np.concatenate([straight, straight, straight, straight, np.zeros(1)]), jnp.int32)
        gather = lambda part: lax.all_gather(part, "shard", axis=0, tiled=True)
        halves = lambda part: jnp.split(part, 2, axis=1)
        parts = [halves(gather(part)) for part in (proj_weight.T, fc1_weight, fc2_weight.T)]
        fc_own, fc_other = (jnp.concatenate(pair, axis=1).reshape(16, BLOCK, -1) for pair in zip(*parts))
        rows = lax.all_gather(jnp.concatenate(vectors), "shard", axis=0, tiled=False)
        pieces = [piece.reshape(16, -1) for piece in jnp.split(rows, np.cumsum(sizes)[:-1], axis=1)]
        rows = jnp.pad(jnp.concatenate(pieces, axis=1).reshape(16, -1, 128), ((0, 0), (0, BLOCK - VECTOR // 128), (0, 0)))
        qkv_own, qkv_other = (
            jnp.concatenate([part.reshape(16, BLOCK, -1), rows], axis=2) for part in halves(gather(qkv_weight))
        )
        shifted = enter(tokens, plan, swap_cores(tokens) if levels == 1 else None)
        out_grad = enter(cotangent, plan, swap_cores(cotangent) if levels == 1 else None)
        labels, values, mask_keys, mask_queries = table
        bias_low, bias_high = (bias_half(side, values, wide8, spread) for side in range(2))
        q_t, k_t, v_t, token_k, token_v, vecs = project(places, shifted, qkv_own, qkv_other, hidden_width)
        low = attend(0, q_t, token_k, v_t, bias_low, mask_queries, mask_keys)
        high = attend(1, q_t, token_k, v_t, bias_high, mask_queries, mask_keys)
        block_out, mid_grad, context_grad_t, fc_keep, fc_send, fc_sums = feed(
            places, shifted, low[1], high[1], out_grad, vecs, fc_own, fc_other
        )
        groups = []
        for g in range(width // 128):
            context_t, _, expo, inverse_sum = low if g < 2 else high
            groups.append(
                attend_back(g, expo, k_t, token_v, q_t, context_grad_t, context_t, inverse_sum, spread, wide16)
            )
        input_grad, qkv_keep, qkv_send = input_side(
            places, shifted, groups, mid_grad, vecs, fc_sums, qkv_own, qkv_other
        )
        block_out = leave_any(block_out, plan, clips, BF)
        input_grad = leave_any(input_grad, plan, clips, F32)
        offsets = jnp.concatenate([group[3] for group in groups]).reshape(HEADS, WIDE)
        table_grad = spill(labels, lax.psum(offsets, ("seq", "shard")), position_table.shape[0])
        small = qkv_keep[:, : VECTOR // 128, width * 3 // 2 :].reshape(16, VECTOR)
        small = lax.psum(small.astype(F32), ("seq", "shard"))
        pieces = jnp.split(small, np.cumsum([count for _, count in VEC_LANES.values()])[:-1], axis=1)
        shards = lax.axis_size("shard")
        small = jnp.concatenate([piece.reshape(shards, -1) for piece in pieces], axis=1)
        small = lax.dynamic_index_in_dim(small, lax.axis_index("shard"), 0, keepdims=False)

        def owned(grad):
            grad = lax.psum(grad.reshape(16 * BLOCK, -1), "seq")
            return lax.psum_scatter(grad, "shard", scatter_dimension=0, tiled=True).astype(F32)

        own_fc = [owned(fc_keep), owned(fc_send)]
        own_qkv = [owned(qkv_keep[:, :, : width * 3 // 2]), owned(qkv_send[:, :, : width * 3 // 2])]
    own_proj, own_fc1, own_fc2 = (
        jnp.concatenate(pair, axis=1)
        for pair in zip(*(jnp.split(part, (width // 2, (width + hidden_width) // 2), axis=1) for part in own_fc))
    )
    own_qkv = jnp.concatenate(own_qkv, axis=1)
    own_f1b, own_g1, own_b1, own_qv, own_pb, own_g2, own_b2, own_f2b = jnp.split(small, np.cumsum(sizes)[:-1])
    return (
        block_out, input_grad, own_g1, own_b1, own_qkv, own_qv, table_grad.T, own_proj.T, own_pb,
        own_g2, own_b2, own_fc1, own_f1b, own_fc2.T, own_f2b,
    )


def solution(mesh):
    return jax.shard_map(
        body,
        mesh=mesh,
        in_specs=(
            P("shard", "seq", None, None),
            P("shard"),
            P("shard"),
            P("shard", None),
            P("shard"),
            P(),
            P(None, "shard"),
            P("shard"),
            P("shard"),
            P("shard"),
            P("shard", None),
            P("shard"),
            P(None, "shard"),
            P("shard"),
            P(),
            P("seq", None),
            P("shard", "seq", None, None),
        ),
        out_specs=(
            P("shard", "seq", None, None),
            P("shard", "seq", None, None),
            P("shard"),
            P("shard"),
            P("shard", None),
            P("shard"),
            P(),
            P(None, "shard"),
            P("shard"),
            P("shard"),
            P("shard"),
            P("shard", None),
            P("shard"),
            P(None, "shard"),
            P("shard"),
        ),
        check_vma=False,
    )
```

time: 806 us -> 296 us (0.37)
  waiting for transfers between devices: 377 us -> 17.7 us
  blocking collectives: 127 us -> 0 us
  matrix products: 116 us -> 0 us
  Pallas kernels: 105 us -> 209 us
  starting transfers between devices: 2.29 us -> 42 us
  local copies, waits for them, and re-layouts: 32.3 us -> 9.66 us
  other arithmetic: 26.9 us -> 10 us
  between operations: 14.7 us -> 1.47 us
    reduce_scatter x3 -> x0, waiting for transfers between devices: 233 us -> none  [owned(): lax.psum_scatter(total, 'shard', scatter_dimension=axis, tiled=True)]
    unnamed x10 -> x0, waiting for transfers between devices: 122 us -> none
    dot_general x26 -> x0, matrix products: 116 us -> none  [the longest x4 14.9 us: nt_first(): lax.dot_general(hot, rows, (((0,), (0,)), ((), ())), preferred_element_ty...]
    pallas_call x4 -> x16, Pallas kernels: 71.5 us -> 172 us  [the longest x4 50.9 us: attend_back(): pl.pallas_call(back_kernel, grid=(nw,), in_specs=[pl.BlockSpec((1, GROUP,...]
    all_gather x2 -> x0, blocking collectives: 85.1 us -> none  [the longest x1 42.7 us: body(): vectors = lax.all_gather(vectors, 'shard', axis=0, tiled=False).astype(F32)]
    psum x2 -> x0, blocking collectives: 41.6 us -> none  [the longest x1 37.5 us: body(): small = lax.psum(small, ('seq', 'shard'))]
    ppermute x0 -> x20, starting transfers between devices: none -> 28.3 us  [hop(): return lax.ppermute(part, ('seq', 'shard'), pairs)]
    psum x2 -> x0, waiting for transfers between devices: 21.8 us -> none  [the longest x1 13.5 us: owned(): total = lax.psum(grad.astype(BF), 'seq')]
  transfers between devices with their start and end apart: 13 -> 33, of which waited for: 6 -> 5; matrix products, arithmetic and copies ran while one was open for 17% -> 5% of each run, Pallas kernels for 8% -> 51%
where the time goes in v2:
time: 296 us; the launch traced here: 290 us
  Pallas kernels  209 us (71%)
  starting transfers between devices  42 us (14%)
  waiting for transfers between devices  17.7 us (6%)
  other arithmetic  10 us (3%)
  local copies, waits for them, and re-layouts  9.66 us (3%)
    pallas_call x4, Pallas kernels, attend_back(): pl.pallas_call(back_kernel, grid=(nw,), in_specs=[pl.BlockSpec((1, GROUP,...  50.9 us
    pallas_call x1, Pallas kernels, feed(): pl.pallas_call(feed_kernel, grid_spec=pltpu.PrefetchScalarGridSpec(num_sc...  44.4 us
    pallas_call x2, Pallas kernels, attend(): pl.pallas_call(attend_kernel, grid=(ng, nw), in_specs=[pl.BlockSpec((1, 1...  36.8 us
    ppermute x20, starting transfers between devices, hop(): return lax.ppermute(part, ('seq', 'shard'), pairs)  28.3 us
    pallas_call x2, Pallas kernels, bias_half(): pl.pallas_call(bias_kernel, grid=(heads,), in_specs=[pl.BlockSpec((1, 1,...  21.5 us
    pallas_call x1, Pallas kernels, input_side(): pl.pallas_call(input_kernel, grid_spec=pltpu.PrefetchScalarGridSpec(num_s...  15.8 us
    pallas_call x1, Pallas kernels, project(): pl.pallas_call(project_kernel, grid_spec=pltpu.PrefetchScalarGridSpec(num...  9.38 us
    pallas_call x2, Pallas kernels, leave(): pl.pallas_call(leave_kernel, out_shape=[jax.ShapeDtypeStruct(windows.shap...  8.37 us
  transfers between devices with their start and end apart: 33, of which 5 were waited for; matrix products, arithmetic and copies ran while one was open for 5% of the time, Pallas kernels for 51%

profile of v2, /device:TPU:0, one launch (start us, length us, event | category | flops | bytes accessed | tf_op | source)
XLA Modules:
  0.0 289.7 jit_solution(16050542777630235995)
XLA Ops:
  0.7 1.9 pack.1
  2.5 3.0 %collective-permute-start = (bf16[32,896]{1,0:T(8,128)(2,1)}, bf16[32,896]{1,0:T(8,128)(2,1)S(1)}, u32[]{:S(2)}, u32[]{:S(2)}) collective-permute-start(bf16[32,896]{1,0:T(8,128)(2,1)} %get-tuple-element.131), channel_id=1, source_target_pairs={{0,4},{1,5},{2,6},{3,7},{4,0},{5,1},{6,2},{7,3},{8,12},{9,13},{10,... | collective-permute-start | bytes 172040 | tf_op jit(solution)/shard_map/ppermute | solution.py:782
  5.5 2.6 collective-permute-start.1
  8.1 0.5 collective-permute-start.6
  8.6 0.8 constant_dynamic-update-slice_fusion.4
  9.5 5.9 %prepare.1 = (s32[2,2816]{1,0:T(2,128)}, f32[16,1,2816]{2,1,0:T(1,128)}, bf16[4,392,128]{2,1,0:T(8,128)(2,1)}, bf16[4,32,392]{2,1,0:T(8,128)(2,1)}) custom-call(s32[392,392]{1,0:T(8,128)} %rel_ref.1, s32[4,2816]{1,0:T(4,128)} %constant.115.clone.maps_ref, bf16[16,2535]{1,0:T(8,128)(2,1)} %bitcast.86, s32[4,392]{1,0:T(4,128)} %region_ref.1, ...), custom_call_target="tpu_custom_call" | custom-call | flops 6000000000 | bytes 21600000 | tf_op jit(solution)/shard_map/prepare/pallas_call | solution.py:225
  15.5 0.7 constant_dynamic-update-slice_fusion.21
  16.2 0.6 concatenate.34.places_ref
  16.8 0.9 collective-permute-start.7
  17.7 3.5 %collective-permute-start.8 = (bf16[32,2304]{1,0:T(8,128)(2,1)S(1)}, bf16[32,2304]{1,0:T(8,128)(2,1)S(1)}, u32[]{:S(2)}, u32[]{:S(2)}) collective-permute-start(bf16[32,2304]{1,0:T(8,128)(2,1)S(1)} %copy-done.4), channel_id=1, source_target_pairs={{0,8},{1,9},{2,10},{3,11},{4,12},{5,13},{6,14},{7,15},{8,0},{9,1},... | collective-permute-start | bytes 442376 | tf_op jit(solution)/shard_map/ppermute | solution.py:782
  21.2 1.8 collective-permute-start.4
  23.0 4.1 %enter.2.x_ref = bf16[4,392,512]{2,1,0:T(8,128)(2,1)} custom-call(bf16[4,392,512]{2,1,0:T(8,128)(2,1)} %bitcast.8.own_ref, bf16[4,392,512]{2,1,0:T(8,128)(2,1)} %bitcast.9.arrived_ref, bf16[392,392]{1,0:T(8,128)(2,1)} %constant.111.clone.order_ref), custom_call_target="tpu_custom_call" | custom-call | flops 4000000000 | bytes 14400000 | tf_op jit(solution)/shard_map/enter/pallas_call | solution.py:704
  27.2 4.1 %enter.3.og_ref = bf16[4,392,512]{2,1,0:T(8,128)(2,1)} custom-call(bf16[4,392,512]{2,1,0:T(8,128)(2,1)} %bitcast.10.own_ref, bf16[4,392,512]{2,1,0:T(8,128)(2,1)} %bitcast.11.arrived_ref, bf16[392,392]{1,0:T(8,128)(2,1)} %constant.111.clone.order_ref), custom_call_target="tpu_custom_call" | custom-call | flops 4000000000 | bytes 14400000 | tf_op jit(solution)/shard_map/enter/pallas_call | solution.py:704
  31.3 10.8 %position_bias.2.bias_ref = f32[8,392,392]{2,1,0:T(8,128)} custom-call(f32[16,1,2816]{2,1,0:T(1,128)} %get-tuple-element.143.val_ref, bf16[256,128]{1,0:T(8,128)(2,1)} %constant.113.clone.l8_ref, bf16[392,768]{1,0:T(8,128)(2,1)} %constant.112.clone.sp_ref), custom_call_target="tpu_custom_call" | custom-call | flops 10000000000 | bytes 36000000 | tf_op jit(solution)/shard_map/position_bias/pallas_call | solution.py:252
  42.2 1.6 collective-permute-start.5
  43.8 10.7 %position_bias.3.bias_ref = f32[8,392,392]{2,1,0:T(8,128)} custom-call(f32[16,1,2816]{2,1,0:T(1,128)} %get-tuple-element.143.val_ref, bf16[256,128]{1,0:T(8,128)(2,1)} %constant.113.clone.l8_ref, bf16[392,768]{1,0:T(8,128)(2,1)} %constant.112.clone.sp_ref), custom_call_target="tpu_custom_call" | custom-call | flops 10000000000 | bytes 36000000 | tf_op jit(solution)/shard_map/position_bias/pallas_call | solution.py:252
  54.6 0.6 collective-permute-start.11
  55.4 2.5 collective-permute-done.10.other_ref
  57.9 9.4 %project.1 = (bf16[4,512,392]{2,1,0:T(8,128)(2,1)}, bf16[4,512,392]{2,1,0:T(8,128)(2,1)}, bf16[4,512,392]{2,1,0:T(8,128)(2,1)}, bf16[4,392,512]{2,1,0:T(8,128)(2...) custom-call(s32[65]{0:T(128)} %concatenate.34.places_ref, bf16[4,392,512]{2,1,0:T(8,128)(2,1)} %enter.2.x_ref, ...), custom_call_target="tpu_custom_call" | custom-call | flops 8999999488 | bytes 32400000 | tf_op jit(solution)/shard_map/project/pallas_call | solution.py:360
  67.8 18.4 %attend.2 = (bf16[4,256,392]{2,1,0:T(8,128)(2,1)}, bf16[4,392,256]{2,1,0:T(8,128)(2,1)}, bf16[4,8,392,392]{3,2,1,0:T(8,128)(2,1)}, f32[4,2,4,392]{3,2,1,0:T(4,128)}) custom-call(bf16[4,512,392]{2,1,0:T(8,128)(2,1)} %get-tuple-element.162.q_ref, bf16[4,392,512]{2,1,0:T(8,128)(2,1)} %get-tuple-element.151.k_ref, ...), custom_call_target="tpu_custom_call" | custom-call | flops 16999999488 | bytes 61200000 | tf_op jit(solution)/shard_map/attend/pallas_call | solution.py:62
  86.3 1.1 collective-permute-start.13
  87.4 18.4 %attend.3 = (bf16[4,256,392]{2,1,0:T(8,128)(2,1)}, bf16[4,392,256]{2,1,0:T(8,128)(2,1)}, bf16[4,8,392,392]{3,2,1,0:T(8,128)(2,1)}, f32[4,2,4,392]{3,2,1,0:T(4,128)}) custom-call(bf16[4,512,392]{2,1,0:T(8,128)(2,1)} %get-tuple-element.162.q_ref, bf16[4,392,512]{2,1,0:T(8,128)(2,1)} %get-tuple-element.151.k_ref, ...), custom_call_target="tpu_custom_call" | custom-call | flops 16999999488 | bytes 61200000 | tf_op jit(solution)/shard_map/attend/pallas_call | solution.py:62
  105.8 1.5 copy-done.15
  107.3 44.4 %feed_forward.1 = (bf16[4,392,512]{2,1,0:T(8,128)(2,1)}, f32[4,392,512]{2,1,0:T(8,128)}, bf16[4,512,392]{2,1,0:T(8,128)(2,1)}, bf16[16,32,2304]{2,1,0:T(8,128)(2...) custom-call(s32[65]{0:T(128)} %concatenate.34.places_ref, bf16[4,392,512]{2,1,0:T(8,128)(2,1)} %enter.2.x_ref, ...), custom_call_target="tpu_custom_call" | custom-call | flops 44000002048 | bytes 158400000 | tf_op jit(solution)/shard_map/feed_forward/pallas_call | solution.py:474
  151.7 0.8 collective-permute-start.15
  152.6 3.9 %leave.2 = (bf16[4,392,512]{2,1,0:T(8,128)(2,1)}, bf16[4,208,512]{2,1,0:T(8,128)(2,1)}) custom-call(bf16[4,392,512]{2,1,0:T(8,128)(2,1)} %get-tuple-element.173.rows_ref, bf16[392,392]{1,0:T(8,128)(2,1)} %constant.123.order_ref), custom_call_target="tpu_custom_call" | custom-call | flops 4000000000 | bytes 14400000 | tf_op jit(solution)/shard_map/leave/pallas_call | solution.py:718
  156.5 13.0 %attend_back.4 = (bf16[4,392,128]{2,1,0:T(8,128)(2,1)}, bf16[4,392,128]{2,1,0:T(8,128)(2,1)}, bf16[4,392,128]{2,1,0:T(8,128)(2,1)}, f32[1,4,2816]{2,1,0:T(4,128)}) custom-call(bf16[4,8,392,392]{3,2,1,0:T(8,128)(2,1)} %get-tuple-element.176.e_ref, bf16[4,512,392]{2,1,0:T(8,128)(2,1)} %get-tuple-element.177.k_ref, ...), custom_call_target="tpu_custom_call" | custom-call | flops 12000000000 | bytes 43200000 | tf_op jit(solution)/shard_map/attend_back/pallas_call | solution.py:158
  169.5 1.6 select_bitcast_fusion.1
  171.1 0.7 copy-done.1
  171.8 0.6 add_convert_fusion
  172.5 1.2 collective-permute-start.16
  173.6 12.6 %attend_back.5 = (bf16[4,392,128]{2,1,0:T(8,128)(2,1)}, bf16[4,392,128]{2,1,0:T(8,128)(2,1)}, bf16[4,392,128]{2,1,0:T(8,128)(2,1)}, f32[1,4,2816]{2,1,0:T(4,128)}) custom-call(bf16[4,8,392,392]{3,2,1,0:T(8,128)(2,1)} %get-tuple-element.176.e_ref, bf16[4,512,392]{2,1,0:T(8,128)(2,1)} %get-tuple-element.177.k_ref, ...), custom_call_target="tpu_custom_call" | custom-call | flops 12000000000 | bytes 43200000 | tf_op jit(solution)/shard_map/attend_back/pallas_call | solution.py:158
  186.2 12.7 %attend_back.6 = (bf16[4,392,128]{2,1,0:T(8,128)(2,1)}, bf16[4,392,128]{2,1,0:T(8,128)(2,1)}, bf16[4,392,128]{2,1,0:T(8,128)(2,1)}, f32[1,4,2816]{2,1,0:T(4,128)}) custom-call(bf16[4,8,392,392]{3,2,1,0:T(8,128)(2,1)} %get-tuple-element.198.e_ref, bf16[4,512,392]{2,1,0:T(8,128)(2,1)} %get-tuple-element.177.k_ref, ...), custom_call_target="tpu_custom_call" | custom-call | flops 12000000000 | bytes 43200000 | tf_op jit(solution)/shard_map/attend_back/pallas_call | solution.py:158
  199.3 1.6 collective-permute-start.17
  200.9 12.6 %attend_back.7 = (bf16[4,392,128]{2,1,0:T(8,128)(2,1)}, bf16[4,392,128]{2,1,0:T(8,128)(2,1)}, bf16[4,392,128]{2,1,0:T(8,128)(2,1)}, f32[1,4,2816]{2,1,0:T(4,128)}) custom-call(bf16[4,8,392,392]{3,2,1,0:T(8,128)(2,1)} %get-tuple-element.198.e_ref, bf16[4,512,392]{2,1,0:T(8,128)(2,1)} %get-tuple-element.177.k_ref, ...), custom_call_target="tpu_custom_call" | custom-call | flops 12000000000 | bytes 43200000 | tf_op jit(solution)/shard_map/attend_back/pallas_call | solution.py:158
  213.6 15.8 %input_side.1 = (bf16[4,392,512]{2,1,0:T(8,128)(2,1)}, bf16[16,32,896]{2,1,0:T(8,128)(2,1)}, bf16[16,32,896]{2,1,0:T(8,128)(2,1)}) custom-call(s32[65]{0:T(128)} %concatenate.34.places_ref, bf16[4,392,512]{2,1,0:T(8,128)(2,1)} %enter.2.x_ref, bf16[4,392,128]{2,1,0:T(8,128)(2,1)} %get-tuple-element.187.dq0, bf16[4,392,128]{2,1,0:T(8,128)(2,1)} %get-tuple-element.188.dk0, ...), custom_call_target="tpu_custom_call" | custom-call | flops 15000000512 | bytes 54000000 | tf_op jit(solution)/shard_map/input_side/pallas_call | solution.py:560
  229.5 0.7 slice_bitcast_fusion.1
  230.6 3.8 %collective-permute-start.20 = (bf16[32,2304]{1,0:T(8,128)(2,1)}, bf16[32,2304]{1,0:T(8,128)(2,1)S(1)}, u32[]{:S(2)}, u32[]{:S(2)}) collective-permute-start(bf16[32,2304]{1,0:T(8,128)(2,1)} %get-tuple-element.250), channel_id=1, source_target_pairs={{0,8},{1,9},{2,10},{3,11},{4,12},{5,13},{6,14},{7,15},{8,0},{9,1},... | collective-permute-start | bytes 442376 | tf_op jit(solution)/shard_map/ppermute | solution.py:782
  234.8 0.8 all_to_all.12
  235.6 5.5 %all-to-all-start = ((f32[16,1,2816]{2,1,0:T(1,128)}), f32[16,1,2816]{2,1,0:T(1,128)S(1)}, u32[]{:S(2)}, u32[]{:S(2)}) async-start(f32[16,1,2816]{2,1,0:T(1,128)} %all_to_all.12), calls=%async_computation | async-start | bytes 360448 | tf_op jit(solution)/shard_map/all_to_all | solution.py:936
  241.1 4.5 %leave.3 = (f32[4,392,512]{2,1,0:T(8,128)}, bf16[4,208,512]{2,1,0:T(8,128)(2,1)}) custom-call(bf16[4,392,512]{2,1,0:T(8,128)(2,1)} %get-tuple-element.233.rows_ref, bf16[392,392]{1,0:T(8,128)(2,1)} %constant.123.order_ref), custom_call_target="tpu_custom_call" | custom-call | flops 4000000000 | bytes 14400000 | tf_op jit(solution)/shard_map/leave/pallas_call | solution.py:718
  245.6 6.6 %all-to-all-done = f32[16,1,2816]{2,1,0:T(1,128)S(1)} async-done(((f32[16,1,2816]{2,1,0:T(1,128)}), f32[16,1,2816]{2,1,0:T(1,128)S(1)}, u32[]{:S(2)}, u32[]{:S(2)}) %all-to-all-start) | async-done | bytes 180256 | tf_op jit(solution)/shard_map/all_to_all | solution.py:936
  252.3 0.8 fusion.7
  253.9 1.3 collective-permute-start.22
  255.2 0.8 broadcast_in_dim.17
  255.9 5.0 %all-to-all-start.1 = ((f32[16,1,2816]{2,1,0:T(1,128)}), f32[16,1,2816]{2,1,0:T(1,128)S(1)}, u32[]{:S(2)}, u32[]{:S(2)}) async-start(f32[16,1,2816]{2,1,0:T(1,128)} %broadcast_in_dim.17), calls=%async_computation.1 | async-start | bytes 360448 | tf_op jit(solution)/shard_map/all_to_all | solution.py:856
  260.9 1.2 convert_select_fusion.1
  262.1 0.7 maximum_bitcast_fusion
  262.9 6.6 %all-to-all-done.1 = f32[16,1,2816]{2,1,0:T(1,128)S(1)} async-done(((f32[16,1,2816]{2,1,0:T(1,128)}), f32[16,1,2816]{2,1,0:T(1,128)S(1)}, u32[]{:S(2)}, u32[]{:S(2)}) %all-to-all-start.1) | async-done | bytes 180256 | tf_op jit(solution)/shard_map/all_to_all | solution.py:856
  269.4 0.7 copy.40
  270.1 0.7 pad_maximum_fusion.1
  270.8 0.6 maximum_bitcast_fusion.1
  271.6 1.1 collective-permute-start.24
  272.7 5.7 %table_rows.1 = f32[16,2535]{1,0:T(8,128)} custom-call(s32[2,2816]{1,0:T(2,128)} %get-tuple-element.237.lab_ref, f32[16,2816]{1,0:T(8,128)} %bitcast.84), custom_call_target="tpu_custom_call" | custom-call | flops 5000000000 | bytes 18000000 | tf_op jit(solution)/shard_map/table_rows/pallas_call | solution.py:277
  278.5 0.9 collective-permute-start.26
  279.4 1.5 collective-permute-start.27
  280.9 2.1 collective-permute-start.28
  283.0 2.0 select_bitcast_fusion
  285.0 1.3 collective-permute-done.27
  286.3 0.6 collective-permute-done.28
  287.1 0.6 fusion.10
  287.7 0.5 slice_bitcast_fusion.9
  288.2 0.6 split.46
  288.8 0.7 pad_maximum_fusion.3
  (108 shorter events, 3.8 us)
Async XLA Ops:
  2.5 14.3 %collective-permute-start = (bf16[32,896]{1,0:T(8,128)(2,1)}, bf16[32,896]{1,0:T(8,128)(2,1)S(1)}, u32[]{:S(2)}, u32[]{:S(2)}) collective-permute-start(bf16[32,896]{1,0:T(8,128)(2,1)} %get-tuple-element.131), channel_id=1, source_target_pairs={{0,4},{1,5},{2,6},{3,7},{4,0},{5,1},{6,2},{7,3},{8,12},{9,13},{10,... | collective-permute-start | bytes 172040 | tf_op jit(solution)/shard_map/ppermute | solution.py:782
  5.5 12.1 %collective-permute-start.1 = (bf16[32,896]{1,0:T(8,128)(2,1)}, bf16[32,896]{1,0:T(8,128)(2,1)S(1)}, u32[]{:S(2)}, u32[]{:S(2)}) collective-permute-start(bf16[32,896]{1,0:T(8,128)(2,1)} %get-tuple-element.131), channel_id=1, source_target_pairs={{0,8},{1,9},{2,10},{3,11},{4,12},{5,13},{6,14},{7,15},{8,0},{9,1},... | collective-permute-start | bytes 172040 | tf_op jit(solution)/shard_map/ppermute | solution.py:782
  8.1 13.0 %collective-permute-start.2 = (bf16[32,896]{1,0:T(8,128)(2,1)}, bf16[32,896]{1,0:T(8,128)(2,1)S(1)}, u32[]{:S(2)}, u32[]{:S(2)}) collective-permute-start(bf16[32,896]{1,0:T(8,128)(2,1)} %get-tuple-element.131), channel_id=1, source_target_pairs={{0,12},{1,13},{2,14},{3,15},{4,8},{5,9},{6,10},{7,11},{8,4},{9,5},... | collective-permute-start | bytes 172040 | tf_op jit(solution)/shard_map/ppermute | solution.py:782
  8.1 13.0 %collective-permute-start.3 = (bf16[1,4,392,512]{3,2,1,0:T(8,128)(2,1)}, bf16[1,4,392,512]{3,2,1,0:T(8,128)(2,1)}, u32[]{:S(2)}, u32[]{:S(2)}) collective-permute-start(bf16[1,4,392,512]{3,2,1,0:T(8,128)(2,1)} %param.23), channel_id=1, source_target_pairs={{0,16},{16,0},{1,17},{17,1},{2,18},{18,2},{3,19},{19,3},{4,20},{20... | collective-permute-start | bytes 4816904 | tf_op jit(solution)/shard_map/ppermute | solution.py:670
  8.1 19.0 %collective-permute-start.6 = (bf16[1,4,392,512]{3,2,1,0:T(8,128)(2,1)}, bf16[1,4,392,512]{3,2,1,0:T(8,128)(2,1)}, u32[]{:S(2)}, u32[]{:S(2)}) collective-permute-start(bf16[1,4,392,512]{3,2,1,0:T(8,128)(2,1)} %param.39), channel_id=1, source_target_pairs={{0,16},{16,0},{1,17},{17,1},{2,18},{18,2},{3,19},{19,3},{4,20},{20... | collective-permute-start | bytes 4816904 | tf_op jit(solution)/shard_map/ppermute | solution.py:670
  9.5 6.0 %copy-start.4 = (bf16[32,2304]{1,0:T(8,128)(2,1)S(1)}, bf16[32,2304]{1,0:T(8,128)(2,1)}, u32[]{:S(2)}) copy-start(bf16[32,2304]{1,0:T(8,128)(2,1)} %get-tuple-element.144) | copy-start | bytes 442372
  9.5 11.7 %copy-start.7 = (bf16[32,896]{1,0:T(8,128)(2,1)S(1)}, bf16[32,896]{1,0:T(8,128)(2,1)}, u32[]{:S(2)}) copy-start(bf16[32,896]{1,0:T(8,128)(2,1)} %get-tuple-element.131) | copy-start | bytes 172036
  16.8 37.7 %collective-permute-start.7 = (bf16[32,2304]{1,0:T(8,128)(2,1)S(1)}, bf16[32,2304]{1,0:T(8,128)(2,1)S(1)}, u32[]{:S(2)}, u32[]{:S(2)}) collective-permute-start(bf16[32,2304]{1,0:T(8,128)(2,1)S(1)} %copy-done.4), channel_id=1, source_target_pairs={{0,4},{1,5},{2,6},{3,7},{4,0},{5,1},{6,2},{7,3},{8,12},{9,13},{10,... | collective-permute-start | bytes 442376 | tf_op jit(solution)/shard_map/ppermute | solution.py:782
  17.7 36.8 %collective-permute-start.8 = (bf16[32,2304]{1,0:T(8,128)(2,1)S(1)}, bf16[32,2304]{1,0:T(8,128)(2,1)S(1)}, u32[]{:S(2)}, u32[]{:S(2)}) collective-permute-start(bf16[32,2304]{1,0:T(8,128)(2,1)S(1)} %copy-done.4), channel_id=1, source_target_pairs={{0,8},{1,9},{2,10},{3,11},{4,12},{5,13},{6,14},{7,15},{8,0},{9,1},... | collective-permute-start | bytes 442376 | tf_op jit(solution)/shard_map/ppermute | solution.py:782
  21.2 33.3 %collective-permute-start.9 = (bf16[32,2304]{1,0:T(8,128)(2,1)S(1)}, bf16[32,2304]{1,0:T(8,128)(2,1)S(1)}, u32[]{:S(2)}, u32[]{:S(2)}) collective-permute-start(bf16[32,2304]{1,0:T(8,128)(2,1)S(1)} %copy-done.4), channel_id=1, source_target_pairs={{0,12},{1,13},{2,14},{3,15},{4,8},{5,9},{6,10},{7,11},{8,4},{9,5},... | collective-permute-start | bytes 442376 | tf_op jit(solution)/shard_map/ppermute | solution.py:782
  21.2 20.9 %collective-permute-start.4 = (bf16[4,32,896]{2,1,0:T(8,128)(2,1)S(1)}, bf16[4,32,896]{2,1,0:T(8,128)(2,1)S(1)}, u32[]{:S(2)}, u32[]{:S(2)}) collective-permute-start(bf16[4,32,896]{2,1,0:T(8,128)(2,1)S(1)} %pad_maximum_fusion.2), channel_id=1, source_target_pairs={{0,2},{1,3},{2,0},{3,1},{4,6},{5,7},{6,4},{7,5},{8,10},{9,11},{10,... | collective-permute-start | bytes 688136 | tf_op jit(solution)/shard_map/ppermute | solution.py:782
  42.2 12.3 %collective-permute-start.5 = (bf16[8,32,896]{2,1,0:T(8,128)(2,1)S(1)}, bf16[8,32,896]{2,1,0:T(8,128)(2,1)S(1)}, u32[]{:S(2)}, u32[]{:S(2)}) collective-permute-start(bf16[8,32,896]{2,1,0:T(8,128)(2,1)S(1)} %get-tuple-element.261), channel_id=1, source_target_pairs={{0,1},{1,0},{2,3},{3,2},{4,5},{5,4},{6,7},{7,6},{8,9},{9,8},{10,11... | collective-permute-start | bytes 1376264 | tf_op jit(solution)/shard_map/ppermute | solution.py:782
  43.8 11.6 %copy-start.12 = (bf16[16,32,2304]{2,1,0:T(8,128)(2,1)S(1)}, bf16[16,32,2304]{2,1,0:T(8,128)(2,1)}, u32[]{:S(2)}) copy-start(bf16[16,32,2304]{2,1,0:T(8,128)(2,1)} %get-tuple-element.271) | copy-start | bytes 7077892
  54.6 12.7 %collective-permute-start.11 = (bf16[4,32,2304]{2,1,0:T(8,128)(2,1)S(1)}, bf16[4,32,2304]{2,1,0:T(8,128)(2,1)S(1)}, u32[]{:S(2)}, u32[]{:S(2)}) collective-permute-start(bf16[4,32,2304]{2,1,0:T(8,128)(2,1)S(1)} %pad_maximum_fusion), channel_id=1, source_target_pairs={{0,2},{1,3},{2,0},{3,1},{4,6},{5,7},{6,4},{7,5},{8,10},{9,11},{10,... | collective-permute-start | bytes 1769480 | tf_op jit(solution)/shard_map/ppermute | solution.py:782
  55.2 2.7 copy-start.14
  55.2 2.7 collective-permute-start.10
  67.4 18.8 %collective-permute-start.12 = (bf16[8,32,2304]{2,1,0:T(8,128)(2,1)S(1)}, bf16[8,32,2304]{2,1,0:T(8,128)(2,1)S(1)}, u32[]{:S(2)}, u32[]{:S(2)}) collective-permute-start(bf16[8,32,2304]{2,1,0:T(8,128)(2,1)S(1)} %get-tuple-element.253), channel_id=1, source_target_pairs={{0,1},{1,0},{2,3},{3,2},{4,5},{5,4},{6,7},{7,6},{8,9},{9,8},{10,11... | collective-permute-start | bytes 3538952 | tf_op jit(solution)/shard_map/ppermute | solution.py:782
  86.3 19.5 %copy-start.13 = (bf16[16,32,2304]{2,1,0:T(8,128)(2,1)}, bf16[16,32,2304]{2,1,0:T(8,128)(2,1)S(1)}, u32[]{:S(2)}) copy-start(bf16[16,32,2304]{2,1,0:T(8,128)(2,1)S(1)} %constant_dynamic-update-slice_fusion.16.own_ref) | copy-start | bytes 7077892
  86.3 19.5 %collective-permute-start.13 = (bf16[16,32,2304]{2,1,0:T(8,128)(2,1)S(1)}, bf16[16,32,2304]{2,1,0:T(8,128)(2,1)S(1)}, u32[]{:S(2)}, u32[]{:S(2)}) collective-permute-start(bf16[16,32,2304]{2,1,0:T(8,128)(2,1)S(1)} %constant_dynamic-update-slice_fusion.16.own_ref), channel_id=1, source_target_pairs={{0,16},{16,0},{1,17},{17,1},{2,18},{18,2},{3,19},{19,3},{4,20},{20... | collective-permute-start | bytes 7077896 | tf_op jit(solution)/shard_map/ppermute | solution.py:670
  105.8 1.5 copy-start.15
  151.7 19.4 %collective-permute-start.15 = (bf16[16,32,2304]{2,1,0:T(8,128)(2,1)}, bf16[16,32,2304]{2,1,0:T(8,128)(2,1)S(1)}, u32[]{:S(2)}, u32[]{:S(2)}) collective-permute-start(bf16[16,32,2304]{2,1,0:T(8,128)(2,1)} %get-tuple-element.186), channel_id=1, source_target_pairs={{0,16},{16,0},{1,17},{17,1},{2,18},{18,2},{3,19},{19,3},{4,20},{20... | collective-permute-start | bytes 7077896 | tf_op jit(solution)/shard_map/ppermute | solution.py:670
  156.5 13.1 %collective-permute-start.14 = (bf16[4,208,512]{2,1,0:T(8,128)(2,1)}, bf16[4,208,512]{2,1,0:T(8,128)(2,1)S(1)}, u32[]{:S(2)}, u32[]{:S(2)}) collective-permute-start(bf16[4,208,512]{2,1,0:T(8,128)(2,1)} %get-tuple-element.174), channel_id=1, source_target_pairs={{0,16},{16,0},{1,17},{17,1},{2,18},{18,2},{3,19},{19,3},{4,20},{20... | collective-permute-start | bytes 2555912 | tf_op jit(solution)/shard_map/ppermute | solution.py:670
  156.5 13.0 %copy-start.2 = (bf16[4,392,512]{2,1,0:T(8,128)(2,1)S(1)}, bf16[4,392,512]{2,1,0:T(8,128)(2,1)}, u32[]{:S(2)}) copy-start(bf16[4,392,512]{2,1,0:T(8,128)(2,1)} %get-tuple-element.175) | copy-start | bytes 4816900
  169.5 2.2 copy-start.1
  172.5 26.5 %collective-permute-start.16 = (bf16[8,32,2304]{2,1,0:T(8,128)(2,1)S(1)}, bf16[8,32,2304]{2,1,0:T(8,128)(2,1)S(1)}, u32[]{:S(2)}, u32[]{:S(2)}) collective-permute-start(bf16[8,32,2304]{2,1,0:T(8,128)(2,1)S(1)} %slice.74), channel_id=1, source_target_pairs={{0,1},{1,0},{2,3},{3,2},{4,5},{5,4},{6,7},{7,6},{8,9},{9,8},{10,11... | collective-permute-start | bytes 3538952 | tf_op jit(solution)/shard_map/ppermute | solution.py:782
  199.3 14.2 %collective-permute-start.17 = (bf16[4,32,2304]{2,1,0:T(8,128)(2,1)S(1)}, bf16[4,32,2304]{2,1,0:T(8,128)(2,1)S(1)}, u32[]{:S(2)}, u32[]{:S(2)}) collective-permute-start(bf16[4,32,2304]{2,1,0:T(8,128)(2,1)S(1)} %slice.76), channel_id=1, source_target_pairs={{0,2},{1,3},{2,0},{3,1},{4,6},{5,7},{6,4},{7,5},{8,10},{9,11},{10,... | collective-permute-start | bytes 1769480 | tf_op jit(solution)/shard_map/ppermute | solution.py:782
  213.6 21.0 %copy-start.8 = (f32[1,4,2816]{2,1,0:T(4,128)S(1)}, f32[1,4,2816]{2,1,0:T(4,128)}, u32[]{:S(2)}) copy-start(f32[1,4,2816]{2,1,0:T(4,128)} %get-tuple-element.225) | copy-start | bytes 135172
  213.6 21.0 %copy-start.9 = (f32[1,4,2816]{2,1,0:T(4,128)S(1)}, f32[1,4,2816]{2,1,0:T(4,128)}, u32[]{:S(2)}) copy-start(f32[1,4,2816]{2,1,0:T(4,128)} %get-tuple-element.226) | copy-start | bytes 135172
  213.6 21.0 %copy-start.10 = (f32[1,4,2816]{2,1,0:T(4,128)S(1)}, f32[1,4,2816]{2,1,0:T(4,128)}, u32[]{:S(2)}) copy-start(f32[1,4,2816]{2,1,0:T(4,128)} %get-tuple-element.227) | copy-start | bytes 135172
  213.6 21.0 %copy-start.11 = (f32[1,4,2816]{2,1,0:T(4,128)S(1)}, f32[1,4,2816]{2,1,0:T(4,128)}, u32[]{:S(2)}) copy-start(f32[1,4,2816]{2,1,0:T(4,128)} %get-tuple-element.228) | copy-start | bytes 135172
  229.4 22.9 %collective-permute-start.18 = (bf16[16,32,896]{2,1,0:T(8,128)(2,1)}, bf16[16,32,896]{2,1,0:T(8,128)(2,1)S(1)}, u32[]{:S(2)}, u32[]{:S(2)}) collective-permute-start(bf16[16,32,896]{2,1,0:T(8,128)(2,1)} %get-tuple-element.223), channel_id=1, source_target_pairs={{0,16},{16,0},{1,17},{17,1},{2,18},{18,2},{3,19},{19,3},{4,20},{20... | collective-permute-start | bytes 2752520 | tf_op jit(solution)/shard_map/ppermute | solution.py:670
  230.2 22.0 %collective-permute-start.19 = (bf16[32,2304]{1,0:T(8,128)(2,1)}, bf16[32,2304]{1,0:T(8,128)(2,1)S(1)}, u32[]{:S(2)}, u32[]{:S(2)}) collective-permute-start(bf16[32,2304]{1,0:T(8,128)(2,1)} %get-tuple-element.251), channel_id=1, source_target_pairs={{0,4},{1,5},{2,6},{3,7},{4,0},{5,1},{6,2},{7,3},{8,12},{9,13},{10,... | collective-permute-start | bytes 442376 | tf_op jit(solution)/shard_map/ppermute | solution.py:782
  230.6 21.6 %collective-permute-start.20 = (bf16[32,2304]{1,0:T(8,128)(2,1)}, bf16[32,2304]{1,0:T(8,128)(2,1)S(1)}, u32[]{:S(2)}, u32[]{:S(2)}) collective-permute-start(bf16[32,2304]{1,0:T(8,128)(2,1)} %get-tuple-element.250), channel_id=1, source_target_pairs={{0,8},{1,9},{2,10},{3,11},{4,12},{5,13},{6,14},{7,15},{8,0},{9,1},... | collective-permute-start | bytes 442376 | tf_op jit(solution)/shard_map/ppermute | solution.py:782
  234.4 17.9 %collective-permute-start.21 = (bf16[32,2304]{1,0:T(8,128)(2,1)S(1)}, bf16[32,2304]{1,0:T(8,128)(2,1)S(1)}, u32[]{:S(2)}, u32[]{:S(2)}) collective-permute-start(bf16[32,2304]{1,0:T(8,128)(2,1)S(1)} %get-tuple-element.249), channel_id=1, source_target_pairs={{0,12},{1,13},{2,14},{3,15},{4,8},{5,9},{6,10},{7,11},{8,4},{9,5},... | collective-permute-start | bytes 442376 | tf_op jit(solution)/shard_map/ppermute | solution.py:782
  235.6 16.6 %all-to-all-start = ((f32[16,1,2816]{2,1,0:T(1,128)}), f32[16,1,2816]{2,1,0:T(1,128)S(1)}, u32[]{:S(2)}, u32[]{:S(2)}) async-start(f32[16,1,2816]{2,1,0:T(1,128)} %all_to_all.12), calls=%async_computation | async-start | bytes 360448 | tf_op jit(solution)/shard_map/all_to_all | solution.py:936
  241.0 12.6 %copy-start.3 = (bf16[16,32,896]{2,1,0:T(8,128)(2,1)S(1)}, bf16[16,32,896]{2,1,0:T(8,128)(2,1)}, u32[]{:S(2)}) copy-start(bf16[16,32,896]{2,1,0:T(8,128)(2,1)} %get-tuple-element.222) | copy-start | bytes 2752516
  252.3 1.3 copy-start.5
  252.3 1.3 copy-start.6
  253.1 7.8 %collective-permute-start.30 = (bf16[32,2304]{1,0:T(8,128)(2,1)}, bf16[32,2304]{1,0:T(8,128)(2,1)}, u32[]{:S(2)}, u32[]{:S(2)}) collective-permute-start(bf16[32,2304]{1,0:T(8,128)(2,1)} %fusion.7), channel_id=1, source_target_pairs={{0,16},{16,0},{1,17},{17,1},{2,18},{18,2},{3,19},{19,3},{4,20},{20... | collective-permute-start | bytes 442376 | tf_op jit(solution)/shard_map/ppermute | solution.py:670
  253.1 2.1 collective-permute-start.23
  253.9 16.2 %collective-permute-start.22 = (bf16[8,32,896]{2,1,0:T(8,128)(2,1)S(1)}, bf16[8,32,896]{2,1,0:T(8,128)(2,1)S(1)}, u32[]{:S(2)}, u32[]{:S(2)}) collective-permute-start(bf16[8,32,896]{2,1,0:T(8,128)(2,1)S(1)} %slice.82), channel_id=1, source_target_pairs={{0,1},{1,0},{2,3},{3,2},{4,5},{5,4},{6,7},{7,6},{8,9},{9,8},{10,11... | collective-permute-start | bytes 1376264 | tf_op jit(solution)/shard_map/ppermute | solution.py:782
  255.9 13.5 %all-to-all-start.1 = ((f32[16,1,2816]{2,1,0:T(1,128)}), f32[16,1,2816]{2,1,0:T(1,128)S(1)}, u32[]{:S(2)}, u32[]{:S(2)}) async-start(f32[16,1,2816]{2,1,0:T(1,128)} %broadcast_in_dim.17), calls=%async_computation.1 | async-start | bytes 360448 | tf_op jit(solution)/shard_map/all_to_all | solution.py:856
  270.1 8.3 %collective-permute-start.25 = (bf16[4,208,512]{2,1,0:T(8,128)(2,1)}, bf16[4,208,512]{2,1,0:T(8,128)(2,1)S(1)}, u32[]{:S(2)}, u32[]{:S(2)}) collective-permute-start(bf16[4,208,512]{2,1,0:T(8,128)(2,1)} %get-tuple-element.239), channel_id=1, source_target_pairs={{0,16},{16,0},{1,17},{17,1},{2,18},{18,2},{3,19},{19,3},{4,20},{20... | collective-permute-start | bytes 2555912 | tf_op jit(solution)/shard_map/ppermute | solution.py:670
  271.6 6.8 %collective-permute-start.24 = (bf16[4,32,896]{2,1,0:T(8,128)(2,1)S(1)}, bf16[4,32,896]{2,1,0:T(8,128)(2,1)S(1)}, u32[]{:S(2)}, u32[]{:S(2)}) collective-permute-start(bf16[4,32,896]{2,1,0:T(8,128)(2,1)S(1)} %slice.83), channel_id=1, source_target_pairs={{0,2},{1,3},{2,0},{3,1},{4,6},{5,7},{6,4},{7,5},{8,10},{9,11},{10,... | collective-permute-start | bytes 688136 | tf_op jit(solution)/shard_map/ppermute | solution.py:782
  272.7 10.2 %copy-start = (f32[4,392,512]{2,1,0:T(8,128)S(1)}, f32[4,392,512]{2,1,0:T(8,128)}, u32[]{:S(2)}) copy-start(f32[4,392,512]{2,1,0:T(8,128)} %get-tuple-element.241) | copy-start | bytes 9633796
  278.5 6.4 %collective-permute-start.26 = (bf16[32,896]{1,0:T(8,128)(2,1)S(1)}, bf16[32,896]{1,0:T(8,128)(2,1)S(1)}, u32[]{:S(2)}, u32[]{:S(2)}) collective-permute-start(bf16[32,896]{1,0:T(8,128)(2,1)S(1)} %get-tuple-element.258), channel_id=1, source_target_pairs={{0,4},{1,5},{2,6},{3,7},{4,0},{5,1},{6,2},{7,3},{8,12},{9,13},{10,... | collective-permute-start | bytes 172040 | tf_op jit(solution)/shard_map/ppermute | solution.py:782
  279.4 6.9 %collective-permute-start.27 = (bf16[32,896]{1,0:T(8,128)(2,1)S(1)}, bf16[32,896]{1,0:T(8,128)(2,1)S(1)}, u32[]{:S(2)}, u32[]{:S(2)}) collective-permute-start(bf16[32,896]{1,0:T(8,128)(2,1)S(1)} %get-tuple-element.260), channel_id=1, source_target_pairs={{0,8},{1,9},{2,10},{3,11},{4,12},{5,13},{6,14},{7,15},{8,0},{9,1},... | collective-permute-start | bytes 172040 | tf_op jit(solution)/shard_map/ppermute | solution.py:782
  280.9 6.1 %collective-permute-start.28 = (bf16[32,896]{1,0:T(8,128)(2,1)S(1)}, bf16[32,896]{1,0:T(8,128)(2,1)S(1)}, u32[]{:S(2)}, u32[]{:S(2)}) collective-permute-start(bf16[32,896]{1,0:T(8,128)(2,1)S(1)} %get-tuple-element.259), channel_id=1, source_target_pairs={{0,12},{1,13},{2,14},{3,15},{4,8},{5,9},{6,10},{7,11},{8,4},{9,5},... | collective-permute-start | bytes 172040 | tf_op jit(solution)/shard_map/ppermute | solution.py:782
  287.0 1.8 collective-permute-start.29
